TPU v7x, 32 devices: a whole 2x2x4 slice. The times are simulated.
32 devices in a mesh: seq: 16 (over z, y, core), tp: 2 (over x).
Axes of the slice: x: 2, y: 2, z: 4, core: 2. Of those that a mesh axis runs over, the one named last changes fastest.
Arguments:
- queries: bfloat16 [4096, 8192], P('seq', 'tp'), may hold values from -12 to 12
- kv_rows: bfloat16 [4096, 2048], P('seq', 'tp'), may hold values from -6 to 6
- vertical: int32 [64, 8], replicated, may hold values from 0 to 63, as said below
- slash: int32 [64, 8], replicated, may hold values from 0 to 11, as said below
Outputs:
- attended: bfloat16 [4096, 8192], P(('seq', 'tp'))
Inputs may be any that keep to these rules, and one draw needn't show every extreme that they name: `vertical`: each row lists 8 distinct blocks in rising order and includes block 0 and block 63. The heads that share one key-value head list together exactly 12 distinct blocks. `slash`: each row lists 8 distinct offsets in rising order, the first 0 and the last 11.
All inputs are finite; a program needn't handle non-finite values.
Results may differ from a plain program's by a relative error of at most 0.0045.
Values may be sent and summed in bfloat16 or wider, within the bound.
No kernel may reach another device: no remote copies, remote signals or barrier semaphores. Data moves between devices by JAX's collectives and lax.ppermute only.
A program may use at most 64 MiB of HBM per device.

v0:
```python
import jax
import jax.numpy as jnp
from jax import lax
from jax.sharding import PartitionSpec as P

HEAD_SIZE = 128
BLK = 64


def as_sent(array):

    def short(part):
        return part.astype(jnp.bfloat16) if part.dtype == jnp.float32 else part

    return jax.tree.map(short, array)


def key_mask(bids, vertical_row, srow):
    dist = bids[:, None] - vertical_row[None, :]
    hit = jnp.any(dist[:, :, None] == srow[None, None, :], axis=2)
    live_v = jnp.logical_and(dist >= 0, jnp.logical_not(hit))
    live_s = bids[:, None] - srow[None, :] >= 0
    live = jnp.concatenate([live_v, live_s], axis=1)
    diag = jnp.concatenate([jnp.zeros(vertical_row.shape, bool), srow == 0])
    rows = jnp.arange(BLK, dtype=jnp.int32)
    lower = rows[None, :] <= rows[:, None]
    return live[:, None, :, None] & (
        jnp.logical_not(diag)[None, None, :, None] | lower[None, :, None, :]
    )


def attend(query_block, vert_block, slash_block, bids, vertical_row, srow):
    count_v = vert_block.shape[0]
    scale = 1.0 / HEAD_SIZE**0.5
    logit_vert = jnp.einsum(
        "unz,syz->unsy",
        query_block,
        vert_block[..., :HEAD_SIZE],
        preferred_element_type=jnp.float32,
    )
    logit_slash = jnp.einsum(
        "unz,suyz->unsy",
        query_block,
        slash_block[..., :HEAD_SIZE],
        preferred_element_type=jnp.float32,
    )
    logit_matrix = jnp.concatenate([logit_vert, logit_slash], axis=2) * scale
    mask = key_mask(bids, vertical_row, srow)
    logit_matrix = jnp.where(mask, logit_matrix, -1e30)
    top = jnp.max(logit_matrix, axis=(2, 3), keepdims=True)
    weights = jnp.where(mask, jnp.exp(logit_matrix - top), 0.0)
    total = jnp.sum(weights, axis=(2, 3))
    probabilities = weights.astype(jnp.bfloat16)
    weighted_sum = jnp.einsum(
        "unsy,syd->und",
        probabilities[:, :, :count_v],
        vert_block[..., HEAD_SIZE:],
        preferred_element_type=jnp.float32,
    )
    weighted_sum = weighted_sum + jnp.einsum(
        "unsy,suyd->und",
        probabilities[:, :, count_v:],
        slash_block[..., HEAD_SIZE:],
        preferred_element_type=jnp.float32,
    )
    return (weighted_sum / total[..., None]).astype(jnp.bfloat16)


def slash_slices(table, starts, key_value_head, block_list):
    pieces = []
    for index in range(starts.shape[0]):
        piece = lax.dynamic_slice(
            table,
            (starts[index], 0, key_value_head, 0),
            (block_list, table.shape[1], 1, table.shape[3]),
        )
        pieces.append(piece[:, :, 0])
    return jnp.stack(pieces, axis=0)


def per_device(queries, kv_rows, vertical, slash):
    tok = queries.shape[0]
    n_tp = lax.axis_size("tp")
    heads_loc = vertical.shape[0] // n_tp
    kv_loc = kv_rows.shape[1] // (2 * HEAD_SIZE)
    group = heads_loc // kv_loc
    block_list = tok // BLK
    seq_pos = lax.axis_index("seq")
    tp_pos = lax.axis_index("tp")
    my_vert = lax.dynamic_slice_in_dim(vertical, tp_pos * heads_loc, heads_loc, 0)
    my_slash = lax.dynamic_slice_in_dim(slash, tp_pos * heads_loc, heads_loc, 0)
    first = seq_pos * block_list
    bids = first + jnp.arange(block_list, dtype=jnp.int32)
    full = lax.all_gather(kv_rows, "seq", axis=0, tiled=True)
    index_table = full.reshape(full.shape[0] // BLK, BLK, kv_loc, 2 * HEAD_SIZE)
    front = 3 * block_list
    padded = jnp.concatenate(
        [jnp.zeros((front, BLK, kv_loc, 2 * HEAD_SIZE), index_table.dtype), index_table], axis=0
    )

    def gather_rows(key_value_head, vertical_row, srow):
        vert_block = index_table[vertical_row, :, key_value_head]
        starts = first + front - srow
        return (vert_block, slash_slices(padded, starts, key_value_head, block_list))

    qheads = jnp.transpose(queries.reshape(block_list, BLK, heads_loc, HEAD_SIZE), (2, 0, 1, 3))

    def one_head(item):
        query_block, vertical_row, srow, key_value_head = item
        vert_block, slash_block = gather_rows(key_value_head, vertical_row, srow)
        return attend(query_block, vert_block, slash_block, bids, vertical_row, srow)

    owners = jnp.arange(heads_loc, dtype=jnp.int32) // group
    outputs = lax.map(one_head, (qheads, my_vert, my_slash, owners))
    attn = jnp.transpose(outputs, (1, 2, 0, 3)).reshape(tok, heads_loc * HEAD_SIZE)
    return lax.all_to_all(as_sent(attn), "tp", split_axis=0, concat_axis=1, tiled=True).astype(
        attn.dtype
    )


def solution(mesh):
    return jax.shard_map(
        per_device,
        mesh=mesh,
        in_specs=(P("seq", "tp"), P("seq", "tp"), P(), P()),
        out_specs=P(("seq", "tp"), None),
        check_vma=False,
    )
```

profile of v0, /device:TPU:1, one launch (start us, length us, event | category | flops | bytes accessed | tf_op | source)
XLA Modules:
  0.0 1315.7 jit_solution(16473721138085479891)
XLA Ops:
  8.2 2.1 copy.45
  10.7 2.2 copy.31
  12.9 74.0 %all-gather.2.cloned.1.call-done = bf16[4096,1024]{1,0:T(8,128)(2,1)} async-done(((bf16[256,1024]{1,0:T(8,128)(2,1)}), bf16[4096,1024]{1,0:T(8,128)(2,1)}) %all-gather.2.cloned.1.call-update) | async-done | bytes 8388624 | tf_op jit(solution)/shard_map/all_gather | solution.py:94
  87.0 14.5 %reshape.99 = bf16[64,64,4,256]{3,2,1,0:T(4,128)(2,1)} reshape(bf16[4096,1024]{1,0:T(8,128)(2,1)} %all-gather.2.cloned.1.call-done) | data formatting | bytes 16777216 | tf_op jit(solution)/shard_map/reshape | solution.py:95
  101.5 8.3 copy.44
  109.8 8.7 copy.32
  118.5 8.9 concatenate.19.clone
  127.4 1141.2 %while.13 = (s32[]{:T(128)}, bf16[32,4,64,128]{3,2,1,0:T(8,128)(2,1)}, s32[32,8]{1,0:T(8,128)S(1)}, s32[32,8]{1,0:T(8,128)S(1)}, bf16[32,4,64,128]{3,2,1,0:T(8,1...) while((s32[]{:T(128)}, ...), condition=%wide.region_4.5_spmd.clone, body=%wide.region_0.4_spmd.clone.sunk | while | flops 137793904 | bytes 10371367 | solution.py:114
  154.9 3.9 gather_fusion
  158.9 1.2 fusion.53
  190.6 3.9 gather_fusion
  194.6 1.1 fusion.53
  226.3 3.9 gather_fusion
  261.9 3.9 gather_fusion
  297.6 3.9 gather_fusion
  301.6 1.1 fusion.53
  333.3 3.9 gather_fusion
  368.9 3.9 gather_fusion
  404.6 3.9 gather_fusion
  440.3 3.9 gather_fusion
  475.9 3.9 gather_fusion
  511.6 3.9 gather_fusion
  547.2 3.9 gather_fusion
  582.9 3.9 gather_fusion
  618.6 3.9 gather_fusion
  654.2 3.9 gather_fusion
  689.9 3.9 gather_fusion
  725.6 3.9 gather_fusion
  761.2 3.9 gather_fusion
  796.9 3.9 gather_fusion
  832.6 3.9 gather_fusion
  868.2 3.9 gather_fusion
  903.9 3.9 gather_fusion
  939.5 3.9 gather_fusion
  975.2 3.9 gather_fusion
  1010.9 3.9 gather_fusion
  1046.5 3.9 gather_fusion
  1082.2 3.9 gather_fusion
  1117.9 3.9 gather_fusion
  1153.5 3.9 gather_fusion
  1189.2 3.9 gather_fusion
  1224.8 3.9 gather_fusion
  1260.5 3.9 gather_fusion
  1268.7 2.9 copy.34
  1271.6 2.3 all_to_all.14
  1273.9 28.5 %all_to_all.19 = bf16[2,128,4096]{2,1,0:T(8,128)(2,1)S(1)} all-to-all(bf16[2,128,4096]{2,1,0:T(8,128)(2,1)} %all_to_all.14), channel_id=1, replica_groups=mesh['seq'=16,'tp'=2] {'tp'}, dimensions={0} | all-to-all | bytes 4194304 | tf_op jit(solution)/shard_map/all_to_all | solution.py:116
  1302.4 2.5 copy.35
  1304.8 4.1 copy.36
  (901 shorter events, 462.8 us)
Async XLA Ops:
  6.5 80.4 %all-gather.2.cloned.1.call-start = ((), (), s32[]{:S(2)}) async-start(), calls=%async_computation.1 | async-start | bytes 8912896 | tf_op jit(solution)/shard_map/all_gather | solution.py:94
Sparse Core Ops, SparseCore 0:
  9.5 77.3 all-gather.1
where the time goes:
time: 1330 us; the launch traced here: 1320 us
  loops' own time  551 us (41%)
  local copies, waits for them, and re-layouts  464 us (35%)
  matrix products  114 us (9%)
  waiting for transfers between devices  74.8 us (6%)
  other arithmetic  70.6 us (5%)
  blocking collectives  28.5 us (2%)
  between operations  13.4 us (1%)
    another operation x1, loops' own time, per_device(): outputs = lax.map(one_head, (qheads, my_vert, my_slash, owners))  551 us
    while x224, local copies, waits for them, and re-layouts  207 us
    gather x32, local copies, waits for them, and re-layouts, gather_rows(): vert_block = index_table[vertical_row, :, key_value_head]  126 us
    all_gather x1, waiting for transfers between devices, per_device(): full = lax.all_gather(kv_rows, 'seq', axis=0, tiled=True)  74 us
    dot_general x32, matrix products, attend(): jnp.einsum('unz,syz->unsy', query_block, vert_block[..., :HEAD_SIZE], pre...  36.7 us
    dot_general x32, matrix products, attend(): jnp.einsum('unz,suyz->unsy', query_block, slash_block[..., :HEAD_SIZE], p...  35.9 us
    dot_general x32, matrix products, attend(): jnp.einsum('unsy,suyd->und', probabilities[:, :, count_v:], slash_block[....  31.5 us
    reduce_sum x32, other arithmetic, attend(): total = jnp.sum(weights, axis=(2, 3))  30.9 us
  transfers between devices with their start and end apart: 1, of which 1 were waited for; matrix products, arithmetic and copies ran while one was open for 0% of the time, Pallas kernels for 0%

commit v1 on v0

v1 whole, which is shorter than its diff:
```python
import functools
import math

import jax
import jax.numpy as jnp
from jax import lax
from jax.experimental import pallas as pl
from jax.experimental.pallas import tpu as pltpu
from jax.sharding import PartitionSpec as P

HEAD_SIZE = 128
BLK = 64
SMAX = 11
PIECE = 16
N_PIECES = (BLK // PIECE) * 2
LANES = 128
NEG = -1e30
SCALE = math.log2(math.e) / math.sqrt(HEAD_SIZE)
ANY = pl.BlockSpec(memory_space=pl.ANY)
VMEM_LIMIT = 48 * 1024 * 1024


def round_up(value, unit):
    return (value + unit - 1) // unit * unit


def last_two(a, b):
    return lax.dot_general(a, b, (((1,), (1,)), ((), ())), preferred_element_type=jnp.float32)


def head_rows(refs, source, block, group):
    rows = slice(block * BLK, (block + 1) * BLK)
    parts = []
    for h in range(group):
        lanes = slice(h * HEAD_SIZE, (h + 1) * HEAD_SIZE)
        part = refs[0][rows, lanes]
        if len(refs) == 2:
            part = jnp.where(source == 0, part, refs[1][rows, lanes])
        parts.append(part)
    return jnp.concatenate(parts, axis=0)


def selectors(n_query, group):
    shape = (n_query, group * BLK, LANES)
    head = lax.broadcasted_iota(jnp.int32, shape, 1) // BLK
    wanted = lax.broadcasted_iota(jnp.int32, shape, 0) * group + head
    return (lax.broadcasted_iota(jnp.int32, shape, 2) == wanted).astype(jnp.bfloat16)


def in_pipeline(count, scores_of, softmax_of, finish):
    scores = scores_of(0)
    waiting = None
    for n in range(count):
        following = scores_of(n + 1) if n + 1 < count else None
        current = softmax_of(n, scores)
        if waiting is not None:
            finish(*waiting)
        waiting = (n, *current)
        scores = following
    finish(*waiting)


def window_kernel(sizes, places, n_src, n_blk, group, pos_ref, *refs):
    n_pieces = len(sizes)
    pieces, refs = refs[:n_pieces], refs[n_pieces:]
    bias_ref, pick_ref, refs = refs[0], refs[1], refs[2:]
    q_refs, refs = refs[:n_src], refs[n_src:]
    acc_ref, ml_ref, table, kaug, vaug, sem = refs
    j, s = pl.program_id(0), pl.program_id(1)
    n_rows = table.shape[0]

    @pl.when((j == 0) & (s == 0))
    def _():
        copies = []
        for index in range(n_pieces):
            rows = pl.ds(places[index] * BLK, sizes[index])
            copies.append(
                pltpu.make_async_copy(pieces[index], table.at[rows], sem.at[index])
            )
        for copy in copies:
            copy.start()
        for copy in copies:
            copy.wait()

    @pl.when(s == 0)
    def _():
        col = pl.multiple_of(j * 2 * HEAD_SIZE, 2 * HEAD_SIZE)
        kaug[:, :HEAD_SIZE] = table[:, pl.ds(col, HEAD_SIZE)]
        vaug[:, :HEAD_SIZE] = table[:, pl.ds(col + HEAD_SIZE, HEAD_SIZE)]
        vaug[:, HEAD_SIZE:] = jnp.ones((n_rows, LANES), jnp.bfloat16)
        for w in range(n_rows // BLK):
            row = jnp.broadcast_to(bias_ref[0, w:w + 1, :], (BLK, LANES))
            kaug[w * BLK:(w + 1) * BLK, HEAD_SIZE:] = row.astype(jnp.bfloat16)

    core = pos_ref[0]
    base = 0 if n_src == 1 else jnp.where(s == 0, core, 1 - core) * n_blk
    span = (SMAX + 1) * BLK
    edge = span - LANES
    rows = group * BLK
    u = lax.broadcasted_iota(jnp.int32, (rows, LANES), 1) - (LANES - BLK)
    t = lax.broadcasted_iota(jnp.int32, (rows, LANES), 0) % BLK
    lane = lax.broadcasted_iota(jnp.int32, (rows, LANES), 1)

    def keys_of(n):
        return pl.ds(pl.multiple_of((base + n) * BLK, BLK), span)

    def scores_of(n):
        q = jnp.concatenate([head_rows(q_refs, s, n, group), pick_ref[base + n]], axis=1)
        return last_two(q, kaug[keys_of(n), :])

    def softmax_of(n, scores):
        last = jnp.where(u > t, NEG, scores[:, edge:])
        scores = jnp.concatenate([scores[:, :edge], last], axis=1)
        top = jnp.max(scores, axis=1, keepdims=True)
        return top, jnp.exp2((scores - top) * SCALE).astype(jnp.bfloat16)

    def finish(n, top, weights):
        total = jnp.dot(weights, vaug[keys_of(n), :], preferred_element_type=jnp.float32)
        acc_ref[0, 0, n] = total[:, :HEAD_SIZE]
        ml_ref[0, 0, n] = jnp.where(lane < LANES // 2, top, total[:, HEAD_SIZE:])

    in_pipeline(n_blk, scores_of, softmax_of, finish)


def window_part(pos, pieces, places, bias, picks, queries, q_recv, n_kv, n_src, n_blk, group, n_win):
    width = group * HEAD_SIZE
    rows = group * BLK
    n_rows = n_win * BLK
    q_specs = [pl.BlockSpec((n_blk * BLK, width), lambda j, s, pos: (0, pos[0] * n_kv + j))]
    q_args = [queries]
    if n_src == 2:
        q_specs.append(pl.BlockSpec((n_blk * BLK, width), lambda j, s, pos: (0, j)))
        q_args.append(q_recv)
    out_spec = pl.BlockSpec((1, 1, n_blk, rows, LANES), lambda j, s, pos: (j, s, 0, 0, 0))
    out_shape = jax.ShapeDtypeStruct((n_kv, n_src, n_blk, rows, LANES), jnp.float32)
    sizes = [piece.shape[0] for piece in pieces]
    keys = n_kv * n_src * n_blk * rows * (SMAX + 1) * BLK
    return pl.pallas_call(
        functools.partial(window_kernel, sizes, places, n_src, n_blk, group),
        grid_spec=pltpu.PrefetchScalarGridSpec(
            num_scalar_prefetch=1,
            grid=(n_kv, n_src),
            in_specs=[ANY] * len(pieces)
            + [
                pl.BlockSpec((1, bias.shape[1], LANES), lambda j, s, pos: (j, 0, 0)),
                pl.BlockSpec(memory_space=pltpu.VMEM),
            ]
            + q_specs,
            out_specs=[out_spec, out_spec],
            scratch_shapes=[
                pltpu.VMEM((n_rows, n_kv * 2 * HEAD_SIZE), jnp.bfloat16),
                pltpu.VMEM((n_rows, 2 * LANES), jnp.bfloat16),
                pltpu.VMEM((n_rows, 2 * LANES), jnp.bfloat16),
                pltpu.SemaphoreType.DMA((len(pieces),)),
            ],
        ),
        out_shape=[out_shape, out_shape],
        compiler_params=pltpu.CompilerParams(vmem_limit_bytes=VMEM_LIMIT),
        cost_estimate=pl.CostEstimate(
            flops=keys * 1024, bytes_accessed=16 * 1024 * 1024, transcendentals=keys
        ),
    )(pos, *pieces, bias, picks, *q_args)


def vertical_kernel(sources, first_kv, n_vert, group, n_blk, n_src, n_dst, other, pos_ref, *refs):
    n_pieces = max(source[0] for source in sources) + 1
    pieces, refs = refs[:n_pieces], refs[n_pieces:]
    bias_ref, pick_ref, refs = refs[0], refs[1], refs[2:]
    q_refs, refs = refs[:n_src], refs[n_src:]
    acc_ref, ml_ref, refs = refs[0], refs[1], refs[2:]
    outs, (table, kaug, vaug, sem) = refs[:n_src], refs[n_src:]
    j, s = pl.program_id(0), pl.program_id(1)
    per_dst = n_blk // n_dst
    n_keys = kaug.shape[0]
    group_rows = n_vert * PIECE

    @pl.when(s == 0)
    def _():
        copies = []
        for index, (piece, part) in enumerate(sources):
            copies.append(
                pltpu.make_async_copy(
                    pieces[piece].at[part, first_kv + j], table.at[pos_ref[2 + index]], sem.at[index]
                )
            )
        for copy in copies:
            copy.start()
        used = (N_PIECES // 2) * group_rows
        if used < n_keys:
            empty = (n_keys - used, LANES)
            kaug[used:, :HEAD_SIZE] = jnp.zeros(empty, jnp.bfloat16)
            vaug[used:, :HEAD_SIZE] = jnp.zeros(empty, jnp.bfloat16)
            kaug[used:, HEAD_SIZE:] = jnp.full(empty, NEG, jnp.bfloat16)
        vaug[:, HEAD_SIZE:] = jnp.ones((n_keys, LANES), jnp.bfloat16)
        for unit in range(n_vert):
            row = jnp.broadcast_to(bias_ref[0, unit:unit + 1, :], (PIECE, LANES))
            row = row.astype(jnp.bfloat16)
            for rg in range(N_PIECES // 2):
                at = rg * group_rows + unit * PIECE
                kaug[at:at + PIECE, HEAD_SIZE:] = row
        for copy in copies:
            copy.wait()
        for rg in range(N_PIECES // 2):
            at = slice(rg * group_rows, (rg + 1) * group_rows)
            kaug[at, :HEAD_SIZE] = table[2 * rg]
            vaug[at, :HEAD_SIZE] = table[2 * rg + 1]

    core, tp_pos = pos_ref[0], pos_ref[1]
    base = 0
    if n_dst > 1:
        base = (1 - tp_pos if other else tp_pos) * per_dst
    if n_src > 1:
        base = base + jnp.where(s == 0, core, 1 - core) * n_blk

    def scores_of(n):
        q = jnp.concatenate([head_rows(q_refs, s, n, group), pick_ref[base + n]], axis=1)
        return last_two(q, kaug[...])

    def softmax_of(n, scores):
        old_top = ml_ref[0, 0, n][:, :1]
        top = jnp.maximum(old_top, jnp.max(scores, axis=1, keepdims=True))
        shrink = jnp.exp2((old_top - top) * SCALE)
        return shrink, jnp.exp2((scores - top) * SCALE).astype(jnp.bfloat16)

    def finish(n, shrink, weights):
        total = jnp.dot(weights, vaug[...], preferred_element_type=jnp.float32)
        old_total = ml_ref[0, 0, n][:, LANES // 2:LANES // 2 + 1]
        weighted = total[:, :HEAD_SIZE] + acc_ref[0, 0, n] * shrink
        out = (weighted / (total[:, HEAD_SIZE:] + old_total * shrink)).astype(jnp.bfloat16)
        out = jnp.concatenate([out[h * BLK:(h + 1) * BLK] for h in range(group)], axis=1)
        for source in range(n_src):

            @pl.when(s == source)
            def _():
                outs[source][n * BLK:(n + 1) * BLK, :] = out

    in_pipeline(per_dst, scores_of, softmax_of, finish)


def vertical_part(
    pos, pieces, sources, first_kv, kvs, bias, picks, queries, q_recv, state,
    n_kv, n_src, n_dst, other, n_blk, group, n_vert,
):
    width = group * HEAD_SIZE
    rows = group * BLK
    per_dst = n_blk // n_dst
    n_keys = round_up(n_vert * BLK, LANES)

    def place(pos):
        if n_dst == 1:
            return 0
        return 1 - pos[1] if other else pos[1]

    q_specs = [
        pl.BlockSpec(
            (per_dst * BLK, width), lambda j, s, pos: (place(pos), pos[0] * n_kv + first_kv + j)
        )
    ]
    q_args = [queries]
    if n_src == 2:
        q_specs.append(
            pl.BlockSpec((per_dst * BLK, width), lambda j, s, pos: (place(pos), first_kv + j))
        )
        q_args.append(q_recv)
    state_spec = pl.BlockSpec(
        (1, 1, per_dst, rows, LANES), lambda j, s, pos: (first_kv + j, s, place(pos), 0, 0)
    )
    out_spec = pl.BlockSpec((per_dst * BLK, width), lambda j, s, pos: (0, j))
    out_shape = jax.ShapeDtypeStruct((per_dst * BLK, width * kvs), jnp.bfloat16)
    keys = kvs * n_src * per_dst * rows * n_keys
    return pl.pallas_call(
        functools.partial(
            vertical_kernel, sources, first_kv, n_vert, group, n_blk, n_src, n_dst, other
        ),
        grid_spec=pltpu.PrefetchScalarGridSpec(
            num_scalar_prefetch=1,
            grid=(kvs, n_src),
            in_specs=[ANY] * len(pieces)
            + [
                pl.BlockSpec((1, bias.shape[1], LANES), lambda j, s, pos: (first_kv + j, 0, 0)),
                pl.BlockSpec(memory_space=pltpu.VMEM),
            ]
            + q_specs
            + [state_spec, state_spec],
            out_specs=[out_spec] * n_src,
            scratch_shapes=[
                pltpu.VMEM((N_PIECES, n_vert * PIECE, LANES), jnp.bfloat16),
                pltpu.VMEM((n_keys, 2 * LANES), jnp.bfloat16),
                pltpu.VMEM((n_keys, 2 * LANES), jnp.bfloat16),
                pltpu.SemaphoreType.DMA((N_PIECES,)),
            ],
        ),
        out_shape=[out_shape] * n_src,
        compiler_params=pltpu.CompilerParams(vmem_limit_bytes=VMEM_LIMIT),
        cost_estimate=pl.CostEstimate(
            flops=keys * 1024, bytes_accessed=8 * 1024 * 1024, transcendentals=keys
        ),
    )(pos, *pieces, bias, picks, *q_args, *state)


def select_kernel(n_kv, n_vert, index_ref, table, *outs):
    for j in range(n_kv):
        for unit in range(n_vert):
            outs[j][unit * PIECE:(unit + 1) * PIECE, :] = table[index_ref[j * n_vert + unit]]


def select_units(index, table, n_kv, n_vert):
    return pl.pallas_call(
        functools.partial(select_kernel, n_kv, n_vert),
        in_specs=[
            pl.BlockSpec(memory_space=pltpu.SMEM),
            pl.BlockSpec(memory_space=pltpu.VMEM),
        ],
        out_specs=[pl.BlockSpec(memory_space=pltpu.VMEM)] * n_kv,
        out_shape=[jax.ShapeDtypeStruct((n_vert * PIECE, LANES), jnp.bfloat16)] * n_kv,
        compiler_params=pltpu.CompilerParams(vmem_limit_bytes=8 * 1024 * 1024),
    )(index, table)


def assemble_kernel(width, n, column_ref, *refs):
    for index in range(n):
        start = pl.multiple_of(column_ref[index] * width, width)
        refs[n][:, pl.ds(start, width)] = refs[index][...]


def assemble(columns, pieces):
    n = len(pieces)
    rows, width = pieces[0].shape
    step = 32
    return pl.pallas_call(
        functools.partial(assemble_kernel, width, n),
        grid_spec=pltpu.PrefetchScalarGridSpec(
            num_scalar_prefetch=1,
            grid=(rows // step,),
            in_specs=[pl.BlockSpec((step, width), lambda i, columns: (i, 0))] * n,
            out_specs=pl.BlockSpec((step, width * n), lambda i, columns: (i, 0)),
        ),
        out_shape=jax.ShapeDtypeStruct((rows, width * n), pieces[0].dtype),
    )(columns, *pieces)


def mask_tables(vert, slash, first, n_query, n_win, n_vert, n_blocks):
    n_kv, group = vert.shape[:2]
    blocks = jnp.arange(n_blocks, dtype=jnp.int32)
    present = jnp.any(vert.reshape(n_kv, -1)[:, :, None] == blocks, axis=1)
    before = blocks[None, :] < blocks[:, None]
    rank = jnp.sum((present[:, None, :] & before[None]).astype(jnp.int32), axis=2)
    unit = jnp.arange(n_vert, dtype=jnp.int32)
    here = present[:, None, :] & (rank[:, None, :] == unit[None, :, None])
    units = jnp.sum(jnp.where(here, blocks, 0), axis=2)

    query = first + jnp.arange(n_query, dtype=jnp.int32)
    window = first - SMAX + jnp.arange(n_win, dtype=jnp.int32)
    offset = query[None, :] - window[:, None]
    by_slash = jnp.any(offset[None, :, :, None, None] == slash[:, None, None, :, :], axis=4)
    by_vert = jnp.any(window[None, :, None, None] == vert[:, None, :, :], axis=3)
    near = (offset >= 0) & (offset <= SMAX) & (window >= 0)[:, None]
    live_w = near[None, :, :, None] & (by_slash | by_vert[:, :, None, :])
    listed = jnp.any(units[:, :, None, None] == vert[:, None, :, :], axis=3)
    far = query[None, None, :] - units[:, :, None] > SMAX
    live_v = far[:, :, :, None] & listed[:, :, None, :]

    def as_rows(live):
        rows = live.shape[1]
        bias = jnp.where(live, 0.0, NEG).astype(jnp.float32).reshape(n_kv, rows, n_query * group)
        pad = ((0, 0), (0, round_up(rows, 8) - rows), (0, LANES - n_query * group))
        return jnp.pad(bias, pad)

    return units, as_rows(live_w), as_rows(live_v)


def paired(queries, kv_rows, vertical, slash):
    n_seq = lax.axis_size("seq")
    n_chip = n_seq // 2
    n_far = n_chip // 2
    tok = queries.shape[0]
    n_blk = tok // BLK
    seq_pos, tp_pos = lax.axis_index("seq"), lax.axis_index("tp")
    core, chip = seq_pos % 2, seq_pos // 2
    near, far = chip % 2, chip // 2
    heads_loc = vertical.shape[0] // 2
    kv_loc = kv_rows.shape[1] // (2 * HEAD_SIZE)
    group = heads_loc // kv_loc
    n_kv = kv_loc // 2
    heads = n_kv * group
    n_blocks = n_seq * n_blk
    n_vert = vertical.shape[1] * 3 // 2 - 1
    n_query = 2 * n_blk
    n_win = n_query + SMAX
    kv_width = n_kv * 2 * HEAD_SIZE
    q_width = heads * HEAD_SIZE

    def by_chip(array, target):
        pairs = []
        for source in range(n_seq):
            to = target(source // 2)
            if to is not None:
                pairs.append((source, 2 * to + source % 2))
        return lax.ppermute(array, "seq", pairs)

    split = kv_rows.reshape(n_blk, BLK // PIECE, PIECE, 2, n_kv, 2, LANES)
    split = jnp.transpose(split, (1, 5, 3, 0, 4, 2, 6)).reshape(n_seq, n_blk * n_kv, PIECE, LANES)
    held = lax.all_to_all(split, "seq", split_axis=0, concat_axis=0, tiled=True)
    held = held.reshape(n_blocks * n_kv, PIECE, LANES)

    to_pair = jnp.concatenate(
        [
            lax.dynamic_slice_in_dim(queries, (1 - core) * q_width, q_width, 1),
            lax.dynamic_slice_in_dim(kv_rows, (1 - core) * kv_width, kv_width, 1),
        ],
        axis=1,
    )
    from_pair = lax.ppermute(to_pair, "seq", [(i, i ^ 1) for i in range(n_seq)])
    mine = lax.dynamic_slice_in_dim(kv_rows, core * kv_width, kv_width, 1)
    theirs = from_pair[:, q_width:]
    here = jnp.where(
        core == 0,
        jnp.concatenate([mine, theirs], axis=0),
        jnp.concatenate([theirs, mine], axis=0),
    )
    extra = SMAX - n_query
    before = by_chip(here, lambda c: c + 1 if c + 1 < n_chip else None)
    back = by_chip(here[-extra * BLK:], lambda c: c + 2 if c + 2 < n_chip else None)

    first_head = tp_pos * heads_loc + core * heads
    my_vert = lax.dynamic_slice_in_dim(vertical, first_head, heads, 0).reshape(n_kv, group, -1)
    my_slash = lax.dynamic_slice_in_dim(slash, first_head, heads, 0).reshape(n_kv, group, -1)
    units, bias_w, bias_v = mask_tables(
        my_vert, my_slash, chip * n_query, n_query, n_win, n_vert, n_blocks
    )
    picks = selectors(n_query, group)

    index = (units * n_kv + jnp.arange(n_kv, dtype=jnp.int32)[:, None]).reshape(-1)
    picked = jnp.stack(select_units(index, held, n_kv, n_vert))
    beside = by_chip(picked, lambda c: c ^ 1)
    both = jnp.where(near == 0, jnp.stack([picked, beside]), jnp.stack([beside, picked]))
    pieces, sources, slots = [both], [(0, 0), (0, 1)], [2 * far, 2 * far + 1]
    for step in range(1, n_far):
        pieces.append(by_chip(both, lambda c: (c + 2 * step) % n_chip))
        sources += [(step, 0), (step, 1)]
        owner = (far - step) % n_far
        slots += [2 * owner, 2 * owner + 1]

    pos = jnp.stack([core, tp_pos] + slots).astype(jnp.int32)
    state = window_part(
        pos, [here, before, back], [SMAX, extra, 0], bias_w, picks, queries, from_pair,
        n_kv, 2, n_blk, group, n_win,
    )

    def swap(array, other_core, other_tp):
        pairs = []
        for source in range(n_seq):
            for t in range(2):
                pairs.append((source * 2 + t, (source ^ other_core) * 2 + (t ^ other_tp)))
        return lax.ppermute(array, ("seq", "tp"), pairs)

    results, columns = [], []
    for other_tp in (1, 0):
        outs = vertical_part(
            pos, pieces, sources, 0, n_kv, bias_v, picks, queries, from_pair, state,
            n_kv, 2, 2, other_tp, n_blk, group, n_vert,
        )
        for other_core in range(2):
            piece = outs[other_core]
            if other_core or other_tp:
                piece = swap(piece, other_core, other_tp)
            results.append(piece)
            from_tp = 1 - tp_pos if other_tp else tp_pos
            from_core = 1 - core if other_core else core
            columns.append(from_tp * 2 + from_core)
    return assemble(jnp.stack(columns).astype(jnp.int32), results)


def gathered(queries, kv_rows, vertical, slash):
    n_seq, n_tp = lax.axis_size("seq"), lax.axis_size("tp")
    tok = queries.shape[0]
    n_blk = tok // BLK
    seq_pos, tp_pos = lax.axis_index("seq"), lax.axis_index("tp")
    heads = vertical.shape[0] // n_tp
    n_kv = kv_rows.shape[1] // (2 * HEAD_SIZE)
    group = heads // n_kv
    n_blocks = n_seq * n_blk
    n_vert = vertical.shape[1] * 3 // 2 - 1
    n_win = n_blk + SMAX
    first = seq_pos * n_blk
    my_vert = lax.dynamic_slice_in_dim(vertical, tp_pos * heads, heads, 0)
    my_slash = lax.dynamic_slice_in_dim(slash, tp_pos * heads, heads, 0)
    units, bias_w, bias_v = mask_tables(
        my_vert.reshape(n_kv, group, -1), my_slash.reshape(n_kv, group, -1),
        first, n_blk, n_win, n_vert, n_blocks,
    )
    picks = selectors(n_blk, group)
    full = lax.all_gather(kv_rows, "seq", axis=0, tiled=True)
    padded = jnp.pad(full, ((SMAX * BLK, 0), (0, 0)))
    window = lax.dynamic_slice_in_dim(padded, first * BLK, n_win * BLK, 0)
    pos = jnp.stack([jnp.int32(0), tp_pos] + [jnp.int32(i) for i in range(N_PIECES)])
    state = window_part(
        pos, [window], [0], bias_w, picks, queries, None, n_kv, 1, n_blk, group, n_win
    )
    blocks = full.reshape(n_blocks, BLK // PIECE, PIECE, n_kv, 2, LANES)
    listed = jnp.stack([blocks[units[j], :, :, j] for j in range(n_kv)])
    listed = jnp.transpose(listed, (2, 4, 0, 1, 3, 5))
    listed = listed.reshape(N_PIECES, n_kv, n_vert * PIECE, LANES)
    (attended,) = vertical_part(
        pos, [listed], [(0, i) for i in range(N_PIECES)], 0, n_kv, bias_v, picks, queries, None,
        state, n_kv, 1, 1, 0, n_blk, group, n_vert,
    )
    return lax.all_to_all(attended, "tp", split_axis=0, concat_axis=1, tiled=True)


def per_device(queries, kv_rows, vertical, slash):
    n_seq, n_tp = lax.axis_size("seq"), lax.axis_size("tp")
    kv_loc = kv_rows.shape[1] // (2 * HEAD_SIZE)
    n_blk = queries.shape[0] // BLK
    if n_seq == 2 * N_PIECES and n_tp == 2 and kv_loc % 2 == 0 and n_blk == 4:
        return paired(queries, kv_rows, vertical, slash)
    return gathered(queries, kv_rows, vertical, slash)


def solution(mesh):
    return jax.shard_map(
        per_device,
        mesh=mesh,
        in_specs=(P("seq", "tp"), P("seq", "tp"), P(), P()),
        out_specs=P(("seq", "tp"), None),
        check_vma=False,
    )
```

time: 1330 us -> 102 us (0.08)
  loops' own time: 551 us -> 0 us
  local copies, waits for them, and re-layouts: 464 us -> 9.74 us
  matrix products: 114 us -> 0 us
  waiting for transfers between devices: 74.8 us -> 9.2 us
  other arithmetic: 70.6 us -> 6.88 us
  Pallas kernels: 0 us -> 48.1 us
  blocking collectives: 28.5 us -> 0 us
  starting transfers between devices: 0.01 us -> 26.7 us
    another operation x1 -> x0, loops' own time: 551 us -> none  [per_device(): outputs = lax.map(one_head, (qheads, my_vert, my_slash, owners))]
    while x224 -> x0, local copies, waits for them, and re-layouts: 207 us -> none
    gather x32 -> x0, local copies, waits for them, and re-layouts: 126 us -> none  [gather_rows(): vert_block = index_table[vertical_row, :, key_value_head]]
    dot_general x128 -> x0, matrix products: 114 us -> none  [the longest x32 36.7 us: attend(): jnp.einsum('unz,syz->unsy', query_block, vert_block[..., :HEAD_SIZE], pre...]
    all_gather x1 -> x0, waiting for transfers between devices: 74 us -> none  [per_device(): full = lax.all_gather(kv_rows, 'seq', axis=0, tiled=True)]
    pallas_call x0 -> x5, Pallas kernels: none -> 48.1 us  [the longest x2 29.3 us: vertical_part(): pl.pallas_call(functools.partial(vertical_kernel, sources, first_kv, n_ve...]
    reduce_sum x32 -> x2, other arithmetic: 30.9 us -> 0.4 us  [the longest x1 0.28 us: mask_tables(): units = jnp.sum(jnp.where(here, blocks, 0), axis=2)]
    another operation x32 -> x1, local copies, waits for them, and re-layouts: 29.5 us -> 0.09 us  [paired(): pos = jnp.stack([core, tp_pos] + slots).astype(jnp.int32)]
  transfers between devices with their start and end apart: 1 -> 11, of which waited for: 1 -> 3; matrix products, arithmetic and copies ran while one was open for 0% -> 12% of each run, Pallas kernels for 0% -> 29%
where the time goes in v1:
time: 102 us; the launch traced here: 101 us
  Pallas kernels  48.1 us (47%)
  starting transfers between devices  26.7 us (26%)
  local copies, waits for them, and re-layouts  9.74 us (10%)
  waiting for transfers between devices  9.2 us (9%)
  other arithmetic  6.88 us (7%)
    pallas_call x2, Pallas kernels, vertical_part(): pl.pallas_call(functools.partial(vertical_kernel, sources, first_kv, n_ve...  29.3 us
    ppermute x6, starting transfers between devices, by_chip(): return lax.ppermute(array, 'seq', pairs)  16.1 us
    pallas_call x1, Pallas kernels, window_part(): pl.pallas_call(functools.partial(window_kernel, sizes, places, n_src, n_b...  13.3 us
    all_to_all x1, starting transfers between devices, paired(): held = lax.all_to_all(split, 'seq', split_axis=0, concat_axis=0, tiled=True)  7.35 us
    ppermute x3, waiting for transfers between devices, swap(): return lax.ppermute(array, ('seq', 'tp'), pairs)  5.95 us
    pallas_call x1, Pallas kernels, assemble(): pl.pallas_call(functools.partial(assemble_kernel, width, n), grid_spec=pl...  4.49 us
    ppermute x3, starting transfers between devices, swap(): return lax.ppermute(array, ('seq', 'tp'), pairs)  3.03 us
    all_to_all x1, waiting for transfers between devices, paired(): held = lax.all_to_all(split, 'seq', split_axis=0, concat_axis=0, tiled=True)  2.44 us
  transfers between devices with their start and end apart: 11, of which 3 were waited for; matrix products, arithmetic and copies ran while one was open for 12% of the time, Pallas kernels for 29%

profile of v1, /device:TPU:1, one launch (start us, length us, event | category | flops | bytes accessed | tf_op | source)
XLA Modules:
  0.0 100.9 jit_solution(6724451770078001680)
XLA Ops:
  0.0 1.6 %reshape.150 = bf16[4,4,16,2,2,2,128]{6,5,4,3,2,1,0:T(2,128)(2,1)S(1)} reshape(bf16[256,1024]{1,0:T(8,128)(2,1)} %param.5) | data formatting | bytes 1048576 | tf_op jit(solution)/shard_map/reshape | solution.py:401
  1.6 0.9 copy.22
  2.4 7.3 %all-to-all-start = ((bf16[16,8,16,128]{3,2,1,0:T(8,128)(2,1)}), bf16[16,8,16,128]{3,2,1,0:T(8,128)(2,1)}, u32[]{:S(2)}, u32[]{:S(2)}) async-start(bf16[16,8,16,128]{3,2,1,0:T(8,128)(2,1)} %bitcast.15), calls=%async_computation | async-start | bytes 1048576 | tf_op jit(solution)/shard_map/all_to_all | solution.py:403
  10.0 1.1 %pad_maximum_fusion = bf16[256,2560]{1,0:T(8,128)(2,1)} fusion(bf16[256,512]{1,0:T(8,128)(2,1)S(1)} %get-tuple-element.22, bf16[256,2048]{1,0:T(8,128)(2,1)S(1)} %constant_dynamic-slice_fusion.3), kind=kLoop, calls=%fused_computation.2 | loop fusion | flops 2621440 | bytes 2621440 | tf_op jit(solution)/shard_map/concatenate | solution.py:406
  11.1 0.2 collective-permute-start.4
  11.6 0.1 fusion.1
  11.7 0.1 convert_reduce_fusion
  11.9 0.3 fusion.2
  12.2 0.1 copy.23
  12.2 0.1 subtract_compare_fusion
  12.4 0.1 compare_reduce_fusion.1
  12.5 0.1 compare_reduce_fusion.2
  12.8 0.2 compare_reduce_fusion
  13.1 0.1 copy.25
  13.2 0.1 and_select_fusion
  13.3 0.4 fusion.refs_4_.refs_5_
  13.7 0.8 collective-permute-done.4.refs_6_.refs_7_
  14.5 1.0 slice.8
  15.5 1.0 %maximum_select_fusion.refs_0_ = bf16[512,512]{1,0:T(8,128)(2,1)} fusion(bf16[256,512]{1,0:T(8,128)(2,1)S(1)} %slice.8, bf16[256,512]{1,0:T(8,128)(2,1)S(1)} %get-tuple-element.21, pred[]{:T(512)S(6)} %eq.103), kind=kLoop, calls=%fused_computation.3 | loop fusion | flops 2359296 | bytes 1048577 | tf_op jit(solution)/shard_map/jit(_where)/select_n | solution.py:416
  16.5 4.1 %collective-permute-start.5 = (bf16[512,512]{1,0:T(8,128)(2,1)}, bf16[512,512]{1,0:T(8,128)(2,1)}, u32[]{:S(2)}, u32[]{:S(2)}) collective-permute-start(bf16[512,512]{1,0:T(8,128)(2,1)} %maximum_select_fusion.refs_0_), channel_id=1, source_target_pairs={{0,4},{2,6},{4,8},{6,10},{8,12},{10,14},{12,16},{14,18},{16,20},{1... | collective-permute-start | bytes 1572872 | tf_op jit(solution)/shard_map/ppermute | solution.py:399
  20.6 0.1 copy.21
  20.7 0.1 add.135.index_ref
  20.7 0.1 copy.30
  20.8 0.7 copy.27
  21.5 2.4 %all-to-all-done = bf16[16,8,16,128]{3,2,1,0:T(8,128)(2,1)} async-done(((bf16[16,8,16,128]{3,2,1,0:T(8,128)(2,1)}), bf16[16,8,16,128]{3,2,1,0:T(8,128)(2,1)}, u32[]{:S(2)}, u32[]{:S(2)}) %all-to-all-start) | async-done | bytes 524320 | tf_op jit(solution)/shard_map/all_to_all | solution.py:403
  24.0 1.1 %shard_map.46 = (bf16[176,128]{1,0:T(8,128)(2,1)S(1)}, bf16[176,128]{1,0:T(8,128)(2,1)S(1)}) custom-call(s32[22]{0:T(128)S(1)} %add.135.index_ref, bf16[128,16,128]{2,1,0:T(8,128)(2,1)} %bitcast.16.table), custom_call_target="tpu_custom_call" | custom-call | tf_op jit(solution)/shard_map/pallas_call | solution.py:308
  25.0 0.7 fusion.6
  25.7 0.9 collective-permute-start
  26.6 1.6 %slice.9 = bf16[192,512]{1,0:T(8,128)(2,1)} slice(bf16[512,512]{1,0:T(8,128)(2,1)} %maximum_select_fusion.refs_0_), slice={[320:512], [0:512]} | slice | bytes 393216 | tf_op jit(solution)/shard_map/slice | solution.py:423
  28.2 3.4 %collective-permute-start.6 = (bf16[192,512]{1,0:T(8,128)(2,1)}, bf16[192,512]{1,0:T(8,128)(2,1)S(1)}, u32[]{:S(2)}, u32[]{:S(2)}) collective-permute-start(bf16[192,512]{1,0:T(8,128)(2,1)} %slice.9), channel_id=1, source_target_pairs={{0,8},{2,10},{4,12},{6,14},{8,16},{10,18},{12,20},{14,22},{16,24},... | collective-permute-start | bytes 589832 | tf_op jit(solution)/shard_map/ppermute | solution.py:399
  31.6 0.7 and_select_fusion.1
  32.3 0.7 select_n.97
  33.0 0.7 copy.26
  33.7 0.1 stack.86.pos_ref
  33.8 1.0 maximum_select_fusion.1.refs_0_
  34.8 3.8 %collective-permute-start.1 = (bf16[2,2,176,128]{3,2,1,0:T(8,128)(2,1)S(1)}, bf16[2,2,176,128]{3,2,1,0:T(8,128)(2,1)S(1)}, u32[]{:S(2)}, u32[]{:S(2)}) collective-permute-start(bf16[2,2,176,128]{3,2,1,0:T(8,128)(2,1)S(1)} %maximum_select_fusion.1.refs_0_), channel_id=1, source_target_pairs={{0,8},{2,10},{4,12},{6,14},{8,16},{10,18},{12,20},{14,22},{16,24},... | collective-permute-start | bytes 540680 | tf_op jit(solution)/shard_map/ppermute | solution.py:399
  38.6 2.1 %collective-permute-start.2 = (bf16[2,2,176,128]{3,2,1,0:T(8,128)(2,1)S(1)}, bf16[2,2,176,128]{3,2,1,0:T(8,128)(2,1)S(1)}, u32[]{:S(2)}, u32[]{:S(2)}) collective-permute-start(bf16[2,2,176,128]{3,2,1,0:T(8,128)(2,1)S(1)} %maximum_select_fusion.1.refs_0_), channel_id=1, source_target_pairs={{0,16},{2,18},{4,20},{6,22},{8,24},{10,26},{12,28},{14,30},{16,0},... | collective-permute-start | bytes 540680 | tf_op jit(solution)/shard_map/ppermute | solution.py:399
  40.7 1.8 %collective-permute-start.3 = (bf16[2,2,176,128]{3,2,1,0:T(8,128)(2,1)S(1)}, bf16[2,2,176,128]{3,2,1,0:T(8,128)(2,1)S(1)}, u32[]{:S(2)}, u32[]{:S(2)}) collective-permute-start(bf16[2,2,176,128]{3,2,1,0:T(8,128)(2,1)S(1)} %maximum_select_fusion.1.refs_0_), channel_id=1, source_target_pairs={{0,24},{2,26},{4,28},{6,30},{8,0},{10,2},{12,4},{14,6},{16,8},{18,... | collective-permute-start | bytes 540680 | tf_op jit(solution)/shard_map/ppermute | solution.py:399
  42.5 13.3 %shard_map.47 = (f32[2,2,4,512,128]{4,3,2,1,0:T(8,128)}, f32[2,2,4,512,128]{4,3,2,1,0:T(8,128)}) custom-call(s32[10]{0:T(128)S(1)} %stack.86.pos_ref, bf16[512,512]{1,0:T(8,128)(2,1)} %maximum_select_fusion.refs_0_, bf16[512,512]{1,0:T(8,128)(2,1)} %collective-permute-done.5.refs_1_, bf16[192,512]{1,0:T(8,128)(2,1)S(1)} %collective-permute-done.6.refs_2_, ...), custom_call_target="tpu_custom_call" | custom-call | flops 6442450944 | bytes 16777216 | tf_op jit(solution)/shard_map/pallas_call | solution.py:138
  55.9 14.6 %shard_map.48 = (bf16[128,2048]{1,0:T(8,128)(2,1)S(1)}, bf16[128,2048]{1,0:T(8,128)(2,1)S(1)}) custom-call(s32[10]{0:T(128)S(1)} %stack.86.pos_ref, bf16[2,2,176,128]{3,2,1,0:T(8,128)(2,1)S(1)} %maximum_select_fusion.1.refs_0_, bf16[2,2,176,128]{3,2,1,0:T(8,128)(2,1)S(1)} %collective-permute-done.1.refs_1_, ...), custom_call_target="tpu_custom_call" | custom-call | flops 3221225472 | bytes 8388608 | tf_op jit(solution)/shard_map/pallas_call | solution.py:271
  70.5 1.3 %collective-permute-start.7 = (bf16[128,2048]{1,0:T(8,128)(2,1)S(1)}, bf16[128,2048]{1,0:T(8,128)(2,1)S(1)}, u32[]{:S(2)}, u32[]{:S(2)}) collective-permute-start(bf16[128,2048]{1,0:T(8,128)(2,1)S(1)} %get-tuple-element.17), channel_id=1, source_target_pairs={{0,1},{1,0},{2,3},{3,2},{4,5},{5,4},{6,7},{7,6},{8,9},{9,8},{10,11... | collective-permute-start | bytes 1572872 | tf_op jit(solution)/shard_map/ppermute | solution.py:455
  71.8 1.7 %collective-permute-start.8 = (bf16[128,2048]{1,0:T(8,128)(2,1)S(1)}, bf16[128,2048]{1,0:T(8,128)(2,1)}, u32[]{:S(2)}, u32[]{:S(2)}) collective-permute-start(bf16[128,2048]{1,0:T(8,128)(2,1)S(1)} %get-tuple-element.18), channel_id=1, source_target_pairs={{0,3},{1,2},{2,1},{3,0},{4,7},{5,6},{6,5},{7,4},{8,11},{9,10},{10,... | collective-permute-start | bytes 1572872 | tf_op jit(solution)/shard_map/ppermute | solution.py:455
  73.5 14.6 %shard_map.49 = (bf16[128,2048]{1,0:T(8,128)(2,1)S(1)}, bf16[128,2048]{1,0:T(8,128)(2,1)S(1)}) custom-call(s32[10]{0:T(128)S(1)} %stack.86.pos_ref, bf16[2,2,176,128]{3,2,1,0:T(8,128)(2,1)S(1)} %maximum_select_fusion.1.refs_0_, bf16[2,2,176,128]{3,2,1,0:T(8,128)(2,1)S(1)} %collective-permute-done.1.refs_1_, ...), custom_call_target="tpu_custom_call" | custom-call | flops 3221225472 | bytes 8388608 | tf_op jit(solution)/shard_map/pallas_call | solution.py:271
  88.2 0.8 copy-done.1
  89.0 0.7 pad_add_fusion.column_ref
  89.6 5.9 %collective-permute-done.8.refs_1_ = bf16[128,2048]{1,0:T(8,128)(2,1)} collective-permute-done((bf16[128,2048]{1,0:T(8,128)(2,1)S(1)}, bf16[128,2048]{1,0:T(8,128)(2,1)}, u32[]{:S(2)}, u32[]{:S(2)}) %collective-permute-start.8) | collective-permute-done | bytes 524320 | tf_op jit(solution)/shard_map/ppermute | solution.py:455
  95.6 0.8 copy-done.4
  96.4 4.5 %shard_map.50 = bf16[128,8192]{1,0:T(8,128)(2,1)} custom-call(s32[4]{0:T(128)} %pad_add_fusion.column_ref, bf16[128,2048]{1,0:T(8,128)(2,1)} %copy-done.3, bf16[128,2048]{1,0:T(8,128)(2,1)} %collective-permute-done.8.refs_1_, bf16[128,2048]{1,0:T(8,128)(2,1)} %copy-done.1, bf16[128,2048]{1,0:T(8,128)(2,1)} %copy-done.4), custom_call_target="tpu_custom_call" | custom-call | tf_op jit(solution)/shard_map/pallas_call | solution.py:330
  (41 shorter events, 0.7 us)
Async XLA Ops:
  0.0 9.8 %copy-start.2 = (bf16[256,1024]{1,0:T(8,128)(2,1)S(1)}, bf16[256,1024]{1,0:T(8,128)(2,1)}, u32[]{:S(2)}) copy-start(bf16[256,1024]{1,0:T(8,128)(2,1)} %param.5) | copy-start | bytes 1572868
  0.0 9.9 %copy-start = (bf16[256,4096]{1,0:T(8,128)(2,1)S(1)}, bf16[256,4096]{1,0:T(8,128)(2,1)}, u32[]{:S(2)}) copy-start(bf16[256,4096]{1,0:T(8,128)(2,1)} %refs_6_.3) | copy-start | bytes 6291460
  2.4 21.5 %all-to-all-start = ((bf16[16,8,16,128]{3,2,1,0:T(8,128)(2,1)}), bf16[16,8,16,128]{3,2,1,0:T(8,128)(2,1)}, u32[]{:S(2)}, u32[]{:S(2)}) async-start(bf16[16,8,16,128]{3,2,1,0:T(8,128)(2,1)} %bitcast.15), calls=%async_computation | async-start | bytes 1048576 | tf_op jit(solution)/shard_map/all_to_all | solution.py:403
  9.9 1.5 %copy-start.5 = (s32[64,8]{0,1:T(8,128)S(1)}, s32[64,8]{0,1:T(8,128)}, u32[]{:S(2)}) copy-start(s32[64,8]{0,1:T(8,128)} %param.7) | copy-start | bytes 6148
  9.9 1.5 %copy-start.6 = (s32[64,8]{0,1:T(8,128)S(1)}, s32[64,8]{0,1:T(8,128)}, u32[]{:S(2)}) copy-start(s32[64,8]{0,1:T(8,128)} %param.6) | copy-start | bytes 6148
  11.1 3.4 %collective-permute-start.4 = (bf16[256,2560]{1,0:T(8,128)(2,1)}, bf16[256,2560]{1,0:T(8,128)(2,1)}, u32[]{:S(2)}, u32[]{:S(2)}) collective-permute-start(bf16[256,2560]{1,0:T(8,128)(2,1)} %pad_maximum_fusion), channel_id=1, source_target_pairs={{0,2},{2,0},{4,6},{6,4},{8,10},{10,8},{12,14},{14,12},{16,18},{18,... | collective-permute-start | bytes 3932168 | tf_op jit(solution)/shard_map/ppermute | solution.py:413
  16.5 26.1 %collective-permute-start.5 = (bf16[512,512]{1,0:T(8,128)(2,1)}, bf16[512,512]{1,0:T(8,128)(2,1)}, u32[]{:S(2)}, u32[]{:S(2)}) collective-permute-start(bf16[512,512]{1,0:T(8,128)(2,1)} %maximum_select_fusion.refs_0_), channel_id=1, source_target_pairs={{0,4},{2,6},{4,8},{6,10},{8,12},{10,14},{12,16},{14,18},{16,20},{1... | collective-permute-start | bytes 1572872 | tf_op jit(solution)/shard_map/ppermute | solution.py:399
  25.7 8.1 %collective-permute-start = (bf16[2,176,128]{2,1,0:T(8,128)(2,1)}, bf16[2,176,128]{2,1,0:T(8,128)(2,1)}, u32[]{:S(2)}, u32[]{:S(2)}) collective-permute-start(bf16[2,176,128]{2,1,0:T(8,128)(2,1)} %get-tuple-element.24), channel_id=1, source_target_pairs={{0,4},{2,6},{4,0},{6,2},{8,12},{10,14},{12,8},{14,10},{16,20},{18,... | collective-permute-start | bytes 270344 | tf_op jit(solution)/shard_map/ppermute | solution.py:399
  28.2 14.3 %collective-permute-start.6 = (bf16[192,512]{1,0:T(8,128)(2,1)}, bf16[192,512]{1,0:T(8,128)(2,1)S(1)}, u32[]{:S(2)}, u32[]{:S(2)}) collective-permute-start(bf16[192,512]{1,0:T(8,128)(2,1)} %slice.9), channel_id=1, source_target_pairs={{0,8},{2,10},{4,12},{6,14},{8,16},{10,18},{12,20},{14,22},{16,24},... | collective-permute-start | bytes 589832 | tf_op jit(solution)/shard_map/ppermute | solution.py:399
  34.8 21.0 %collective-permute-start.1 = (bf16[2,2,176,128]{3,2,1,0:T(8,128)(2,1)S(1)}, bf16[2,2,176,128]{3,2,1,0:T(8,128)(2,1)S(1)}, u32[]{:S(2)}, u32[]{:S(2)}) collective-permute-start(bf16[2,2,176,128]{3,2,1,0:T(8,128)(2,1)S(1)} %maximum_select_fusion.1.refs_0_), channel_id=1, source_target_pairs={{0,8},{2,10},{4,12},{6,14},{8,16},{10,18},{12,20},{14,22},{16,24},... | collective-permute-start | bytes 540680 | tf_op jit(solution)/shard_map/ppermute | solution.py:399
  38.6 17.3 %collective-permute-start.2 = (bf16[2,2,176,128]{3,2,1,0:T(8,128)(2,1)S(1)}, bf16[2,2,176,128]{3,2,1,0:T(8,128)(2,1)S(1)}, u32[]{:S(2)}, u32[]{:S(2)}) collective-permute-start(bf16[2,2,176,128]{3,2,1,0:T(8,128)(2,1)S(1)} %maximum_select_fusion.1.refs_0_), channel_id=1, source_target_pairs={{0,16},{2,18},{4,20},{6,22},{8,24},{10,26},{12,28},{14,30},{16,0},... | collective-permute-start | bytes 540680 | tf_op jit(solution)/shard_map/ppermute | solution.py:399
  40.7 15.1 %collective-permute-start.3 = (bf16[2,2,176,128]{3,2,1,0:T(8,128)(2,1)S(1)}, bf16[2,2,176,128]{3,2,1,0:T(8,128)(2,1)S(1)}, u32[]{:S(2)}, u32[]{:S(2)}) collective-permute-start(bf16[2,2,176,128]{3,2,1,0:T(8,128)(2,1)S(1)} %maximum_select_fusion.1.refs_0_), channel_id=1, source_target_pairs={{0,24},{2,26},{4,28},{6,30},{8,0},{10,2},{12,4},{14,6},{16,8},{18,... | collective-permute-start | bytes 540680 | tf_op jit(solution)/shard_map/ppermute | solution.py:399
  70.5 19.1 %collective-permute-start.7 = (bf16[128,2048]{1,0:T(8,128)(2,1)S(1)}, bf16[128,2048]{1,0:T(8,128)(2,1)S(1)}, u32[]{:S(2)}, u32[]{:S(2)}) collective-permute-start(bf16[128,2048]{1,0:T(8,128)(2,1)S(1)} %get-tuple-element.17), channel_id=1, source_target_pairs={{0,1},{1,0},{2,3},{3,2},{4,5},{5,4},{6,7},{7,6},{8,9},{9,8},{10,11... | collective-permute-start | bytes 1572872 | tf_op jit(solution)/shard_map/ppermute | solution.py:455
  71.8 23.8 %collective-permute-start.8 = (bf16[128,2048]{1,0:T(8,128)(2,1)S(1)}, bf16[128,2048]{1,0:T(8,128)(2,1)}, u32[]{:S(2)}, u32[]{:S(2)}) collective-permute-start(bf16[128,2048]{1,0:T(8,128)(2,1)S(1)} %get-tuple-element.18), channel_id=1, source_target_pairs={{0,3},{1,2},{2,1},{3,0},{4,7},{5,6},{6,5},{7,4},{8,11},{9,10},{10,... | collective-permute-start | bytes 1572872 | tf_op jit(solution)/shard_map/ppermute | solution.py:455
  88.2 0.8 copy-start.1
  89.0 6.6 %collective-permute-start.9 = (bf16[128,2048]{1,0:T(8,128)(2,1)S(1)}, bf16[128,2048]{1,0:T(8,128)(2,1)S(1)}, u32[]{:S(2)}, u32[]{:S(2)}) collective-permute-start(bf16[128,2048]{1,0:T(8,128)(2,1)S(1)} %get-tuple-element.20), channel_id=1, source_target_pairs={{0,2},{1,3},{2,0},{3,1},{4,6},{5,7},{6,4},{7,5},{8,10},{9,11},{10,... | collective-permute-start | bytes 1572872 | tf_op jit(solution)/shard_map/ppermute | solution.py:455
  89.6 6.0 %copy-start.3 = (bf16[128,2048]{1,0:T(8,128)(2,1)}, bf16[128,2048]{1,0:T(8,128)(2,1)S(1)}, u32[]{:S(2)}) copy-start(bf16[128,2048]{1,0:T(8,128)(2,1)S(1)} %collective-permute-done.7.refs_0_) | copy-start | bytes 1572868
  95.6 0.8 copy-start.4

commit v2 on v1

v2 whole, which is shorter than its diff:
```python
import functools
import math

import jax
import jax.numpy as jnp
from jax import lax
from jax.experimental import pallas as pl
from jax.experimental.pallas import tpu as pltpu
from jax.sharding import PartitionSpec as P

HEAD_SIZE = 128
BLK = 64
SMAX = 11
PIECE = 16
N_PIECES = (BLK // PIECE) * 2
LANES = 128
NEG = -1e30
SCALE = math.log2(math.e) / math.sqrt(HEAD_SIZE)
LOG_SCALE = math.sqrt(HEAD_SIZE)
ANY = pl.BlockSpec(memory_space=pl.ANY)


VMEM_LIMIT = 32 * 1024 * 1024
ALL_VMEM = 60 * 1024 * 1024


def round_up(value, unit):
    return (value + unit - 1) // unit * unit


def head_rows(ref, block, group):
    rows = slice(block * BLK, (block + 1) * BLK)
    heads = [ref[rows, h * HEAD_SIZE:(h + 1) * HEAD_SIZE] for h in range(group)]
    return jnp.concatenate(heads, axis=0)


def with_selector(q, block, group):
    shape = (q.shape[0], LANES)
    wanted = lax.broadcasted_iota(jnp.int32, shape, 0) // BLK + block * group
    pick = lax.broadcasted_iota(jnp.int32, shape, 1) == wanted
    return jnp.concatenate([q, jnp.where(pick, 1.0, 0.0).astype(jnp.bfloat16)], axis=1)


def in_pipeline(count, scores_of, softmax_of, finish):
    scores = scores_of(0)
    waiting = None
    for n in range(count):
        following = scores_of(n + 1) if n + 1 < count else None
        current = softmax_of(n, scores)
        if waiting is not None:
            finish(*waiting)
        waiting = (n, *current)
        scores = following
    finish(*waiting)


def tiles(array):
    return [array[:, at:at + LANES] for at in range(0, array.shape[1], LANES)]


def row_top(parts):
    top = functools.reduce(jnp.maximum, parts)
    return jnp.broadcast_to(jnp.max(top, axis=1, keepdims=True), top.shape)


def exponents(parts, top):
    return jnp.concatenate(
        [jnp.exp2((part - top) * SCALE).astype(jnp.bfloat16) for part in parts], axis=1
    )


def start_all(copies):
    for copy in copies:
        copy.start()


def wait_all(copies):
    for copy in copies:
        copy.wait()


def spread_mask(table, block_of_key, n_keys):
    shape = (LANES, n_keys)
    key = lax.broadcasted_iota(jnp.int32, shape, 1)
    own = lax.broadcasted_iota(jnp.int32, shape, 0) == block_of_key(key)
    own = jnp.where(own, 1.0, 0.0).astype(jnp.bfloat16)
    return jnp.dot(table, own, preferred_element_type=jnp.float32).astype(jnp.bfloat16)


def window_kernel(sizes, places, n_kv, n_src, n_blk, group, pos_ref, *refs):
    n_pieces = len(sizes)
    pieces, refs = refs[:n_pieces], refs[n_pieces:]
    bias_ref, refs = refs[0], refs[1:]
    q_in, refs = refs[:n_src], refs[n_src:]
    acc_out, lse_out, table, mask, kaug, vaug, q_ref, acc_ref, lse_ref, sem, turn_sem = refs
    core = pos_ref[0]
    n_rows = table.shape[1]
    n_lanes = kaug.shape[3]
    n_mask = bias_ref.shape[1]
    width = group * HEAD_SIZE
    span = (SMAX + 1) * BLK
    rows = group * BLK
    tok = n_blk * BLK
    n_pairs = n_src * n_blk // 2
    count = iter(range(sem.shape[0]))

    loads = []
    for j in range(n_kv):
        mine = []
        lanes = pl.ds(j * 2 * HEAD_SIZE, 2 * HEAD_SIZE)
        for index in range(n_pieces):
            at = pl.ds(places[index] * BLK, sizes[index])
            mine.append((pieces[index].at[:, lanes], table.at[j, at]))
        mine.append((bias_ref.at[j], mask.at[j]))
        first = pl.multiple_of((core * n_kv + j) * width, width)
        q_lanes = [pl.ds(first, width), pl.ds(j * width, width)]
        for source in range(n_src):
            at = pl.ds((j * n_src + source) * tok, tok)
            mine.append((q_in[source].at[:, q_lanes[source]], q_ref.at[at]))
        loads.append([pltpu.make_async_copy(*pair, sem.at[next(count)]) for pair in mine])
    for mine in loads:
        start_all(mine)
    for j in range(n_kv):
        vaug[j, :, HEAD_SIZE:] = jnp.ones((n_rows, LANES), jnp.bfloat16)
        for odd in range(2):
            kaug[j, odd, HEAD_SIZE + n_mask:, :] = jnp.zeros((LANES - n_mask, n_lanes), jnp.bfloat16)
    for j in range(n_kv):
        wait_all(loads[j])
        for odd in range(2):
            kaug[j, odd, :HEAD_SIZE, :] = table[j, odd * BLK:odd * BLK + n_lanes, :HEAD_SIZE].T
            kaug[j, odd, HEAD_SIZE:HEAD_SIZE + n_mask, :] = spread_mask(
                mask[j], lambda key: key // BLK + odd, n_lanes
            )
        vaug[j, :, :HEAD_SIZE] = table[j, :, HEAD_SIZE:]

    u = lax.broadcasted_iota(jnp.int32, (rows, LANES), 1) - (LANES - BLK)
    t = lax.broadcasted_iota(jnp.int32, (rows, LANES), 0) % BLK

    def stores(turn):
        blocks = pl.ds(2 * turn, 2)
        return [
            pltpu.make_async_copy(acc_ref.at[blocks], acc_out.at[blocks], turn_sem.at[turn, 0]),
            pltpu.make_async_copy(lse_ref.at[blocks], lse_out.at[blocks], turn_sem.at[turn, 1]),
        ]

    def two_blocks(turn, carry):
        j, pair = turn // n_pairs, turn % n_pairs
        base = 2 * pair
        if n_src == 2:
            per = n_blk // 2
            base = jnp.where(pair < per, core, 1 - core) * n_blk + 2 * (pair % per)
        q_rows = q_ref.at[pl.ds(pl.multiple_of(2 * turn * BLK, 2 * BLK), 2 * BLK)]
        even = pl.ds(pl.multiple_of(base * BLK, LANES), span)

        def scores_of(n):
            q = with_selector(head_rows(q_rows, n, group), base + n, group)
            return jnp.dot(q, kaug[j, n, :, even], preferred_element_type=jnp.float32)

        def softmax_of(n, scores):
            parts = tiles(scores)
            parts[-1] = jnp.where(u > t, NEG, parts[-1])
            top = row_top(parts)
            return top, exponents(parts, top)

        def finish(n, top, weights):
            at = pl.ds(pl.multiple_of((base + n) * BLK, BLK), span)
            total = jnp.dot(weights, vaug[j, at, :], preferred_element_type=jnp.float32)
            acc_ref[2 * turn + n] = total[:, :HEAD_SIZE] / total[:, HEAD_SIZE:]
            lse_ref[2 * turn + n] = top + jnp.log(total[:, HEAD_SIZE:]) * LOG_SCALE

        in_pipeline(2, scores_of, softmax_of, finish)
        start_all(stores(turn))
        return carry

    lax.fori_loop(0, n_kv * n_pairs, two_blocks, 0)
    for turn in range(n_kv * n_pairs):
        wait_all(stores(turn))


def window_part(pos, pieces, places, bias, queries, q_recv, n_kv, n_src, n_blk, group, n_win):
    width = group * HEAD_SIZE
    rows = group * BLK
    n_rows = n_win * BLK
    n_turns = n_kv * n_src * n_blk // 2
    q_args = [queries] if n_src == 1 else [queries, q_recv]
    out_shape = jax.ShapeDtypeStruct((2 * n_turns, rows, LANES), jnp.float32)
    sizes = [piece.shape[0] for piece in pieces]
    keys = 2 * n_turns * rows * (SMAX + 1) * BLK
    return pl.pallas_call(
        functools.partial(window_kernel, sizes, places, n_kv, n_src, n_blk, group),
        in_specs=[pl.BlockSpec(memory_space=pltpu.SMEM)]
        + [ANY] * (len(pieces) + 1 + n_src),
        out_specs=[ANY, ANY],
        scratch_shapes=[
            pltpu.VMEM((n_kv, n_rows, 2 * HEAD_SIZE), jnp.bfloat16),
            pltpu.VMEM(bias.shape, jnp.bfloat16),
            pltpu.VMEM((n_kv, 2, 2 * LANES, n_rows - BLK), jnp.bfloat16),
            pltpu.VMEM((n_kv, n_rows, 2 * LANES), jnp.bfloat16),
            pltpu.VMEM((2 * n_turns * BLK, width), jnp.bfloat16),
            pltpu.VMEM(out_shape.shape, jnp.float32),
            pltpu.VMEM(out_shape.shape, jnp.float32),
            pltpu.SemaphoreType.DMA((n_kv * (len(pieces) + 1 + n_src),)),
            pltpu.SemaphoreType.DMA((n_turns, 2)),
        ],
        out_shape=[out_shape, out_shape],
        compiler_params=pltpu.CompilerParams(vmem_limit_bytes=VMEM_LIMIT),
        cost_estimate=pl.CostEstimate(
            flops=keys * 1024, bytes_accessed=16 * 1024 * 1024, transcendentals=keys
        ),
    )(pos, *pieces, bias, *q_args)


def vertical_kernel(sources, kvs, n_kv, n_vert, group, n_blk, n_src, n_dst, other, pos_ref, *refs):
    n_pieces = max(source[0] for source in sources) + 1
    n_mine = len(kvs)
    pieces, refs = refs[:n_pieces], refs[n_pieces:]
    bias_ref, refs = refs[0], refs[1:]
    q_in, refs = refs[:n_src], refs[n_src:]
    acc_in, lse_in, refs = refs[0], refs[1], refs[2:]
    outs_ref, refs = refs[:n_mine * n_src], refs[n_mine * n_src:]
    table, mask, kaug, vaug, q_ref, acc_ref, lse_ref, out_ref, sem, turn_sem = refs
    core, tp_pos = pos_ref[0], pos_ref[1]
    per_dst = n_blk // n_dst
    n_keys = vaug.shape[1]
    n_mask = bias_ref.shape[1]
    group_rows = n_vert * PIECE
    used = (N_PIECES // 2) * group_rows
    width = group * HEAD_SIZE
    base = 0
    if n_dst > 1:
        base = (1 - tp_pos if other else tp_pos) * per_dst
    count = iter(range(sem.shape[0]))

    loads = []
    for m, j in enumerate(kvs):
        for index, (piece, part) in enumerate(sources):
            slot = pos_ref[2 + index]
            rows = pl.ds(pl.multiple_of((slot // 2) * group_rows, PIECE), group_rows)
            loads.append(
                pltpu.make_async_copy(
                    pieces[piece].at[part, j], table.at[m, slot % 2, rows], sem.at[next(count)]
                )
            )
        loads.append(pltpu.make_async_copy(bias_ref.at[j], mask.at[m], sem.at[next(count)]))
    q_rows = pl.ds(pl.multiple_of(base * BLK, BLK), per_dst * BLK)

    def turn_loads(m, source, turn):
        j = kvs[m]
        first = pl.multiple_of((core * n_kv + j) * width, width)
        q_lanes = [pl.ds(first, width), pl.ds(j * width, width)]
        blocks = pl.ds((j * n_src + source) * n_blk + base, per_dst)
        return [
            pltpu.make_async_copy(
                q_in[source].at[q_rows, q_lanes[source]], q_ref.at[turn], turn_sem.at[turn, 0]
            ),
            pltpu.make_async_copy(
                acc_in.at[blocks], acc_ref.at[turn], turn_sem.at[turn, 1]
            ),
            pltpu.make_async_copy(
                lse_in.at[blocks], lse_ref.at[turn], turn_sem.at[turn, 2]
            ),
        ]

    start_all(loads)
    for m in range(n_mine):
        for source in range(n_src):
            start_all(turn_loads(m, source, m * n_src + source))
    for m in range(n_mine):
        if used < n_keys:
            empty = jnp.zeros((n_keys - used, LANES), jnp.bfloat16)
            table[m, 0, used:] = empty
            table[m, 1, used:] = empty
        vaug[m, :, HEAD_SIZE:] = jnp.ones((n_keys, LANES), jnp.bfloat16)
        kaug[m, HEAD_SIZE + n_mask:, :] = jnp.zeros((LANES - n_mask, n_keys), jnp.bfloat16)
    wait_all(loads)
    for m in range(n_mine):
        kaug[m, :HEAD_SIZE, :] = table[m, 0].T
        kaug[m, HEAD_SIZE:HEAD_SIZE + n_mask, :] = spread_mask(
            mask[m], lambda key: key % group_rows // PIECE, n_keys
        )
        if used < n_keys:
            kaug[m, HEAD_SIZE:HEAD_SIZE + n_mask, used:] = jnp.full((n_mask, n_keys - used), NEG, jnp.bfloat16)
        vaug[m, :, :HEAD_SIZE] = table[m, 1]

    def one_turn(turn, carry):
        j = turn // n_src
        first_block = base
        if n_src == 2:
            first_block = base + jnp.where(turn % 2 == 0, core, 1 - core) * n_blk
        wait_all(turn_loads(0, 0, turn))

        def scores_of(n):
            q = with_selector(head_rows(q_ref.at[turn], n, group), first_block + n, group)
            return jnp.dot(q, kaug[j], preferred_element_type=jnp.float32)

        def softmax_of(n, scores):
            old = lse_ref[turn, n]
            parts = tiles(scores)
            top = jnp.maximum(old, row_top(parts))
            return jnp.exp2((old - top) * SCALE), exponents(parts, top)

        def finish(n, shrink, weights):
            total = jnp.dot(weights, vaug[j], preferred_element_type=jnp.float32)
            weighted = total[:, :HEAD_SIZE] + acc_ref[turn, n] * shrink
            out = (weighted / (total[:, HEAD_SIZE:] + shrink)).astype(jnp.bfloat16)
            for h in range(group):
                lanes = slice(h * HEAD_SIZE, (h + 1) * HEAD_SIZE)
                out_ref[turn, n * BLK:(n + 1) * BLK, lanes] = out[h * BLK:(h + 1) * BLK]

        in_pipeline(per_dst, scores_of, softmax_of, finish)
        return carry

    lax.fori_loop(0, n_mine * n_src, one_turn, 0)
    stores = [
        pltpu.make_async_copy(out_ref.at[turn], outs_ref[turn], turn_sem.at[turn, 3])
        for turn in range(n_mine * n_src)
    ]
    start_all(stores)
    wait_all(stores)


def vertical_part(
    pos, pieces, sources, kvs, bias, queries, q_recv, state, n_kv, n_src, n_dst, other, n_blk, group, n_vert
):
    n_mine = len(kvs)
    n_turns = n_mine * n_src
    width = group * HEAD_SIZE
    rows = group * BLK
    per_dst = n_blk // n_dst
    n_keys = round_up(n_vert * BLK, LANES)
    q_args = [queries] if n_src == 1 else [queries, q_recv]
    out_shape = jax.ShapeDtypeStruct((per_dst * BLK, width), jnp.bfloat16)
    keys = n_turns * per_dst * rows * n_keys
    args = [*pieces, bias, *q_args, *state]
    return pl.pallas_call(
        functools.partial(
            vertical_kernel, sources, kvs, n_kv, n_vert, group, n_blk, n_src, n_dst, other
        ),
        in_specs=[pl.BlockSpec(memory_space=pltpu.SMEM)] + [ANY] * len(args),
        out_specs=[ANY] * n_turns,
        scratch_shapes=[
            pltpu.VMEM((n_mine, 2, n_keys, LANES), jnp.bfloat16),
            pltpu.VMEM((n_mine,) + bias.shape[1:], jnp.bfloat16),
            pltpu.VMEM((n_mine, 2 * LANES, n_keys), jnp.bfloat16),
            pltpu.VMEM((n_mine, n_keys, 2 * LANES), jnp.bfloat16),
            pltpu.VMEM((n_turns, per_dst * BLK, width), jnp.bfloat16),
            pltpu.VMEM((n_turns, per_dst, rows, LANES), jnp.float32),
            pltpu.VMEM((n_turns, per_dst, rows, LANES), jnp.float32),
            pltpu.VMEM((n_turns, per_dst * BLK, width), jnp.bfloat16),
            pltpu.SemaphoreType.DMA((n_mine * (N_PIECES + 1),)),
            pltpu.SemaphoreType.DMA((n_turns, 4)),
        ],
        out_shape=[out_shape] * n_turns,
        compiler_params=pltpu.CompilerParams(vmem_limit_bytes=(16 + round_up(8 * n_keys // 768, 8)) * 1024 * 1024),
        cost_estimate=pl.CostEstimate(
            flops=keys * 1024, bytes_accessed=8 * 1024 * 1024, transcendentals=keys
        ),
    )(pos, *args)


def split_kernel(n_kv, kv_ref, out_ref):
    for side in range(2):
        for j in range(n_kv):
            for part in range(2):
                lanes = ((side * n_kv + j) * 2 + part) * LANES
                for block in range(kv_ref.shape[0] // BLK):
                    for rg in range(BLK // PIECE):
                        at = block * BLK + rg * PIECE
                        out_ref[(rg * 2 + part) * 2 + side, block * n_kv + j] = kv_ref[
                            at:at + PIECE, lanes:lanes + LANES
                        ]


def split_rows(kv_rows, n_kv):
    n_blk = kv_rows.shape[0] // BLK
    return pl.pallas_call(
        functools.partial(split_kernel, n_kv),
        in_specs=[pl.BlockSpec(memory_space=pltpu.VMEM)],
        out_specs=pl.BlockSpec(memory_space=pltpu.VMEM),
        out_shape=jax.ShapeDtypeStruct((2 * N_PIECES, n_blk * n_kv, PIECE, LANES), kv_rows.dtype),
        compiler_params=pltpu.CompilerParams(vmem_limit_bytes=ALL_VMEM),
    )(kv_rows)


def select_kernel(n_kv, n_vert, index_ref, table, out):
    for j in range(n_kv):
        for unit in range(n_vert):
            rows = slice(unit * PIECE, (unit + 1) * PIECE)
            out[j, rows, :] = table[index_ref[j * n_vert + unit]]


def select_units(index, table, n_kv, n_vert):
    return pl.pallas_call(
        functools.partial(select_kernel, n_kv, n_vert),
        in_specs=[
            pl.BlockSpec(memory_space=pltpu.SMEM),
            pl.BlockSpec(memory_space=pltpu.VMEM),
        ],
        out_specs=pl.BlockSpec(memory_space=pltpu.VMEM),
        out_shape=jax.ShapeDtypeStruct((n_kv, n_vert * PIECE, LANES), jnp.bfloat16),
        compiler_params=pltpu.CompilerParams(vmem_limit_bytes=8 * 1024 * 1024),
    )(index, table)


def assemble_kernel(widths, column_ref, *refs):
    n = len(widths)
    pieces, out, buffers, sem = refs[:n], refs[n], refs[n + 1:-1], refs[-1]
    loads = [pltpu.make_async_copy(pieces[i], buffers[i], sem.at[0, i]) for i in range(n)]
    start_all(loads)
    stores = []
    for i in range(n):
        loads[i].wait()
        start = pl.multiple_of(column_ref[i], LANES)
        stores.append(
            pltpu.make_async_copy(buffers[i], out.at[:, pl.ds(start, widths[i])], sem.at[1, i])
        )
        stores[-1].start()
    wait_all(stores)


def assemble(columns, pieces):
    rows = pieces[0].shape[0]
    widths = [piece.shape[1] for piece in pieces]
    return pl.pallas_call(
        functools.partial(assemble_kernel, widths),
        in_specs=[pl.BlockSpec(memory_space=pltpu.SMEM)] + [ANY] * len(pieces),
        out_specs=ANY,
        out_shape=jax.ShapeDtypeStruct((rows, sum(widths)), pieces[0].dtype),
        scratch_shapes=[pltpu.VMEM(piece.shape, piece.dtype) for piece in pieces]
        + [pltpu.SemaphoreType.DMA((2, len(pieces)))],
        compiler_params=pltpu.CompilerParams(vmem_limit_bytes=ALL_VMEM),
    )(columns, *pieces)


def mask_tables(vert, slash, first, n_query, n_win, n_vert, n_blocks):
    n_kv, group = vert.shape[:2]
    blocks = jnp.arange(n_blocks, dtype=jnp.int32)
    present = jnp.any(vert.reshape(n_kv, -1)[:, :, None] == blocks, axis=1)
    before = blocks[None, :] < blocks[:, None]
    rank = jnp.sum((present[:, None, :] & before[None]).astype(jnp.int32), axis=2)
    unit = jnp.arange(n_vert, dtype=jnp.int32)
    chosen = present[:, None, :] & (rank[:, None, :] == unit[None, :, None])
    units = jnp.sum(jnp.where(chosen, blocks, 0), axis=2)

    def as_rows(live):
        bias = jnp.where(live, 0.0, NEG).astype(jnp.bfloat16)
        bias = bias.reshape(n_kv, n_query * group, live.shape[-1])
        return jnp.pad(bias, ((0, 0), (0, 0), (0, LANES - live.shape[-1])))

    query = first + jnp.arange(n_query, dtype=jnp.int32)
    window = first - SMAX + jnp.arange(n_win, dtype=jnp.int32)
    offset = query[:, None] - window[None, :]
    by_slash = jnp.any(offset[None, :, None, :, None] == slash[:, None, :, None, :], axis=4)
    by_vert = jnp.any(window[None, None, :, None] == vert[:, :, None, :], axis=3)
    near = (offset >= 0) & (offset <= SMAX) & (window >= 0)[None, :]
    live_w = near[None, :, None, :] & (by_slash | by_vert[:, None, :, :])
    listed = jnp.any(units[:, None, :, None] == vert[:, :, None, :], axis=3)
    far = query[None, :, None] - units[:, None, :] > SMAX
    live_v = far[:, :, None, :] & listed[:, None, :, :]
    return units, as_rows(live_w), as_rows(live_v)


def paired(queries, kv_rows, vertical, slash):
    n_seq = lax.axis_size("seq")
    n_chip = n_seq // 2
    n_far = n_chip // 2
    tok = queries.shape[0]
    n_blk = tok // BLK
    seq_pos, tp_pos = lax.axis_index("seq"), lax.axis_index("tp")
    core, chip = seq_pos % 2, seq_pos // 2
    near, far = chip % 2, chip // 2
    heads_loc = vertical.shape[0] // 2
    kv_loc = kv_rows.shape[1] // (2 * HEAD_SIZE)
    group = heads_loc // kv_loc
    n_kv = kv_loc // 2
    heads = n_kv * group
    n_blocks = n_seq * n_blk
    n_vert = vertical.shape[1] * 3 // 2 - 1
    n_query = 2 * n_blk
    n_win = n_query + SMAX
    kv_width = n_kv * 2 * HEAD_SIZE
    q_width = heads * HEAD_SIZE

    def by_chip(array, target):
        pairs = []
        for source in range(n_seq):
            to = target(source // 2)
            if to is not None:
                pairs.append((source, 2 * to + source % 2))
        return lax.ppermute(array, "seq", pairs)

    to_pair = jnp.concatenate(
        [
            lax.dynamic_slice_in_dim(queries, (1 - core) * q_width, q_width, 1),
            lax.dynamic_slice_in_dim(kv_rows, (1 - core) * kv_width, kv_width, 1),
        ],
        axis=1,
    )
    from_pair = lax.ppermute(to_pair, "seq", [(i, i ^ 1) for i in range(n_seq)])

    rows, _ = lax.optimization_barrier((kv_rows, to_pair))
    held = lax.all_to_all(split_rows(rows, n_kv), "seq", split_axis=0, concat_axis=0, tiled=True)
    held = held.reshape(n_blocks * n_kv, PIECE, LANES)

    mine = lax.dynamic_slice_in_dim(kv_rows, core * kv_width, kv_width, 1)
    theirs = from_pair[:, q_width:]
    here = jnp.where(
        core == 0,
        jnp.concatenate([mine, theirs], axis=0),
        jnp.concatenate([theirs, mine], axis=0),
    )
    extra = SMAX - n_query
    tail = jnp.where(core == 0, theirs[-extra * BLK:], mine[-extra * BLK:])
    before = by_chip(here, lambda c: c + 1 if c + 1 < n_chip else None)
    back = by_chip(tail, lambda c: c + 2 if c + 2 < n_chip else None)

    vertical, slash, here, tail = lax.optimization_barrier((vertical, slash, here, tail))
    first_head = tp_pos * heads_loc + core * heads
    my_vert = lax.dynamic_slice_in_dim(vertical, first_head, heads, 0).reshape(n_kv, group, -1)
    my_slash = lax.dynamic_slice_in_dim(slash, first_head, heads, 0).reshape(n_kv, group, -1)
    units, bias_w, bias_v = mask_tables(
        my_vert, my_slash, chip * n_query, n_query, n_win, n_vert, n_blocks
    )

    index = (units * n_kv + jnp.arange(n_kv, dtype=jnp.int32)[:, None]).reshape(-1)
    picked = select_units(index, held, n_kv, n_vert)
    beside = by_chip(picked, lambda c: c ^ 1)
    both = jnp.where(near == 0, jnp.stack([picked, beside]), jnp.stack([beside, picked]))
    pieces, sources, slots = [both], [(0, 0), (0, 1)], [2 * far, 2 * far + 1]
    for step in range(1, n_far):
        pieces.append(by_chip(both, lambda c: (c + 2 * step) % n_chip))
        sources += [(step, 0), (step, 1)]
        owner = (far - step) % n_far
        slots += [2 * owner, 2 * owner + 1]

    pos = jnp.stack([core, tp_pos] + slots).astype(jnp.int32)
    state = window_part(
        pos, [here, before, back], [SMAX, extra, 0], bias_w, queries, from_pair,
        n_kv, 2, n_blk, group, n_win,
    )

    def swap(array, other_core, other_tp):
        pairs = []
        for source in range(n_seq):
            for t in range(2):
                pairs.append((source * 2 + t, (source ^ other_core) * 2 + (t ^ other_tp)))
        return lax.ppermute(array, ("seq", "tp"), pairs)

    results = []
    for other_tp, kvs in [(1, (j,)) for j in range(n_kv)] + [(0, tuple(range(n_kv)))]:
        outs = vertical_part(
            pos, pieces, sources, kvs, bias_v, queries, from_pair, state,
            n_kv, 2, 2, other_tp, n_blk, group, n_vert,
        )
        outs, state = lax.optimization_barrier((outs, state))
        from_tp = 1 - tp_pos if other_tp else tp_pos
        for other_core in (0, 1):
            from_core = 1 - core if other_core else core
            for m, j in enumerate(kvs):
                piece = outs[m * 2 + other_core]
                if other_core or other_tp:
                    piece = swap(piece, other_core, other_tp)
                column = ((from_tp * 2 + from_core) * n_kv + j) * group * HEAD_SIZE
                results.append((piece, column))
    columns = jnp.stack([column for _, column in results]).astype(jnp.int32)
    return assemble(columns, [piece for piece, _ in results])


def gathered(queries, kv_rows, vertical, slash):
    n_seq, n_tp = lax.axis_size("seq"), lax.axis_size("tp")
    tok = queries.shape[0]
    n_blk = tok // BLK
    seq_pos, tp_pos = lax.axis_index("seq"), lax.axis_index("tp")
    heads = vertical.shape[0] // n_tp
    n_kv = kv_rows.shape[1] // (2 * HEAD_SIZE)
    group = heads // n_kv
    n_blocks = n_seq * n_blk
    n_vert = vertical.shape[1] * 3 // 2 - 1
    n_win = n_blk + SMAX
    first = seq_pos * n_blk
    my_vert = lax.dynamic_slice_in_dim(vertical, tp_pos * heads, heads, 0)
    my_slash = lax.dynamic_slice_in_dim(slash, tp_pos * heads, heads, 0)
    units, bias_w, bias_v = mask_tables(
        my_vert.reshape(n_kv, group, -1), my_slash.reshape(n_kv, group, -1),
        first, n_blk, n_win, n_vert, n_blocks,
    )
    full = lax.all_gather(kv_rows, "seq", axis=0, tiled=True)
    padded = jnp.pad(full, ((SMAX * BLK, 0), (0, 0)))
    window = lax.dynamic_slice_in_dim(padded, first * BLK, n_win * BLK, 0)
    pos = jnp.stack([jnp.int32(0), tp_pos] + [jnp.int32(i) for i in range(N_PIECES)])
    state = window_part(
        pos, [window], [0], bias_w, queries, None, n_kv, 1, n_blk, group, n_win
    )
    blocks = full.reshape(n_blocks, BLK // PIECE, PIECE, n_kv, 2, LANES)
    listed = jnp.stack([blocks[units[j], :, :, j] for j in range(n_kv)])
    listed = jnp.transpose(listed, (2, 4, 0, 1, 3, 5))
    listed = listed.reshape(N_PIECES, n_kv, n_vert * PIECE, LANES)
    outs = vertical_part(
        pos, [listed], [(0, i) for i in range(N_PIECES)], tuple(range(n_kv)), bias_v, queries, None,
        state, n_kv, 1, 1, 0, n_blk, group, n_vert,
    )
    attended = jnp.concatenate(outs, axis=1)
    return lax.all_to_all(attended, "tp", split_axis=0, concat_axis=1, tiled=True)


def per_device(queries, kv_rows, vertical, slash):
    n_seq, n_tp = lax.axis_size("seq"), lax.axis_size("tp")
    kv_loc = kv_rows.shape[1] // (2 * HEAD_SIZE)
    n_blk = queries.shape[0] // BLK
    if n_seq == 2 * N_PIECES and n_tp == 2 and kv_loc % 2 == 0 and n_blk == 4:
        return paired(queries, kv_rows, vertical, slash)
    return gathered(queries, kv_rows, vertical, slash)


def solution(mesh):
    return jax.shard_map(
        per_device,
        mesh=mesh,
        in_specs=(P("seq", "tp"), P("seq", "tp"), P(), P()),
        out_specs=P(("seq", "tp"), None),
        check_vma=False,
    )
```

time: 102 us -> 93.3 us (0.915)
  Pallas kernels: 48.1 us -> 37.3 us
  starting transfers between devices: 26.7 us -> 30.7 us
  local copies, waits for them, and re-layouts: 9.74 us -> 7.02 us
  waiting for transfers between devices: 9.2 us -> 10.3 us
    pallas_call x4 -> x6, Pallas kernels: 47 us -> 36.2 us  [the longest x3 18.4 us: vertical_part(): pl.pallas_call(functools.partial(vertical_kernel, sources, kvs, n_kv, n_v...]
    ppermute x6, waiting for transfers between devices: 0.02 us -> 4.76 us  [by_chip(): return lax.ppermute(array, 'seq', pairs)]
    ppermute x3 -> x6, waiting for transfers between devices: 5.95 us -> 3.72 us  [swap(): return lax.ppermute(array, ('seq', 'tp'), pairs)]
    ppermute x3 -> x6, starting transfers between devices: 3.03 us -> 5.1 us  [swap(): return lax.ppermute(array, ('seq', 'tp'), pairs)]
    ppermute x6, starting transfers between devices: 16.1 us -> 18.1 us  [by_chip(): return lax.ppermute(array, 'seq', pairs)]
    unnamed x14 -> x18, local copies, waits for them, and re-layouts: 1.63 us -> 3.58 us
    slice x1 -> x0, local copies, waits for them, and re-layouts: 1.61 us -> none  [paired(): here[-extra * BLK:]]
    reshape x1 -> x0, local copies, waits for them, and re-layouts: 1.55 us -> none  [paired(): split = kv_rows.reshape(n_blk, BLK // PIECE, PIECE, 2, n_kv, 2, LANES)]
  transfers between devices with their start and end apart: 11 -> 14, of which waited for: 3 -> 3; matrix products, arithmetic and copies ran while one was open for 12% -> 8% of each run, Pallas kernels for 29% -> 32%
where the time goes in v2:
time: 93.3 us; the launch traced here: 92.8 us
  Pallas kernels  37.3 us (40%)
  starting transfers between devices  30.7 us (33%)
  waiting for transfers between devices  10.3 us (11%)
  other arithmetic  7.19 us (8%)
  local copies, waits for them, and re-layouts  7.02 us (8%)
    pallas_call x3, Pallas kernels, vertical_part(): pl.pallas_call(functools.partial(vertical_kernel, sources, kvs, n_kv, n_v...  18.4 us
    ppermute x6, starting transfers between devices, by_chip(): return lax.ppermute(array, 'seq', pairs)  18.1 us
    pallas_call x1, Pallas kernels, window_part(): pl.pallas_call(functools.partial(window_kernel, sizes, places, n_kv, n_sr...  12.8 us
    all_to_all x1, starting transfers between devices, paired(): lax.all_to_all(split_rows(rows, n_kv), 'seq', split_axis=0, concat_axis=0...  7.41 us
    ppermute x6, starting transfers between devices, swap(): return lax.ppermute(array, ('seq', 'tp'), pairs)  5.1 us
    ppermute x6, waiting for transfers between devices, by_chip(): return lax.ppermute(array, 'seq', pairs)  4.76 us
    ppermute x6, waiting for transfers between devices, swap(): return lax.ppermute(array, ('seq', 'tp'), pairs)  3.72 us
    unnamed x18, local copies, waits for them, and re-layouts  3.58 us
  transfers between devices with their start and end apart: 14, of which 3 were waited for; matrix products, arithmetic and copies ran while one was open for 8% of the time, Pallas kernels for 32%

profile of v2, /device:TPU:1, one launch (start us, length us, event | category | flops | bytes accessed | tf_op | source)
XLA Modules:
  0.0 92.8 jit_solution(18338217007657216911)
XLA Ops:
  0.0 1.4 %constant_dynamic-slice_fusion.3 = bf16[256,2048]{1,0:T(8,128)(2,1)S(1)} fusion(bf16[256,4096]{1,0:T(8,128)(2,1)} %refs_5_.5, s32[]{:T(128)S(6)} %select_n.92), kind=kLoop, calls=%fused_computation.25 | loop fusion | bytes 2097156 | tf_op jit(solution)/shard_map/dynamic_slice | solution.py:494
  1.4 0.8 constant_dynamic-slice_fusion.4
  2.2 1.1 %pad_maximum_fusion = bf16[256,2560]{1,0:T(8,128)(2,1)} fusion(bf16[256,512]{1,0:T(8,128)(2,1)S(1)} %get-tuple-element.58, bf16[256,2048]{1,0:T(8,128)(2,1)S(1)} %constant_dynamic-slice_fusion.3), kind=kLoop, calls=%fused_computation | loop fusion | flops 2621440 | bytes 2621440 | tf_op jit(solution)/shard_map/concatenate | solution.py:492
  3.4 1.9 %shard_map.46 = bf16[16,8,16,128]{3,2,1,0:T(8,128)(2,1)} custom-call(bf16[256,1024]{1,0:T(8,128)(2,1)} %kv_ref), custom_call_target="tpu_custom_call" | custom-call | tf_op jit(solution)/shard_map/pallas_call | solution.py:376
  5.3 7.4 %all-to-all-start = ((bf16[16,8,16,128]{3,2,1,0:T(8,128)(2,1)}), bf16[16,8,16,128]{3,2,1,0:T(8,128)(2,1)}, u32[]{:S(2)}, u32[]{:S(2)}) async-start(bf16[16,8,16,128]{3,2,1,0:T(8,128)(2,1)} %shard_map.46), calls=%async_computation | async-start | bytes 1048576 | tf_op jit(solution)/shard_map/all_to_all | solution.py:502
  12.8 0.1 stack.93.pos_ref
  13.0 0.1 and_and_fusion
  13.2 2.1 %maximum_select_fusion.refs_0_ = bf16[512,512]{1,0:T(8,128)(2,1)} fusion(bf16[256,512]{1,0:T(8,128)(2,1)S(1)} %slice.13, bf16[256,512]{1,0:T(8,128)(2,1)} %get-tuple-element.57, pred[]{:T(512)S(6)} %eq.85), kind=kLoop, calls=%fused_computation.1 | loop fusion | flops 2359296 | bytes 1048577 | tf_op jit(solution)/shard_map/jit(_where)/select_n | solution.py:507
  15.3 4.1 %collective-permute-start.5 = (bf16[512,512]{1,0:T(8,128)(2,1)}, bf16[512,512]{1,0:T(8,128)(2,1)}, u32[]{:S(2)}, u32[]{:S(2)}) collective-permute-start(bf16[512,512]{1,0:T(8,128)(2,1)} %maximum_select_fusion.refs_0_), channel_id=1, source_target_pairs={{0,4},{2,6},{4,8},{6,10},{8,12},{10,14},{12,16},{14,18},{16,20},{1... | collective-permute-start | bytes 1572872 | tf_op jit(solution)/shard_map/ppermute | solution.py:490
  19.4 1.7 %dynamic-slice_select_fusion = bf16[192,512]{1,0:T(8,128)(2,1)} fusion(bf16[256,1024]{1,0:T(8,128)(2,1)} %kv_ref, s32[]{:T(128)S(6)} %add.154, s32[]{:T(128)S(6)} %select_n.91, bf16[256,2560]{1,0:T(8,128)(2,1)S(1)} %collective-permute-done.refs_5_.refs_6_, pred[]{:T(512)S(6)} %eq.85), kind=kLoop, calls=%fused_computation.3 | loop fusion | flops 98304 | bytes 589833 | tf_op jit(solution)/shard_map/jit(_where)/select_n | solution.py:513
  21.1 3.0 %collective-permute-start.6 = (bf16[192,512]{1,0:T(8,128)(2,1)}, bf16[192,512]{1,0:T(8,128)(2,1)}, u32[]{:S(2)}, u32[]{:S(2)}) collective-permute-start(bf16[192,512]{1,0:T(8,128)(2,1)} %dynamic-slice_select_fusion), channel_id=1, source_target_pairs={{0,8},{2,10},{4,12},{6,14},{8,16},{10,18},{12,20},{14,22},{16,24},... | collective-permute-start | bytes 589832 | tf_op jit(solution)/shard_map/ppermute | solution.py:490
  24.1 0.1 copy.13
  24.2 0.1 eq.86
  24.3 0.1 fusion
  24.4 0.1 convert_reduce_fusion
  24.5 0.3 fusion.2
  24.8 0.1 copy.15
  24.9 0.1 copy.14
  25.0 0.1 add.149.index_ref
  25.0 1.8 %all-to-all-done = bf16[16,8,16,128]{3,2,1,0:T(8,128)(2,1)} async-done(((bf16[16,8,16,128]{3,2,1,0:T(8,128)(2,1)}), bf16[16,8,16,128]{3,2,1,0:T(8,128)(2,1)}, u32[]{:S(2)}, u32[]{:S(2)}) %all-to-all-start) | async-done | bytes 524320 | tf_op jit(solution)/shard_map/all_to_all | solution.py:502
  26.9 1.1 %shard_map.47 = bf16[2,176,128]{2,1,0:T(8,128)(2,1)S(1)} custom-call(s32[22]{0:T(128)S(1)} %add.149.index_ref, bf16[128,16,128]{2,1,0:T(8,128)(2,1)} %bitcast.18.table), custom_call_target="tpu_custom_call" | custom-call | tf_op jit(solution)/shard_map/pallas_call | solution.py:393
  28.0 0.9 %collective-permute-start.1 = (bf16[2,176,128]{2,1,0:T(8,128)(2,1)S(1)}, bf16[2,176,128]{2,1,0:T(8,128)(2,1)}, u32[]{:S(2)}, u32[]{:S(2)}) collective-permute-start(bf16[2,176,128]{2,1,0:T(8,128)(2,1)S(1)} %shard_map.47), channel_id=1, source_target_pairs={{0,4},{2,6},{4,0},{6,2},{8,12},{10,14},{12,8},{14,10},{16,20},{18,... | collective-permute-start | bytes 270344 | tf_op jit(solution)/shard_map/ppermute | solution.py:490
  28.9 0.1 compare_reduce_fusion.1
  29.0 0.1 compare_reduce_fusion.2
  29.2 0.2 compare_reduce_fusion
  29.6 4.7 %collective-permute-done.1 = bf16[2,176,128]{2,1,0:T(8,128)(2,1)} collective-permute-done((bf16[2,176,128]{2,1,0:T(8,128)(2,1)S(1)}, bf16[2,176,128]{2,1,0:T(8,128)(2,1)}, u32[]{:S(2)}, u32[]{:S(2)}) %collective-permute-start.1) | collective-permute-done | bytes 90144 | tf_op jit(solution)/shard_map/ppermute | solution.py:490
  34.4 1.0 %maximum_select_fusion.1.refs_0_ = bf16[2,2,176,128]{3,2,1,0:T(8,128)(2,1)S(1)} fusion(bf16[1,2,176,128]{3,2,1,0:T(8,128)(2,1)} %bitcast.20, bf16[1,2,176,128]{3,2,1,0:T(8,128)(2,1)S(1)} %bitcast.31, pred[]{:T(512)S(6)} %eq.84), kind=kLoop, calls=%fused_computation.4 | loop fusion | flops 270336 | bytes 360449 | tf_op jit(solution)/shard_map/jit(_where)/select_n | solution.py:528
  35.4 4.9 %collective-permute-start.2 = (bf16[2,2,176,128]{3,2,1,0:T(8,128)(2,1)S(1)}, bf16[2,2,176,128]{3,2,1,0:T(8,128)(2,1)S(1)}, u32[]{:S(2)}, u32[]{:S(2)}) collective-permute-start(bf16[2,2,176,128]{3,2,1,0:T(8,128)(2,1)S(1)} %maximum_select_fusion.1.refs_0_), channel_id=1, source_target_pairs={{0,8},{2,10},{4,12},{6,14},{8,16},{10,18},{12,20},{14,22},{16,24},... | collective-permute-start | bytes 540680 | tf_op jit(solution)/shard_map/ppermute | solution.py:490
  40.2 3.0 %collective-permute-start.3 = (bf16[2,2,176,128]{3,2,1,0:T(8,128)(2,1)S(1)}, bf16[2,2,176,128]{3,2,1,0:T(8,128)(2,1)S(1)}, u32[]{:S(2)}, u32[]{:S(2)}) collective-permute-start(bf16[2,2,176,128]{3,2,1,0:T(8,128)(2,1)S(1)} %maximum_select_fusion.1.refs_0_), channel_id=1, source_target_pairs={{0,16},{2,18},{4,20},{6,22},{8,24},{10,26},{12,28},{14,30},{16,0},... | collective-permute-start | bytes 540680 | tf_op jit(solution)/shard_map/ppermute | solution.py:490
  43.2 2.3 %collective-permute-start.4 = (bf16[2,2,176,128]{3,2,1,0:T(8,128)(2,1)S(1)}, bf16[2,2,176,128]{3,2,1,0:T(8,128)(2,1)S(1)}, u32[]{:S(2)}, u32[]{:S(2)}) collective-permute-start(bf16[2,2,176,128]{3,2,1,0:T(8,128)(2,1)S(1)} %maximum_select_fusion.1.refs_0_), channel_id=1, source_target_pairs={{0,24},{2,26},{4,28},{6,30},{8,0},{10,2},{12,4},{14,6},{16,8},{18,... | collective-permute-start | bytes 540680 | tf_op jit(solution)/shard_map/ppermute | solution.py:490
  45.5 12.8 %shard_map.48 = (f32[16,512,128]{2,1,0:T(8,128)S(1)}, f32[16,512,128]{2,1,0:T(8,128)S(1)}) custom-call(s32[10]{0:T(128)S(1)} %stack.93.pos_ref, bf16[512,512]{1,0:T(8,128)(2,1)} %maximum_select_fusion.refs_0_, bf16[512,512]{1,0:T(8,128)(2,1)} %collective-permute-done.5.refs_1_, bf16[192,512]{1,0:T(8,128)(2,1)} %collective-permute-done.6.refs_2_, ...), custom_call_target="tpu_custom_call" | custom-call | flops 6442450944 | bytes 16777216 | tf_op jit(solution)/shard_map/pallas_call | solution.py:189
  58.3 4.9 %shard_map.49 = (bf16[128,1024]{1,0:T(8,128)(2,1)S(1)}, bf16[128,1024]{1,0:T(8,128)(2,1)}) custom-call(s32[10]{0:T(128)S(1)} %stack.93.pos_ref, bf16[2,2,176,128]{3,2,1,0:T(8,128)(2,1)S(1)} %maximum_select_fusion.1.refs_0_, bf16[2,2,176,128]{3,2,1,0:T(8,128)(2,1)S(1)} %collective-permute-done.2.refs_1_, ...), custom_call_target="tpu_custom_call" | custom-call | flops 1610612736 | bytes 8388608 | tf_op jit(solution)/shard_map/pallas_call | solution.py:335
  63.2 1.2 %collective-permute-start.7 = (bf16[128,1024]{1,0:T(8,128)(2,1)S(1)}, bf16[128,1024]{1,0:T(8,128)(2,1)S(1)}, u32[]{:S(2)}, u32[]{:S(2)}) collective-permute-start(bf16[128,1024]{1,0:T(8,128)(2,1)S(1)} %get-tuple-element.39), channel_id=1, source_target_pairs={{0,1},{1,0},{2,3},{3,2},{4,5},{5,4},{6,7},{7,6},{8,9},{9,8},{10,11... | collective-permute-start | bytes 786440 | tf_op jit(solution)/shard_map/ppermute | solution.py:547
  64.5 1.8 %collective-permute-start.8 = (bf16[128,1024]{1,0:T(8,128)(2,1)}, bf16[128,1024]{1,0:T(8,128)(2,1)}, u32[]{:S(2)}, u32[]{:S(2)}) collective-permute-start(bf16[128,1024]{1,0:T(8,128)(2,1)} %get-tuple-element.40), channel_id=1, source_target_pairs={{0,3},{1,2},{2,1},{3,0},{4,7},{5,6},{6,5},{7,4},{8,11},{9,10},{10,... | collective-permute-start | bytes 786440 | tf_op jit(solution)/shard_map/ppermute | solution.py:547
  66.3 5.0 %shard_map.50 = (bf16[128,1024]{1,0:T(8,128)(2,1)}, bf16[128,1024]{1,0:T(8,128)(2,1)}) custom-call(s32[10]{0:T(128)S(1)} %stack.93.pos_ref, bf16[2,2,176,128]{3,2,1,0:T(8,128)(2,1)S(1)} %maximum_select_fusion.1.refs_0_, bf16[2,2,176,128]{3,2,1,0:T(8,128)(2,1)S(1)} %collective-permute-done.2.refs_1_, ...), custom_call_target="tpu_custom_call" | custom-call | flops 1610612736 | bytes 8388608 | tf_op jit(solution)/shard_map/pallas_call | solution.py:335
  71.3 1.3 %collective-permute-start.9 = (bf16[128,1024]{1,0:T(8,128)(2,1)}, bf16[128,1024]{1,0:T(8,128)(2,1)}, u32[]{:S(2)}, u32[]{:S(2)}) collective-permute-start(bf16[128,1024]{1,0:T(8,128)(2,1)} %get-tuple-element.45), channel_id=1, source_target_pairs={{0,1},{1,0},{2,3},{3,2},{4,5},{5,4},{6,7},{7,6},{8,9},{9,8},{10,11... | collective-permute-start | bytes 786440 | tf_op jit(solution)/shard_map/ppermute | solution.py:547
  72.5 0.3 collective-permute-start.10
  72.8 8.5 %shard_map.51 = (bf16[128,1024]{1,0:T(8,128)(2,1)S(1)}, bf16[128,1024]{1,0:T(8,128)(2,1)}, bf16[128,1024]{1,0:T(8,128)(2,1)S(1)}, bf16[128,1024]{1,0:T(8,128)(2,1)}) custom-call(s32[10]{0:T(128)S(1)} %stack.93.pos_ref, bf16[2,2,176,128]{3,2,1,0:T(8,128)(2,1)S(1)} %maximum_select_fusion.1.refs_0_, ...), custom_call_target="tpu_custom_call" | custom-call | flops 3221225472 | bytes 8388608 | tf_op jit(solution)/shard_map/pallas_call | solution.py:335
  81.3 0.7 copy-done.1
  82.1 0.7 copy-done.2
  82.8 0.4 collective-permute-start.11
  83.1 0.7 copy-done.4
  83.8 0.1 collective-permute-start.12
  84.0 0.6 stack.82.column_ref
  84.6 3.7 %collective-permute-done.10.refs_3_ = bf16[128,1024]{1,0:T(8,128)(2,1)} collective-permute-done((bf16[128,1024]{1,0:T(8,128)(2,1)}, bf16[128,1024]{1,0:T(8,128)(2,1)}, u32[]{:S(2)}, u32[]{:S(2)}) %collective-permute-start.10) | collective-permute-done | bytes 262176 | tf_op jit(solution)/shard_map/ppermute | solution.py:547
  88.3 0.7 copy-done.5
  89.0 0.7 copy-done.6
  89.7 3.1 %shard_map.52 = bf16[128,8192]{1,0:T(8,128)(2,1)} custom-call(s32[8]{0:T(128)} %stack.82.column_ref, bf16[128,1024]{1,0:T(8,128)(2,1)} %copy-done.4, bf16[128,1024]{1,0:T(8,128)(2,1)} %collective-permute-done.8.refs_1_, bf16[128,1024]{1,0:T(8,128)(2,1)} %collective-permute-done.9.refs_2_, bf16[128,1024]{1,0:T(8,128)(2,1)} %collective-permute-done.10.refs_3_, ...), custom_call_target="tpu_custom_call" | custom-call | tf_op jit(solution)/shard_map/pallas_call | solution.py:424
  (40 shorter events, 0.5 us)
Async XLA Ops:
  0.0 1.4 %copy-start.3 = (bf16[256,1024]{1,0:T(8,128)(2,1)S(1)}, bf16[256,1024]{1,0:T(8,128)(2,1)}, u32[]{:S(2)}) copy-start(bf16[256,1024]{1,0:T(8,128)(2,1)} %kv_ref) | copy-start | bytes 1572868
  3.3 20.7 %copy-start.7 = (s32[64,8]{0,1:T(8,128)S(1)}, s32[64,8]{0,1:T(8,128)}, u32[]{:S(2)}) copy-start(s32[64,8]{0,1:T(8,128)} %param.7) | copy-start | bytes 6148
  3.3 20.7 %copy-start.8 = (s32[64,8]{0,1:T(8,128)S(1)}, s32[64,8]{0,1:T(8,128)}, u32[]{:S(2)}) copy-start(s32[64,8]{0,1:T(8,128)} %param.6) | copy-start | bytes 6148
  3.3 9.8 %collective-permute-start = (bf16[256,2560]{1,0:T(8,128)(2,1)}, bf16[256,2560]{1,0:T(8,128)(2,1)S(1)}, u32[]{:S(2)}, u32[]{:S(2)}) collective-permute-start(bf16[256,2560]{1,0:T(8,128)(2,1)} %pad_maximum_fusion), channel_id=1, source_target_pairs={{0,2},{2,0},{4,6},{6,4},{8,10},{10,8},{12,14},{14,12},{16,18},{18,... | collective-permute-start | bytes 3932168 | tf_op jit(solution)/shard_map/ppermute | solution.py:499
  5.3 21.6 %all-to-all-start = ((bf16[16,8,16,128]{3,2,1,0:T(8,128)(2,1)}), bf16[16,8,16,128]{3,2,1,0:T(8,128)(2,1)}, u32[]{:S(2)}, u32[]{:S(2)}) async-start(bf16[16,8,16,128]{3,2,1,0:T(8,128)(2,1)} %shard_map.46), calls=%async_computation | async-start | bytes 1048576 | tf_op jit(solution)/shard_map/all_to_all | solution.py:502
  12.7 32.7 %copy-start = (bf16[256,4096]{1,0:T(8,128)(2,1)S(1)}, bf16[256,4096]{1,0:T(8,128)(2,1)}, u32[]{:S(2)}) copy-start(bf16[256,4096]{1,0:T(8,128)(2,1)} %refs_5_.5) | copy-start | bytes 6291460
  15.3 30.2 %collective-permute-start.5 = (bf16[512,512]{1,0:T(8,128)(2,1)}, bf16[512,512]{1,0:T(8,128)(2,1)}, u32[]{:S(2)}, u32[]{:S(2)}) collective-permute-start(bf16[512,512]{1,0:T(8,128)(2,1)} %maximum_select_fusion.refs_0_), channel_id=1, source_target_pairs={{0,4},{2,6},{4,8},{6,10},{8,12},{10,14},{12,16},{14,18},{16,20},{1... | collective-permute-start | bytes 1572872 | tf_op jit(solution)/shard_map/ppermute | solution.py:490
  21.1 24.4 %collective-permute-start.6 = (bf16[192,512]{1,0:T(8,128)(2,1)}, bf16[192,512]{1,0:T(8,128)(2,1)}, u32[]{:S(2)}, u32[]{:S(2)}) collective-permute-start(bf16[192,512]{1,0:T(8,128)(2,1)} %dynamic-slice_select_fusion), channel_id=1, source_target_pairs={{0,8},{2,10},{4,12},{6,14},{8,16},{10,18},{12,20},{14,22},{16,24},... | collective-permute-start | bytes 589832 | tf_op jit(solution)/shard_map/ppermute | solution.py:490
  28.0 6.4 %collective-permute-start.1 = (bf16[2,176,128]{2,1,0:T(8,128)(2,1)S(1)}, bf16[2,176,128]{2,1,0:T(8,128)(2,1)}, u32[]{:S(2)}, u32[]{:S(2)}) collective-permute-start(bf16[2,176,128]{2,1,0:T(8,128)(2,1)S(1)} %shard_map.47), channel_id=1, source_target_pairs={{0,4},{2,6},{4,0},{6,2},{8,12},{10,14},{12,8},{14,10},{16,20},{18,... | collective-permute-start | bytes 270344 | tf_op jit(solution)/shard_map/ppermute | solution.py:490
  35.4 22.9 %collective-permute-start.2 = (bf16[2,2,176,128]{3,2,1,0:T(8,128)(2,1)S(1)}, bf16[2,2,176,128]{3,2,1,0:T(8,128)(2,1)S(1)}, u32[]{:S(2)}, u32[]{:S(2)}) collective-permute-start(bf16[2,2,176,128]{3,2,1,0:T(8,128)(2,1)S(1)} %maximum_select_fusion.1.refs_0_), channel_id=1, source_target_pairs={{0,8},{2,10},{4,12},{6,14},{8,16},{10,18},{12,20},{14,22},{16,24},... | collective-permute-start | bytes 540680 | tf_op jit(solution)/shard_map/ppermute | solution.py:490
  40.2 18.1 %collective-permute-start.3 = (bf16[2,2,176,128]{3,2,1,0:T(8,128)(2,1)S(1)}, bf16[2,2,176,128]{3,2,1,0:T(8,128)(2,1)S(1)}, u32[]{:S(2)}, u32[]{:S(2)}) collective-permute-start(bf16[2,2,176,128]{3,2,1,0:T(8,128)(2,1)S(1)} %maximum_select_fusion.1.refs_0_), channel_id=1, source_target_pairs={{0,16},{2,18},{4,20},{6,22},{8,24},{10,26},{12,28},{14,30},{16,0},... | collective-permute-start | bytes 540680 | tf_op jit(solution)/shard_map/ppermute | solution.py:490
  43.2 15.1 %collective-permute-start.4 = (bf16[2,2,176,128]{3,2,1,0:T(8,128)(2,1)S(1)}, bf16[2,2,176,128]{3,2,1,0:T(8,128)(2,1)S(1)}, u32[]{:S(2)}, u32[]{:S(2)}) collective-permute-start(bf16[2,2,176,128]{3,2,1,0:T(8,128)(2,1)S(1)} %maximum_select_fusion.1.refs_0_), channel_id=1, source_target_pairs={{0,24},{2,26},{4,28},{6,30},{8,0},{10,2},{12,4},{14,6},{16,8},{18,... | collective-permute-start | bytes 540680 | tf_op jit(solution)/shard_map/ppermute | solution.py:490
  63.2 19.9 %collective-permute-start.7 = (bf16[128,1024]{1,0:T(8,128)(2,1)S(1)}, bf16[128,1024]{1,0:T(8,128)(2,1)S(1)}, u32[]{:S(2)}, u32[]{:S(2)}) collective-permute-start(bf16[128,1024]{1,0:T(8,128)(2,1)S(1)} %get-tuple-element.39), channel_id=1, source_target_pairs={{0,1},{1,0},{2,3},{3,2},{4,5},{5,4},{6,7},{7,6},{8,9},{9,8},{10,11... | collective-permute-start | bytes 786440 | tf_op jit(solution)/shard_map/ppermute | solution.py:547
  64.5 20.1 %collective-permute-start.8 = (bf16[128,1024]{1,0:T(8,128)(2,1)}, bf16[128,1024]{1,0:T(8,128)(2,1)}, u32[]{:S(2)}, u32[]{:S(2)}) collective-permute-start(bf16[128,1024]{1,0:T(8,128)(2,1)} %get-tuple-element.40), channel_id=1, source_target_pairs={{0,3},{1,2},{2,1},{3,0},{4,7},{5,6},{6,5},{7,4},{8,11},{9,10},{10,... | collective-permute-start | bytes 786440 | tf_op jit(solution)/shard_map/ppermute | solution.py:547
  71.3 13.3 %collective-permute-start.9 = (bf16[128,1024]{1,0:T(8,128)(2,1)}, bf16[128,1024]{1,0:T(8,128)(2,1)}, u32[]{:S(2)}, u32[]{:S(2)}) collective-permute-start(bf16[128,1024]{1,0:T(8,128)(2,1)} %get-tuple-element.45), channel_id=1, source_target_pairs={{0,1},{1,0},{2,3},{3,2},{4,5},{5,4},{6,7},{7,6},{8,9},{9,8},{10,11... | collective-permute-start | bytes 786440 | tf_op jit(solution)/shard_map/ppermute | solution.py:547
  72.5 15.8 %collective-permute-start.10 = (bf16[128,1024]{1,0:T(8,128)(2,1)}, bf16[128,1024]{1,0:T(8,128)(2,1)}, u32[]{:S(2)}, u32[]{:S(2)}) collective-permute-start(bf16[128,1024]{1,0:T(8,128)(2,1)} %get-tuple-element.46), channel_id=1, source_target_pairs={{0,3},{1,2},{2,1},{3,0},{4,7},{5,6},{6,5},{7,4},{8,11},{9,10},{10,... | collective-permute-start | bytes 786440 | tf_op jit(solution)/shard_map/ppermute | solution.py:547
  81.3 0.7 copy-start.1
  82.1 0.7 copy-start.2
  82.8 5.5 %collective-permute-start.11 = (bf16[128,1024]{1,0:T(8,128)(2,1)}, bf16[128,1024]{1,0:T(8,128)(2,1)S(1)}, u32[]{:S(2)}, u32[]{:S(2)}) collective-permute-start(bf16[128,1024]{1,0:T(8,128)(2,1)} %get-tuple-element.55), channel_id=1, source_target_pairs={{0,2},{1,3},{2,0},{3,1},{4,6},{5,7},{6,4},{7,5},{8,10},{9,11},{10,... | collective-permute-start | bytes 786440 | tf_op jit(solution)/shard_map/ppermute | solution.py:547
  83.1 0.7 copy-start.4
  83.8 4.5 %collective-permute-start.12 = (bf16[128,1024]{1,0:T(8,128)(2,1)}, bf16[128,1024]{1,0:T(8,128)(2,1)S(1)}, u32[]{:S(2)}, u32[]{:S(2)}) collective-permute-start(bf16[128,1024]{1,0:T(8,128)(2,1)} %get-tuple-element.56), channel_id=1, source_target_pairs={{0,2},{1,3},{2,0},{3,1},{4,6},{5,7},{6,4},{7,5},{8,10},{9,11},{10,... | collective-permute-start | bytes 786440 | tf_op jit(solution)/shard_map/ppermute | solution.py:547
  88.3 0.7 copy-start.5
  89.0 0.7 copy-start.6

commit v3 on v2

--- a/solution.py
+++ b/solution.py
@@ -87,7 +87,8 @@
     return jnp.dot(table, own, preferred_element_type=jnp.float32).astype(jnp.bfloat16)
 
 
-def window_kernel(sizes, places, n_kv, n_src, n_blk, group, pos_ref, *refs):
+def window_kernel(sizes, places, kvs, n_kv, n_src, n_blk, group, pos_ref, *refs):
+    n_mine = len(kvs)
     n_pieces = len(sizes)
     pieces, refs = refs[:n_pieces], refs[n_pieces:]
     bias_ref, refs = refs[0], refs[1:]
@@ -105,33 +106,33 @@
     count = iter(range(sem.shape[0]))
 
     loads = []
-    for j in range(n_kv):
+    for m, j in enumerate(kvs):
         mine = []
         lanes = pl.ds(j * 2 * HEAD_SIZE, 2 * HEAD_SIZE)
         for index in range(n_pieces):
             at = pl.ds(places[index] * BLK, sizes[index])
-            mine.append((pieces[index].at[:, lanes], table.at[j, at]))
-        mine.append((bias_ref.at[j], mask.at[j]))
+            mine.append((pieces[index].at[:, lanes], table.at[m, at]))
+        mine.append((bias_ref.at[j], mask.at[m]))
         first = pl.multiple_of((core * n_kv + j) * width, width)
         q_lanes = [pl.ds(first, width), pl.ds(j * width, width)]
         for source in range(n_src):
-            at = pl.ds((j * n_src + source) * tok, tok)
+            at = pl.ds((m * n_src + source) * tok, tok)
             mine.append((q_in[source].at[:, q_lanes[source]], q_ref.at[at]))
         loads.append([pltpu.make_async_copy(*pair, sem.at[next(count)]) for pair in mine])
     for mine in loads:
         start_all(mine)
-    for j in range(n_kv):
-        vaug[j, :, HEAD_SIZE:] = jnp.ones((n_rows, LANES), jnp.bfloat16)
+    for m in range(n_mine):
+        vaug[m, :, HEAD_SIZE:] = jnp.ones((n_rows, LANES), jnp.bfloat16)
         for odd in range(2):
-            kaug[j, odd, HEAD_SIZE + n_mask:, :] = jnp.zeros((LANES - n_mask, n_lanes), jnp.bfloat16)
-    for j in range(n_kv):
-        wait_all(loads[j])
+            kaug[m, odd, HEAD_SIZE + n_mask:, :] = jnp.zeros((LANES - n_mask, n_lanes), jnp.bfloat16)
+    for m in range(n_mine):
+        wait_all(loads[m])
         for odd in range(2):
-            kaug[j, odd, :HEAD_SIZE, :] = table[j, odd * BLK:odd * BLK + n_lanes, :HEAD_SIZE].T
-            kaug[j, odd, HEAD_SIZE:HEAD_SIZE + n_mask, :] = spread_mask(
-                mask[j], lambda key: key // BLK + odd, n_lanes
+            kaug[m, odd, :HEAD_SIZE, :] = table[m, odd * BLK:odd * BLK + n_lanes, :HEAD_SIZE].T
+            kaug[m, odd, HEAD_SIZE:HEAD_SIZE + n_mask, :] = spread_mask(
+                mask[m], lambda key: key // BLK + odd, n_lanes
             )
-        vaug[j, :, :HEAD_SIZE] = table[j, :, HEAD_SIZE:]
+        vaug[m, :, :HEAD_SIZE] = table[m, :, HEAD_SIZE:]
 
     u = lax.broadcasted_iota(jnp.int32, (rows, LANES), 1) - (LANES - BLK)
     t = lax.broadcasted_iota(jnp.int32, (rows, LANES), 0) % BLK
@@ -144,7 +145,7 @@
         ]
 
     def two_blocks(turn, carry):
-        j, pair = turn // n_pairs, turn % n_pairs
+        m, pair = turn // n_pairs, turn % n_pairs
         base = 2 * pair
         if n_src == 2:
             per = n_blk // 2
@@ -154,7 +155,7 @@
 
         def scores_of(n):
             q = with_selector(head_rows(q_rows, n, group), base + n, group)
-            return jnp.dot(q, kaug[j, n, :, even], preferred_element_type=jnp.float32)
+            return jnp.dot(q, kaug[m, n, :, even], preferred_element_type=jnp.float32)
 
         def softmax_of(n, scores):
             parts = tiles(scores)
@@ -164,7 +165,7 @@
 
         def finish(n, top, weights):
             at = pl.ds(pl.multiple_of((base + n) * BLK, BLK), span)
-            total = jnp.dot(weights, vaug[j, at, :], preferred_element_type=jnp.float32)
+            total = jnp.dot(weights, vaug[m, at, :], preferred_element_type=jnp.float32)
             acc_ref[2 * turn + n] = total[:, :HEAD_SIZE] / total[:, HEAD_SIZE:]
             lse_ref[2 * turn + n] = top + jnp.log(total[:, HEAD_SIZE:]) * LOG_SCALE
 
@@ -172,34 +173,35 @@
         start_all(stores(turn))
         return carry
 
-    lax.fori_loop(0, n_kv * n_pairs, two_blocks, 0)
-    for turn in range(n_kv * n_pairs):
+    lax.fori_loop(0, n_mine * n_pairs, two_blocks, 0)
+    for turn in range(n_mine * n_pairs):
         wait_all(stores(turn))
 
 
-def window_part(pos, pieces, places, bias, queries, q_recv, n_kv, n_src, n_blk, group, n_win):
+def window_part(pos, pieces, places, kvs, bias, queries, q_recv, n_kv, n_src, n_blk, group, n_win):
+    n_mine = len(kvs)
     width = group * HEAD_SIZE
     rows = group * BLK
     n_rows = n_win * BLK
-    n_turns = n_kv * n_src * n_blk // 2
+    n_turns = n_mine * n_src * n_blk // 2
     q_args = [queries] if n_src == 1 else [queries, q_recv]
     out_shape = jax.ShapeDtypeStruct((2 * n_turns, rows, LANES), jnp.float32)
     sizes = [piece.shape[0] for piece in pieces]
     keys = 2 * n_turns * rows * (SMAX + 1) * BLK
     return pl.pallas_call(
-        functools.partial(window_kernel, sizes, places, n_kv, n_src, n_blk, group),
+        functools.partial(window_kernel, sizes, places, kvs, n_kv, n_src, n_blk, group),
         in_specs=[pl.BlockSpec(memory_space=pltpu.SMEM)]
         + [ANY] * (len(pieces) + 1 + n_src),
         out_specs=[ANY, ANY],
         scratch_shapes=[
-            pltpu.VMEM((n_kv, n_rows, 2 * HEAD_SIZE), jnp.bfloat16),
-            pltpu.VMEM(bias.shape, jnp.bfloat16),
-            pltpu.VMEM((n_kv, 2, 2 * LANES, n_rows - BLK), jnp.bfloat16),
-            pltpu.VMEM((n_kv, n_rows, 2 * LANES), jnp.bfloat16),
+            pltpu.VMEM((n_mine, n_rows, 2 * HEAD_SIZE), jnp.bfloat16),
+            pltpu.VMEM((n_mine,) + bias.shape[1:], jnp.bfloat16),
+            pltpu.VMEM((n_mine, 2, 2 * LANES, n_rows - BLK), jnp.bfloat16),
+            pltpu.VMEM((n_mine, n_rows, 2 * LANES), jnp.bfloat16),
             pltpu.VMEM((2 * n_turns * BLK, width), jnp.bfloat16),
             pltpu.VMEM(out_shape.shape, jnp.float32),
             pltpu.VMEM(out_shape.shape, jnp.float32),
-            pltpu.SemaphoreType.DMA((n_kv * (len(pieces) + 1 + n_src),)),
+            pltpu.SemaphoreType.DMA((n_mine * (len(pieces) + 1 + n_src),)),
             pltpu.SemaphoreType.DMA((n_turns, 2)),
         ],
         out_shape=[out_shape, out_shape],
@@ -210,14 +212,15 @@
     )(pos, *pieces, bias, *q_args)
 
 
-def vertical_kernel(sources, kvs, n_kv, n_vert, group, n_blk, n_src, n_dst, other, pos_ref, *refs):
+def vertical_kernel(sources, kvs, n_kv, n_vert, group, n_blk, n_src, n_dst, other, direct, pos_ref, *refs):
     n_pieces = max(source[0] for source in sources) + 1
     n_mine = len(kvs)
     pieces, refs = refs[:n_pieces], refs[n_pieces:]
     bias_ref, refs = refs[0], refs[1:]
     q_in, refs = refs[:n_src], refs[n_src:]
-    acc_in, lse_in, refs = refs[0], refs[1], refs[2:]
-    outs_ref, refs = refs[:n_mine * n_src], refs[n_mine * n_src:]
+    states_in, refs = refs[:2], refs[2:]
+    n_outs = 1 + n_mine * (n_src - 1) if direct else n_mine * n_src
+    outs_ref, refs = refs[:n_outs], refs[n_outs:]
     table, mask, kaug, vaug, q_ref, acc_ref, lse_ref, out_ref, sem, turn_sem = refs
     core, tp_pos = pos_ref[0], pos_ref[1]
     per_dst = n_blk // n_dst
@@ -254,10 +257,10 @@
                 q_in[source].at[q_rows, q_lanes[source]], q_ref.at[turn], turn_sem.at[turn, 0]
             ),
             pltpu.make_async_copy(
-                acc_in.at[blocks], acc_ref.at[turn], turn_sem.at[turn, 1]
+                states_in[0].at[blocks], acc_ref.at[turn], turn_sem.at[turn, 1]
             ),
             pltpu.make_async_copy(
-                lse_in.at[blocks], lse_ref.at[turn], turn_sem.at[turn, 2]
+                states_in[1].at[blocks], lse_ref.at[turn], turn_sem.at[turn, 2]
             ),
         ]
 
@@ -311,16 +314,25 @@
         return carry
 
     lax.fori_loop(0, n_mine * n_src, one_turn, 0)
-    stores = [
-        pltpu.make_async_copy(out_ref.at[turn], outs_ref[turn], turn_sem.at[turn, 3])
-        for turn in range(n_mine * n_src)
-    ]
+    stores = []
+    for m in range(n_mine):
+        for source in range(n_src):
+            turn = m * n_src + source
+            if direct and source == 0:
+                column = pl.multiple_of(((tp_pos * n_src + core) * n_kv + kvs[m]) * width, width)
+                target = outs_ref[0].at[:, pl.ds(column, width)]
+            elif direct:
+                target = outs_ref[1 + m]
+            else:
+                target = outs_ref[turn]
+            stores.append(pltpu.make_async_copy(out_ref.at[turn], target, turn_sem.at[turn, 3]))
     start_all(stores)
     wait_all(stores)
 
 
 def vertical_part(
-    pos, pieces, sources, kvs, bias, queries, q_recv, state, n_kv, n_src, n_dst, other, n_blk, group, n_vert
+    pos, pieces, sources, kvs, bias, queries, q_recv, states,
+    n_kv, n_src, n_dst, other, direct, n_blk, group, n_vert,
 ):
     n_mine = len(kvs)
     n_turns = n_mine * n_src
@@ -329,15 +341,19 @@
     per_dst = n_blk // n_dst
     n_keys = round_up(n_vert * BLK, LANES)
     q_args = [queries] if n_src == 1 else [queries, q_recv]
-    out_shape = jax.ShapeDtypeStruct((per_dst * BLK, width), jnp.bfloat16)
+    piece = jax.ShapeDtypeStruct((per_dst * BLK, width), jnp.bfloat16)
+    out_shapes = [piece] * n_turns
+    if direct:
+        whole = (per_dst * BLK, width * n_kv * n_src * n_dst)
+        out_shapes = [jax.ShapeDtypeStruct(whole, jnp.bfloat16)] + [piece] * (n_mine * (n_src - 1))
     keys = n_turns * per_dst * rows * n_keys
-    args = [*pieces, bias, *q_args, *state]
+    args = [*pieces, bias, *q_args, *states]
     return pl.pallas_call(
         functools.partial(
-            vertical_kernel, sources, kvs, n_kv, n_vert, group, n_blk, n_src, n_dst, other
+            vertical_kernel, sources, kvs, n_kv, n_vert, group, n_blk, n_src, n_dst, other, direct
         ),
         in_specs=[pl.BlockSpec(memory_space=pltpu.SMEM)] + [ANY] * len(args),
-        out_specs=[ANY] * n_turns,
+        out_specs=[ANY] * len(out_shapes),
         scratch_shapes=[
             pltpu.VMEM((n_mine, 2, n_keys, LANES), jnp.bfloat16),
             pltpu.VMEM((n_mine,) + bias.shape[1:], jnp.bfloat16),
@@ -350,7 +366,7 @@
             pltpu.SemaphoreType.DMA((n_mine * (N_PIECES + 1),)),
             pltpu.SemaphoreType.DMA((n_turns, 4)),
         ],
-        out_shape=[out_shape] * n_turns,
+        out_shape=out_shapes,
         compiler_params=pltpu.CompilerParams(vmem_limit_bytes=(16 + round_up(8 * n_keys // 768, 8)) * 1024 * 1024),
         cost_estimate=pl.CostEstimate(
             flops=keys * 1024, bytes_accessed=8 * 1024 * 1024, transcendentals=keys
@@ -402,34 +418,36 @@
     )(index, table)
 
 
-def assemble_kernel(widths, column_ref, *refs):
-    n = len(widths)
-    pieces, out, buffers, sem = refs[:n], refs[n], refs[n + 1:-1], refs[-1]
+def assemble_kernel(n, column_ref, *refs):
+    pieces, (_, out), buffers, sem = refs[:n], refs[n:n + 2], refs[n + 2:-1], refs[-1]
     loads = [pltpu.make_async_copy(pieces[i], buffers[i], sem.at[0, i]) for i in range(n)]
     start_all(loads)
     stores = []
     for i in range(n):
         loads[i].wait()
-        start = pl.multiple_of(column_ref[i], LANES)
+        width = buffers[i].shape[1]
+        start = pl.multiple_of(column_ref[i], width)
         stores.append(
-            pltpu.make_async_copy(buffers[i], out.at[:, pl.ds(start, widths[i])], sem.at[1, i])
+            pltpu.make_async_copy(buffers[i], out.at[:, pl.ds(start, width)], sem.at[1, i])
         )
         stores[-1].start()
     wait_all(stores)
 
 
-def assemble(columns, pieces):
-    rows = pieces[0].shape[0]
-    widths = [piece.shape[1] for piece in pieces]
+def assemble(out, results, vmem):
+    pieces = [piece for piece, _ in results]
+    columns = jnp.stack([column for _, column in results]).astype(jnp.int32)
+    n = len(pieces)
     return pl.pallas_call(
-        functools.partial(assemble_kernel, widths),
-        in_specs=[pl.BlockSpec(memory_space=pltpu.SMEM)] + [ANY] * len(pieces),
+        functools.partial(assemble_kernel, n),
+        in_specs=[pl.BlockSpec(memory_space=pltpu.SMEM)] + [ANY] * (n + 1),
         out_specs=ANY,
-        out_shape=jax.ShapeDtypeStruct((rows, sum(widths)), pieces[0].dtype),
+        out_shape=jax.ShapeDtypeStruct(out.shape, out.dtype),
         scratch_shapes=[pltpu.VMEM(piece.shape, piece.dtype) for piece in pieces]
-        + [pltpu.SemaphoreType.DMA((2, len(pieces)))],
-        compiler_params=pltpu.CompilerParams(vmem_limit_bytes=ALL_VMEM),
-    )(columns, *pieces)
+        + [pltpu.SemaphoreType.DMA((2, n))],
+        input_output_aliases={n + 1: 0},
+        compiler_params=pltpu.CompilerParams(vmem_limit_bytes=vmem),
+    )(columns, *pieces, out)
 
 
 def mask_tables(vert, slash, first, n_query, n_win, n_vert, n_blocks):
@@ -489,21 +507,15 @@
                 pairs.append((source, 2 * to + source % 2))
         return lax.ppermute(array, "seq", pairs)
 
-    to_pair = jnp.concatenate(
-        [
-            lax.dynamic_slice_in_dim(queries, (1 - core) * q_width, q_width, 1),
-            lax.dynamic_slice_in_dim(kv_rows, (1 - core) * kv_width, kv_width, 1),
-        ],
-        axis=1,
-    )
-    from_pair = lax.ppermute(to_pair, "seq", [(i, i ^ 1) for i in range(n_seq)])
-
-    rows, _ = lax.optimization_barrier((kv_rows, to_pair))
+    pair = [(i, i ^ 1) for i in range(n_seq)]
+    kv_other = lax.dynamic_slice_in_dim(kv_rows, (1 - core) * kv_width, kv_width, 1)
+    theirs = lax.ppermute(kv_other, "seq", pair)
+
+    rows, _ = lax.optimization_barrier((kv_rows, kv_other))
     held = lax.all_to_all(split_rows(rows, n_kv), "seq", split_axis=0, concat_axis=0, tiled=True)
     held = held.reshape(n_blocks * n_kv, PIECE, LANES)
 
     mine = lax.dynamic_slice_in_dim(kv_rows, core * kv_width, kv_width, 1)
-    theirs = from_pair[:, q_width:]
     here = jnp.where(
         core == 0,
         jnp.concatenate([mine, theirs], axis=0),
@@ -514,7 +526,10 @@
     before = by_chip(here, lambda c: c + 1 if c + 1 < n_chip else None)
     back = by_chip(tail, lambda c: c + 2 if c + 2 < n_chip else None)
 
-    vertical, slash, here, tail = lax.optimization_barrier((vertical, slash, here, tail))
+    q_rows, here, tail = lax.optimization_barrier((queries, here, tail))
+    q_other = lax.dynamic_slice_in_dim(q_rows, (1 - core) * q_width, q_width, 1)
+    from_pair = lax.ppermute(q_other, "seq", pair)
+
     first_head = tp_pos * heads_loc + core * heads
     my_vert = lax.dynamic_slice_in_dim(vertical, first_head, heads, 0).reshape(n_kv, group, -1)
     my_slash = lax.dynamic_slice_in_dim(slash, first_head, heads, 0).reshape(n_kv, group, -1)
@@ -524,6 +539,7 @@
 
     index = (units * n_kv + jnp.arange(n_kv, dtype=jnp.int32)[:, None]).reshape(-1)
     picked = select_units(index, held, n_kv, n_vert)
+    picked, from_pair = lax.optimization_barrier((picked, from_pair))
     beside = by_chip(picked, lambda c: c ^ 1)
     both = jnp.where(near == 0, jnp.stack([picked, beside]), jnp.stack([beside, picked]))
     pieces, sources, slots = [both], [(0, 0), (0, 1)], [2 * far, 2 * far + 1]
@@ -534,8 +550,8 @@
         slots += [2 * owner, 2 * owner + 1]
 
     pos = jnp.stack([core, tp_pos] + slots).astype(jnp.int32)
-    state = window_part(
-        pos, [here, before, back], [SMAX, extra, 0], bias_w, queries, from_pair,
+    states = window_part(
+        pos, [here, back, before], [SMAX, 0, extra], tuple(range(n_kv)), bias_w, queries, from_pair,
         n_kv, 2, n_blk, group, n_win,
     )
 
@@ -549,21 +565,21 @@
     results = []
     for other_tp, kvs in [(1, (j,)) for j in range(n_kv)] + [(0, tuple(range(n_kv)))]:
         outs = vertical_part(
-            pos, pieces, sources, kvs, bias_v, queries, from_pair, state,
-            n_kv, 2, 2, other_tp, n_blk, group, n_vert,
+            pos, pieces, sources, kvs, bias_v, queries, from_pair, states,
+            n_kv, 2, 2, other_tp, not other_tp, n_blk, group, n_vert,
         )
-        outs, state = lax.optimization_barrier((outs, state))
+        outs, states = lax.optimization_barrier((outs, states))
         from_tp = 1 - tp_pos if other_tp else tp_pos
-        for other_core in (0, 1):
+        if not other_tp:
+            out, *outs = outs
+        cores = (0, 1) if other_tp else (1,)
+        turns = [(j, other_core) for j in kvs for other_core in cores]
+        for (j, other_core), piece in zip(turns, outs, strict=True):
             from_core = 1 - core if other_core else core
-            for m, j in enumerate(kvs):
-                piece = outs[m * 2 + other_core]
-                if other_core or other_tp:
-                    piece = swap(piece, other_core, other_tp)
-                column = ((from_tp * 2 + from_core) * n_kv + j) * group * HEAD_SIZE
-                results.append((piece, column))
-    columns = jnp.stack([column for _, column in results]).astype(jnp.int32)
-    return assemble(columns, [piece for piece, _ in results])
+            column = ((from_tp * 2 + from_core) * n_kv + j) * group * HEAD_SIZE
+            results.append((swap(piece, other_core, other_tp), column))
+    early = 2 * (n_kv - 1)
+    return assemble(assemble(out, results[:early], ALL_VMEM), results[early:], VMEM_LIMIT // 4)
 
 
 def gathered(queries, kv_rows, vertical, slash):
@@ -588,8 +604,8 @@
     padded = jnp.pad(full, ((SMAX * BLK, 0), (0, 0)))
     window = lax.dynamic_slice_in_dim(padded, first * BLK, n_win * BLK, 0)
     pos = jnp.stack([jnp.int32(0), tp_pos] + [jnp.int32(i) for i in range(N_PIECES)])
-    state = window_part(
-        pos, [window], [0], bias_w, queries, None, n_kv, 1, n_blk, group, n_win
+    states = window_part(
+        pos, [window], [0], tuple(range(n_kv)), bias_w, queries, None, n_kv, 1, n_blk, group, n_win
     )
     blocks = full.reshape(n_blocks, BLK // PIECE, PIECE, n_kv, 2, LANES)
     listed = jnp.stack([blocks[units[j], :, :, j] for j in range(n_kv)])
@@ -597,9 +613,9 @@
     listed = listed.reshape(N_PIECES, n_kv, n_vert * PIECE, LANES)
     outs = vertical_part(
         pos, [listed], [(0, i) for i in range(N_PIECES)], tuple(range(n_kv)), bias_v, queries, None,
-        state, n_kv, 1, 1, 0, n_blk, group, n_vert,
-    )
-    attended = jnp.concatenate(outs, axis=1)
+        states, n_kv, 1, 1, 0, True, n_blk, group, n_vert,
+    )
+    attended = outs[0]
     return lax.all_to_all(attended, "tp", split_axis=0, concat_axis=1, tiled=True)
 
 

time: 93.3 us -> 89 us (0.954)
  starting transfers between devices: 30.7 us -> 28.1 us
  other arithmetic: 7.19 us -> 4.66 us
  local copies, waits for them, and re-layouts: 7.02 us -> 4.62 us
  Pallas kernels: 37.3 us -> 39.3 us
  waiting for transfers between devices: 10.3 us -> 11.4 us
    ppermute x6, waiting for transfers between devices: 4.76 us -> 7.64 us  [by_chip(): return lax.ppermute(array, 'seq', pairs)]
    ppermute x6, starting transfers between devices: 18.1 us -> 15.7 us  [by_chip(): return lax.ppermute(array, 'seq', pairs)]
    pallas_call x2 -> x3, Pallas kernels: 15.9 us -> 17.7 us  [the longest x1 12.7 us: window_part(): pl.pallas_call(functools.partial(window_kernel, sizes, places, kvs, n_kv,...]
    unnamed x18 -> x10, local copies, waits for them, and re-layouts: 3.58 us -> 1.76 us
    concatenate x1 -> x0, other arithmetic: 1.15 us -> none  [paired(): jnp.concatenate([lax.dynamic_slice_in_dim(queries, (1 - core) * q_width,...]
    select_n x1, other arithmetic: 2.15 us -> 1.01 us  [paired(): jnp.where(core == 0, jnp.concatenate([mine, theirs], axis=0), jnp.concate...]
    ppermute x6, waiting for transfers between devices: 3.72 us -> 2.66 us  [swap(): return lax.ppermute(array, ('seq', 'tp'), pairs)]
    select_n x1, other arithmetic: 0.99 us -> 0.02 us  [paired(): jnp.where(near == 0, jnp.stack([picked, beside]), jnp.stack([beside, pick...]
  transfers between devices with their start and end apart: 14 -> 15, of which waited for: 3 -> 4; matrix products, arithmetic and copies ran while one was open for 8% -> 7% of each run, Pallas kernels for 32% -> 36%
where the time goes in v3:
time: 89 us; the launch traced here: 88.5 us
  Pallas kernels  39.3 us (44%)
  starting transfers between devices  28.1 us (32%)
  waiting for transfers between devices  11.4 us (13%)
  other arithmetic  4.66 us (5%)
  local copies, waits for them, and re-layouts  4.62 us (5%)
    pallas_call x3, Pallas kernels, vertical_part(): pl.pallas_call(functools.partial(vertical_kernel, sources, kvs, n_kv, n_v...  18.5 us
    ppermute x6, starting transfers between devices, by_chip(): return lax.ppermute(array, 'seq', pairs)  15.7 us
    pallas_call x1, Pallas kernels, window_part(): pl.pallas_call(functools.partial(window_kernel, sizes, places, kvs, n_kv,...  12.7 us
    ppermute x6, waiting for transfers between devices, by_chip(): return lax.ppermute(array, 'seq', pairs)  7.64 us
    all_to_all x1, starting transfers between devices, paired(): lax.all_to_all(split_rows(rows, n_kv), 'seq', split_axis=0, concat_axis=0...  7.33 us
    pallas_call x2, Pallas kernels, assemble(): pl.pallas_call(functools.partial(assemble_kernel, n), in_specs=[pl.BlockS...  4.94 us
    ppermute x6, starting transfers between devices, swap(): return lax.ppermute(array, ('seq', 'tp'), pairs)  4.86 us
    ppermute x6, waiting for transfers between devices, swap(): return lax.ppermute(array, ('seq', 'tp'), pairs)  2.66 us
  transfers between devices with their start and end apart: 15, of which 4 were waited for; matrix products, arithmetic and copies ran while one was open for 7% of the time, Pallas kernels for 36%

profile of v3, /device:TPU:1, one launch (start us, length us, event | category | flops | bytes accessed | tf_op | source)
XLA Modules:
  0.0 88.5 jit_solution(4120183866829050519)
XLA Ops:
  0.0 1.1 %constant_dynamic-slice_fusion.2 = (bf16[256,512]{1,0:T(8,128)(2,1)S(1)}, bf16[256,512]{1,0:T(8,128)(2,1)S(1)}) fusion(bf16[256,1024]{1,0:T(8,128)(2,1)} %kv_ref, s32[]{:T(128)S(6)} %select_n.94, s32[]{:T(128)S(6)} %select_n.92), kind=kLoop, calls=%fused_computation.23 | loop fusion | bytes 1048584 | tf_op jit(solution)/shard_map/dynamic_slice | solution.py:518
  1.1 0.1 collective-permute-start
  1.2 2.0 %shard_map.46 = bf16[16,8,16,128]{3,2,1,0:T(8,128)(2,1)} custom-call(bf16[256,1024]{1,0:T(8,128)(2,1)} %kv_ref), custom_call_target="tpu_custom_call" | custom-call | tf_op jit(solution)/shard_map/pallas_call | solution.py:392
  3.3 7.3 %all-to-all-start = ((bf16[16,8,16,128]{3,2,1,0:T(8,128)(2,1)}), bf16[16,8,16,128]{3,2,1,0:T(8,128)(2,1)}, u32[]{:S(2)}, u32[]{:S(2)}) async-start(bf16[16,8,16,128]{3,2,1,0:T(8,128)(2,1)} %shard_map.46), calls=%async_computation | async-start | bytes 1048576 | tf_op jit(solution)/shard_map/all_to_all | solution.py:515
  10.7 0.1 constant_dynamic-slice_fusion
  10.9 0.1 eq.85
  11.0 0.1 fusion
  11.1 0.1 convert_reduce_fusion
  11.2 0.3 fusion.2
  11.5 0.1 copy.17
  11.7 0.3 compare_reduce_fusion
  11.9 0.1 compare_reduce_fusion.2
  12.1 1.7 %dynamic-slice_select_fusion = bf16[192,512]{1,0:T(8,128)(2,1)} fusion(bf16[256,1024]{1,0:T(8,128)(2,1)} %kv_ref, s32[]{:T(128)S(6)} %add.149, s32[]{:T(128)S(6)} %select_n.94, bf16[256,512]{1,0:T(8,128)(2,1)S(1)} %collective-permute-done, pred[]{:T(512)S(6)} %eq.92), kind=kLoop, calls=%fused_computation.2 | loop fusion | flops 98304 | bytes 589833 | tf_op jit(solution)/shard_map/jit(_where)/select_n | solution.py:525
  13.7 1.0 %maximum_select_fusion.refs_0_ = bf16[512,512]{1,0:T(8,128)(2,1)} fusion(bf16[256,512]{1,0:T(8,128)(2,1)S(1)} %collective-permute-done, bf16[256,512]{1,0:T(8,128)(2,1)S(1)} %get-tuple-element.55, pred[]{:T(512)S(6)} %eq.92), kind=kLoop, calls=%fused_computation | loop fusion | flops 2359296 | bytes 1048577 | tf_op jit(solution)/shard_map/jit(_where)/select_n | solution.py:519
  14.8 1.1 %constant_dynamic-slice_fusion.1 = bf16[256,2048]{1,0:T(8,128)(2,1)} fusion(bf16[256,4096]{1,0:T(8,128)(2,1)S(1)} %copy-done, s32[]{:T(128)S(6)} %select_n.98), kind=kLoop, calls=%fused_computation.22 | loop fusion | bytes 2097156 | tf_op jit(solution)/shard_map/dynamic_slice | solution.py:530
  15.8 0.2 collective-permute-start.1
  16.0 0.1 compare_reduce_fusion.1
  16.1 0.1 copy.16
  16.2 0.1 add.137.index_ref
  16.3 0.1 and_and_fusion
  16.4 4.3 %collective-permute-start.7 = (bf16[512,512]{1,0:T(8,128)(2,1)}, bf16[512,512]{1,0:T(8,128)(2,1)}, u32[]{:S(2)}, u32[]{:S(2)}) collective-permute-start(bf16[512,512]{1,0:T(8,128)(2,1)} %maximum_select_fusion.refs_0_), channel_id=1, source_target_pairs={{0,4},{2,6},{4,8},{6,10},{8,12},{10,14},{12,16},{14,18},{16,20},{1... | collective-permute-start | bytes 1572872 | tf_op jit(solution)/shard_map/ppermute | solution.py:508
  20.7 0.1 subtract_compare_fusion
  20.7 3.0 %collective-permute-start.6 = (bf16[192,512]{1,0:T(8,128)(2,1)}, bf16[192,512]{1,0:T(8,128)(2,1)}, u32[]{:S(2)}, u32[]{:S(2)}) collective-permute-start(bf16[192,512]{1,0:T(8,128)(2,1)} %dynamic-slice_select_fusion), channel_id=1, source_target_pairs={{0,8},{2,10},{4,12},{6,14},{8,16},{10,18},{12,20},{14,22},{16,24},... | collective-permute-start | bytes 589832 | tf_op jit(solution)/shard_map/ppermute | solution.py:508
  23.7 1.0 %all-to-all-done = bf16[16,8,16,128]{3,2,1,0:T(8,128)(2,1)} async-done(((bf16[16,8,16,128]{3,2,1,0:T(8,128)(2,1)}), bf16[16,8,16,128]{3,2,1,0:T(8,128)(2,1)}, u32[]{:S(2)}, u32[]{:S(2)}) %all-to-all-start) | async-done | bytes 524320 | tf_op jit(solution)/shard_map/all_to_all | solution.py:515
  24.8 1.1 %shard_map.47 = bf16[2,176,128]{2,1,0:T(8,128)(2,1)S(1)} custom-call(s32[22]{0:T(128)S(1)} %add.137.index_ref, bf16[128,16,128]{2,1,0:T(8,128)(2,1)} %bitcast.14.table), custom_call_target="tpu_custom_call" | custom-call | tf_op jit(solution)/shard_map/pallas_call | solution.py:409
  25.9 0.9 %collective-permute-start.2 = (bf16[2,176,128]{2,1,0:T(8,128)(2,1)S(1)}, bf16[2,176,128]{2,1,0:T(8,128)(2,1)S(1)}, u32[]{:S(2)}, u32[]{:S(2)}) collective-permute-start(bf16[2,176,128]{2,1,0:T(8,128)(2,1)S(1)} %shard_map.47), channel_id=1, source_target_pairs={{0,4},{2,6},{4,0},{6,2},{8,12},{10,14},{12,8},{14,10},{16,20},{18,... | collective-permute-start | bytes 270344 | tf_op jit(solution)/shard_map/ppermute | solution.py:508
  27.0 0.1 stack.86.pos_ref
  27.1 6.8 %collective-permute-done.2 = bf16[2,176,128]{2,1,0:T(8,128)(2,1)S(1)} collective-permute-done((bf16[2,176,128]{2,1,0:T(8,128)(2,1)S(1)}, bf16[2,176,128]{2,1,0:T(8,128)(2,1)S(1)}, u32[]{:S(2)}, u32[]{:S(2)}) %collective-permute-start.2) | collective-permute-done | bytes 90144 | tf_op jit(solution)/shard_map/ppermute | solution.py:508
  33.9 6.0 %collective-permute-start.5 = (bf16[2,2,176,128]{3,2,1,0:T(8,128)(2,1)S(1)}, bf16[2,2,176,128]{3,2,1,0:T(8,128)(2,1)S(1)}, u32[]{:S(2)}, u32[]{:S(2)}) collective-permute-start(bf16[2,2,176,128]{3,2,1,0:T(8,128)(2,1)S(1)} %maximum_select_fusion.1.refs_0_), channel_id=1, source_target_pairs={{0,24},{2,26},{4,28},{6,30},{8,0},{10,2},{12,4},{14,6},{16,8},{18,... | collective-permute-start | bytes 540680 | tf_op jit(solution)/shard_map/ppermute | solution.py:508
  40.0 1.4 %collective-permute-start.3 = (bf16[2,2,176,128]{3,2,1,0:T(8,128)(2,1)S(1)}, bf16[2,2,176,128]{3,2,1,0:T(8,128)(2,1)S(1)}, u32[]{:S(2)}, u32[]{:S(2)}) collective-permute-start(bf16[2,2,176,128]{3,2,1,0:T(8,128)(2,1)S(1)} %maximum_select_fusion.1.refs_0_), channel_id=1, source_target_pairs={{0,8},{2,10},{4,12},{6,14},{8,16},{10,18},{12,20},{14,22},{16,24},... | collective-permute-start | bytes 540680 | tf_op jit(solution)/shard_map/ppermute | solution.py:508
  41.4 1.0 %copy-done.1 = bf16[512,512]{1,0:T(8,128)(2,1)S(1)} copy-done((bf16[512,512]{1,0:T(8,128)(2,1)S(1)}, bf16[512,512]{1,0:T(8,128)(2,1)}, u32[]{:S(2)}) %copy-start.1) | copy-done | bytes 524312
  42.4 12.7 %shard_map.48 = (f32[16,512,128]{2,1,0:T(8,128)S(1)}, f32[16,512,128]{2,1,0:T(8,128)S(1)}) custom-call(s32[10]{0:T(128)S(1)} %stack.86.pos_ref, bf16[512,512]{1,0:T(8,128)(2,1)S(1)} %copy-done.1, bf16[192,512]{1,0:T(8,128)(2,1)} %collective-permute-done.6.refs_1_, bf16[512,512]{1,0:T(8,128)(2,1)} %collective-permute-done.7.refs_2_, ...), custom_call_target="tpu_custom_call" | custom-call | flops 6442450944 | bytes 16777216 | tf_op jit(solution)/shard_map/pallas_call | solution.py:191
  55.2 0.8 collective-permute-done.4.refs_2_
  56.0 4.9 %shard_map.49 = (bf16[128,1024]{1,0:T(8,128)(2,1)S(1)}, bf16[128,1024]{1,0:T(8,128)(2,1)}) custom-call(s32[10]{0:T(128)S(1)} %stack.86.pos_ref, bf16[2,2,176,128]{3,2,1,0:T(8,128)(2,1)S(1)} %maximum_select_fusion.1.refs_0_, bf16[2,2,176,128]{3,2,1,0:T(8,128)(2,1)S(1)} %collective-permute-done.3.refs_1_, ...), custom_call_target="tpu_custom_call" | custom-call | flops 1610612736 | bytes 8388608 | tf_op jit(solution)/shard_map/pallas_call | solution.py:351
  60.9 1.3 %collective-permute-start.12 = (bf16[128,1024]{1,0:T(8,128)(2,1)S(1)}, bf16[128,1024]{1,0:T(8,128)(2,1)S(1)}, u32[]{:S(2)}, u32[]{:S(2)}) collective-permute-start(bf16[128,1024]{1,0:T(8,128)(2,1)S(1)} %get-tuple-element.52), channel_id=1, source_target_pairs={{0,1},{1,0},{2,3},{3,2},{4,5},{5,4},{6,7},{7,6},{8,9},{9,8},{10,11... | collective-permute-start | bytes 786440 | tf_op jit(solution)/shard_map/ppermute | solution.py:563
  62.2 1.4 %collective-permute-start.13 = (bf16[128,1024]{1,0:T(8,128)(2,1)}, bf16[128,1024]{1,0:T(8,128)(2,1)}, u32[]{:S(2)}, u32[]{:S(2)}) collective-permute-start(bf16[128,1024]{1,0:T(8,128)(2,1)} %get-tuple-element.53), channel_id=1, source_target_pairs={{0,3},{1,2},{2,1},{3,0},{4,7},{5,6},{6,5},{7,4},{8,11},{9,10},{10,... | collective-permute-start | bytes 786440 | tf_op jit(solution)/shard_map/ppermute | solution.py:563
  63.6 5.0 %shard_map.50 = (bf16[128,1024]{1,0:T(8,128)(2,1)}, bf16[128,1024]{1,0:T(8,128)(2,1)}) custom-call(s32[10]{0:T(128)S(1)} %stack.86.pos_ref, bf16[2,2,176,128]{3,2,1,0:T(8,128)(2,1)S(1)} %maximum_select_fusion.1.refs_0_, bf16[2,2,176,128]{3,2,1,0:T(8,128)(2,1)S(1)} %collective-permute-done.3.refs_1_, ...), custom_call_target="tpu_custom_call" | custom-call | flops 1610612736 | bytes 8388608 | tf_op jit(solution)/shard_map/pallas_call | solution.py:351
  68.6 1.3 %collective-permute-start.8 = (bf16[128,1024]{1,0:T(8,128)(2,1)}, bf16[128,1024]{1,0:T(8,128)(2,1)S(1)}, u32[]{:S(2)}, u32[]{:S(2)}) collective-permute-start(bf16[128,1024]{1,0:T(8,128)(2,1)} %get-tuple-element.43), channel_id=1, source_target_pairs={{0,1},{1,0},{2,3},{3,2},{4,5},{5,4},{6,7},{7,6},{8,9},{9,8},{10,11... | collective-permute-start | bytes 786440 | tf_op jit(solution)/shard_map/ppermute | solution.py:563
  69.9 0.3 collective-permute-start.9
  70.2 8.6 %shard_map.51 = (bf16[128,8192]{1,0:T(8,128)(2,1)}, bf16[128,1024]{1,0:T(8,128)(2,1)}, bf16[128,1024]{1,0:T(8,128)(2,1)}) custom-call(s32[10]{0:T(128)S(1)} %stack.86.pos_ref, bf16[2,2,176,128]{3,2,1,0:T(8,128)(2,1)S(1)} %maximum_select_fusion.1.refs_0_, bf16[2,2,176,128]{3,2,1,0:T(8,128)(2,1)S(1)} %collective-permute-done.3.refs_1_, ...), custom_call_target="tpu_custom_call" | custom-call | flops 3221225472 | bytes 8388608 | tf_op jit(solution)/shard_map/pallas_call | solution.py:351
  78.8 0.4 collective-permute-start.10
  79.3 0.7 copy-done.2
  80.0 0.2 collective-permute-start.11
  80.1 0.6 pad_add_fusion.1.column_ref
  80.8 0.1 pad_add_fusion.column_ref
  80.9 2.4 %shard_map.52.refs_4_ = bf16[128,8192]{1,0:T(8,128)(2,1)} custom-call(s32[2]{0:T(128)} %pad_add_fusion.1.column_ref, bf16[128,1024]{1,0:T(8,128)(2,1)} %copy-done.2, bf16[128,1024]{1,0:T(8,128)(2,1)} %collective-permute-done.13.refs_1_, bf16[128,8192]{1,0:T(8,128)(2,1)} %get-tuple-element.54.refs_2_), custom_call_target="tpu_custom_call", output_to_operand_aliasing={{}: (3, {})} | custom-call | tf_op jit(solution)/shard_map/pallas_call | solution.py:441
  83.3 2.6 %collective-permute-done.9.refs_1_ = bf16[128,1024]{1,0:T(8,128)(2,1)} collective-permute-done((bf16[128,1024]{1,0:T(8,128)(2,1)}, bf16[128,1024]{1,0:T(8,128)(2,1)}, u32[]{:S(2)}, u32[]{:S(2)}) %collective-permute-start.9) | collective-permute-done | bytes 262176 | tf_op jit(solution)/shard_map/ppermute | solution.py:563
  86.0 2.5 %shard_map.53 = bf16[128,8192]{1,0:T(8,128)(2,1)} custom-call(s32[4]{0:T(128)S(1)} %pad_add_fusion.column_ref, bf16[128,1024]{1,0:T(8,128)(2,1)S(1)} %collective-permute-done.8.refs_0_, bf16[128,1024]{1,0:T(8,128)(2,1)} %collective-permute-done.9.refs_1_, bf16[128,1024]{1,0:T(8,128)(2,1)S(1)} %collective-permute-done.10.refs_2_, ...), custom_call_target="tpu_custom_call", output_to_operand_aliasing={{}: (5, {})} | custom-call | tf_op jit(solution)/shard_map/pallas_call | solution.py:441
  (34 shorter events, 0.4 us)
Async XLA Ops:
  0.0 10.7 %copy-start.3 = (s32[64,8]{0,1:T(8,128)S(1)}, s32[64,8]{0,1:T(8,128)}, u32[]{:S(2)}) copy-start(s32[64,8]{0,1:T(8,128)} %param.7) | copy-start | bytes 6148
  0.0 10.7 %copy-start.4 = (s32[64,8]{0,1:T(8,128)S(1)}, s32[64,8]{0,1:T(8,128)}, u32[]{:S(2)}) copy-start(s32[64,8]{0,1:T(8,128)} %param.6) | copy-start | bytes 6148
  1.1 13.7 %copy-start = (bf16[256,4096]{1,0:T(8,128)(2,1)S(1)}, bf16[256,4096]{1,0:T(8,128)(2,1)}, u32[]{:S(2)}) copy-start(bf16[256,4096]{1,0:T(8,128)(2,1)} %refs_5_.5) | copy-start | bytes 6291460
  1.1 11.0 %collective-permute-start = (bf16[256,512]{1,0:T(8,128)(2,1)S(1)}, bf16[256,512]{1,0:T(8,128)(2,1)S(1)}, u32[]{:S(2)}, u32[]{:S(2)}) collective-permute-start(bf16[256,512]{1,0:T(8,128)(2,1)S(1)} %get-tuple-element.56), channel_id=1, source_target_pairs={{0,2},{2,0},{4,6},{6,4},{8,10},{10,8},{12,14},{14,12},{16,18},{18,... | collective-permute-start | bytes 786440 | tf_op jit(solution)/shard_map/ppermute | solution.py:512
  3.3 21.5 %all-to-all-start = ((bf16[16,8,16,128]{3,2,1,0:T(8,128)(2,1)}), bf16[16,8,16,128]{3,2,1,0:T(8,128)(2,1)}, u32[]{:S(2)}, u32[]{:S(2)}) async-start(bf16[16,8,16,128]{3,2,1,0:T(8,128)(2,1)} %shard_map.46), calls=%async_computation | async-start | bytes 1048576 | tf_op jit(solution)/shard_map/all_to_all | solution.py:515
  15.8 10.0 %collective-permute-start.1 = (bf16[256,2048]{1,0:T(8,128)(2,1)}, bf16[256,2048]{1,0:T(8,128)(2,1)S(1)}, u32[]{:S(2)}, u32[]{:S(2)}) collective-permute-start(bf16[256,2048]{1,0:T(8,128)(2,1)} %constant_dynamic-slice_fusion.1), channel_id=1, source_target_pairs={{0,2},{2,0},{4,6},{6,4},{8,10},{10,8},{12,14},{14,12},{16,18},{18,... | collective-permute-start | bytes 3145736 | tf_op jit(solution)/shard_map/ppermute | solution.py:531
  16.4 25.0 %collective-permute-start.7 = (bf16[512,512]{1,0:T(8,128)(2,1)}, bf16[512,512]{1,0:T(8,128)(2,1)}, u32[]{:S(2)}, u32[]{:S(2)}) collective-permute-start(bf16[512,512]{1,0:T(8,128)(2,1)} %maximum_select_fusion.refs_0_), channel_id=1, source_target_pairs={{0,4},{2,6},{4,8},{6,10},{8,12},{10,14},{12,16},{14,18},{16,20},{1... | collective-permute-start | bytes 1572872 | tf_op jit(solution)/shard_map/ppermute | solution.py:508
  20.7 20.6 %collective-permute-start.6 = (bf16[192,512]{1,0:T(8,128)(2,1)}, bf16[192,512]{1,0:T(8,128)(2,1)}, u32[]{:S(2)}, u32[]{:S(2)}) collective-permute-start(bf16[192,512]{1,0:T(8,128)(2,1)} %dynamic-slice_select_fusion), channel_id=1, source_target_pairs={{0,8},{2,10},{4,12},{6,14},{8,16},{10,18},{12,20},{14,22},{16,24},... | collective-permute-start | bytes 589832 | tf_op jit(solution)/shard_map/ppermute | solution.py:508
  25.9 8.0 %collective-permute-start.2 = (bf16[2,176,128]{2,1,0:T(8,128)(2,1)S(1)}, bf16[2,176,128]{2,1,0:T(8,128)(2,1)S(1)}, u32[]{:S(2)}, u32[]{:S(2)}) collective-permute-start(bf16[2,176,128]{2,1,0:T(8,128)(2,1)S(1)} %shard_map.47), channel_id=1, source_target_pairs={{0,4},{2,6},{4,0},{6,2},{8,12},{10,14},{12,8},{14,10},{16,20},{18,... | collective-permute-start | bytes 270344 | tf_op jit(solution)/shard_map/ppermute | solution.py:508
  33.9 21.3 %collective-permute-start.5 = (bf16[2,2,176,128]{3,2,1,0:T(8,128)(2,1)S(1)}, bf16[2,2,176,128]{3,2,1,0:T(8,128)(2,1)S(1)}, u32[]{:S(2)}, u32[]{:S(2)}) collective-permute-start(bf16[2,2,176,128]{3,2,1,0:T(8,128)(2,1)S(1)} %maximum_select_fusion.1.refs_0_), channel_id=1, source_target_pairs={{0,24},{2,26},{4,28},{6,30},{8,0},{10,2},{12,4},{14,6},{16,8},{18,... | collective-permute-start | bytes 540680 | tf_op jit(solution)/shard_map/ppermute | solution.py:508
  40.0 16.0 %collective-permute-start.4 = (bf16[2,2,176,128]{3,2,1,0:T(8,128)(2,1)S(1)}, bf16[2,2,176,128]{3,2,1,0:T(8,128)(2,1)S(1)}, u32[]{:S(2)}, u32[]{:S(2)}) collective-permute-start(bf16[2,2,176,128]{3,2,1,0:T(8,128)(2,1)S(1)} %maximum_select_fusion.1.refs_0_), channel_id=1, source_target_pairs={{0,16},{2,18},{4,20},{6,22},{8,24},{10,26},{12,28},{14,30},{16,0},... | collective-permute-start | bytes 540680 | tf_op jit(solution)/shard_map/ppermute | solution.py:508
  40.0 16.0 %collective-permute-start.3 = (bf16[2,2,176,128]{3,2,1,0:T(8,128)(2,1)S(1)}, bf16[2,2,176,128]{3,2,1,0:T(8,128)(2,1)S(1)}, u32[]{:S(2)}, u32[]{:S(2)}) collective-permute-start(bf16[2,2,176,128]{3,2,1,0:T(8,128)(2,1)S(1)} %maximum_select_fusion.1.refs_0_), channel_id=1, source_target_pairs={{0,8},{2,10},{4,12},{6,14},{8,16},{10,18},{12,20},{14,22},{16,24},... | collective-permute-start | bytes 540680 | tf_op jit(solution)/shard_map/ppermute | solution.py:508
  41.4 1.0 %copy-start.1 = (bf16[512,512]{1,0:T(8,128)(2,1)S(1)}, bf16[512,512]{1,0:T(8,128)(2,1)}, u32[]{:S(2)}) copy-start(bf16[512,512]{1,0:T(8,128)(2,1)} %maximum_select_fusion.refs_0_) | copy-start | bytes 1572868
  60.9 18.4 %collective-permute-start.12 = (bf16[128,1024]{1,0:T(8,128)(2,1)S(1)}, bf16[128,1024]{1,0:T(8,128)(2,1)S(1)}, u32[]{:S(2)}, u32[]{:S(2)}) collective-permute-start(bf16[128,1024]{1,0:T(8,128)(2,1)S(1)} %get-tuple-element.52), channel_id=1, source_target_pairs={{0,1},{1,0},{2,3},{3,2},{4,5},{5,4},{6,7},{7,6},{8,9},{9,8},{10,11... | collective-permute-start | bytes 786440 | tf_op jit(solution)/shard_map/ppermute | solution.py:563
  62.2 18.7 %collective-permute-start.13 = (bf16[128,1024]{1,0:T(8,128)(2,1)}, bf16[128,1024]{1,0:T(8,128)(2,1)}, u32[]{:S(2)}, u32[]{:S(2)}) collective-permute-start(bf16[128,1024]{1,0:T(8,128)(2,1)} %get-tuple-element.53), channel_id=1, source_target_pairs={{0,3},{1,2},{2,1},{3,0},{4,7},{5,6},{6,5},{7,4},{8,11},{9,10},{10,... | collective-permute-start | bytes 786440 | tf_op jit(solution)/shard_map/ppermute | solution.py:563
  68.6 14.7 %collective-permute-start.8 = (bf16[128,1024]{1,0:T(8,128)(2,1)}, bf16[128,1024]{1,0:T(8,128)(2,1)S(1)}, u32[]{:S(2)}, u32[]{:S(2)}) collective-permute-start(bf16[128,1024]{1,0:T(8,128)(2,1)} %get-tuple-element.43), channel_id=1, source_target_pairs={{0,1},{1,0},{2,3},{3,2},{4,5},{5,4},{6,7},{7,6},{8,9},{9,8},{10,11... | collective-permute-start | bytes 786440 | tf_op jit(solution)/shard_map/ppermute | solution.py:563
  69.9 16.1 %collective-permute-start.9 = (bf16[128,1024]{1,0:T(8,128)(2,1)}, bf16[128,1024]{1,0:T(8,128)(2,1)}, u32[]{:S(2)}, u32[]{:S(2)}) collective-permute-start(bf16[128,1024]{1,0:T(8,128)(2,1)} %get-tuple-element.44), channel_id=1, source_target_pairs={{0,3},{1,2},{2,1},{3,0},{4,7},{5,6},{6,5},{7,4},{8,11},{9,10},{10,... | collective-permute-start | bytes 786440 | tf_op jit(solution)/shard_map/ppermute | solution.py:563
  78.8 7.1 %collective-permute-start.10 = (bf16[128,1024]{1,0:T(8,128)(2,1)}, bf16[128,1024]{1,0:T(8,128)(2,1)S(1)}, u32[]{:S(2)}, u32[]{:S(2)}) collective-permute-start(bf16[128,1024]{1,0:T(8,128)(2,1)} %get-tuple-element.50), channel_id=1, source_target_pairs={{0,2},{1,3},{2,0},{3,1},{4,6},{5,7},{6,4},{7,5},{8,10},{9,11},{10,... | collective-permute-start | bytes 786440 | tf_op jit(solution)/shard_map/ppermute | solution.py:563
  79.3 0.7 copy-start.2
  80.0 6.0 %collective-permute-start.11 = (bf16[128,1024]{1,0:T(8,128)(2,1)}, bf16[128,1024]{1,0:T(8,128)(2,1)S(1)}, u32[]{:S(2)}, u32[]{:S(2)}) collective-permute-start(bf16[128,1024]{1,0:T(8,128)(2,1)} %get-tuple-element.51), channel_id=1, source_target_pairs={{0,2},{1,3},{2,0},{3,1},{4,6},{5,7},{6,4},{7,5},{8,10},{9,11},{10,... | collective-permute-start | bytes 786440 | tf_op jit(solution)/shard_map/ppermute | solution.py:563

commit v4 on v3

--- a/solution.py
+++ b/solution.py
@@ -374,7 +374,11 @@
     )(pos, *args)
 
 
-def split_kernel(n_kv, kv_ref, out_ref):
+def split_kernel(n_kv, core_ref, kv_ref, out_ref, other_ref, mine_ref):
+    half = other_ref.shape[1]
+    core = core_ref[0]
+    other_ref[...] = kv_ref[:, pl.ds(pl.multiple_of((1 - core) * half, half), half)]
+    mine_ref[...] = kv_ref[:, pl.ds(pl.multiple_of(core * half, half), half)]
     for side in range(2):
         for j in range(n_kv):
             for part in range(2):
@@ -387,15 +391,38 @@
                         ]
 
 
-def split_rows(kv_rows, n_kv):
-    n_blk = kv_rows.shape[0] // BLK
+def split_rows(core, kv_rows, n_kv):
+    rows, width = kv_rows.shape
+    pieces = (2 * N_PIECES, rows // BLK * n_kv, PIECE, LANES)
     return pl.pallas_call(
         functools.partial(split_kernel, n_kv),
-        in_specs=[pl.BlockSpec(memory_space=pltpu.VMEM)],
-        out_specs=pl.BlockSpec(memory_space=pltpu.VMEM),
-        out_shape=jax.ShapeDtypeStruct((2 * N_PIECES, n_blk * n_kv, PIECE, LANES), kv_rows.dtype),
+        in_specs=[pl.BlockSpec(memory_space=pltpu.SMEM), pl.BlockSpec(memory_space=pltpu.VMEM)],
+        out_specs=[pl.BlockSpec(memory_space=pltpu.VMEM)] * 3,
+        out_shape=[
+            jax.ShapeDtypeStruct(shape, kv_rows.dtype)
+            for shape in (pieces, (rows, width // 2), (rows, width // 2))
+        ],
         compiler_params=pltpu.CompilerParams(vmem_limit_bytes=ALL_VMEM),
-    )(kv_rows)
+    )(core[None], kv_rows)
+
+
+def join_kernel(core_ref, mine_ref, theirs_ref, here_ref, tail_ref):
+    rows = mine_ref.shape[0]
+    core = core_ref[0]
+    here_ref[pl.ds(pl.multiple_of(core * rows, rows), rows), :] = mine_ref[...]
+    here_ref[pl.ds(pl.multiple_of((1 - core) * rows, rows), rows), :] = theirs_ref[...]
+    tail_ref[...] = here_ref[2 * rows - tail_ref.shape[0]:, :]
+
+
+def join_rows(core, mine, theirs, tail):
+    rows, width = mine.shape
+    return pl.pallas_call(
+        join_kernel,
+        in_specs=[pl.BlockSpec(memory_space=pltpu.SMEM)] + [pl.BlockSpec(memory_space=pltpu.VMEM)] * 2,
+        out_specs=[pl.BlockSpec(memory_space=pltpu.VMEM)] * 2,
+        out_shape=[jax.ShapeDtypeStruct((size, width), mine.dtype) for size in (2 * rows, tail)],
+        compiler_params=pltpu.CompilerParams(vmem_limit_bytes=VMEM_LIMIT // 4),
+    )(core[None], mine, theirs)
 
 
 def select_kernel(n_kv, n_vert, index_ref, table, out):
@@ -508,21 +535,14 @@
         return lax.ppermute(array, "seq", pairs)
 
     pair = [(i, i ^ 1) for i in range(n_seq)]
-    kv_other = lax.dynamic_slice_in_dim(kv_rows, (1 - core) * kv_width, kv_width, 1)
+    split, kv_other, mine = split_rows(core, kv_rows, n_kv)
     theirs = lax.ppermute(kv_other, "seq", pair)
 
-    rows, _ = lax.optimization_barrier((kv_rows, kv_other))
-    held = lax.all_to_all(split_rows(rows, n_kv), "seq", split_axis=0, concat_axis=0, tiled=True)
+    held = lax.all_to_all(split, "seq", split_axis=0, concat_axis=0, tiled=True)
     held = held.reshape(n_blocks * n_kv, PIECE, LANES)
 
-    mine = lax.dynamic_slice_in_dim(kv_rows, core * kv_width, kv_width, 1)
-    here = jnp.where(
-        core == 0,
-        jnp.concatenate([mine, theirs], axis=0),
-        jnp.concatenate([theirs, mine], axis=0),
-    )
     extra = SMAX - n_query
-    tail = jnp.where(core == 0, theirs[-extra * BLK:], mine[-extra * BLK:])
+    here, tail = join_rows(core, mine, theirs, extra * BLK)
     before = by_chip(here, lambda c: c + 1 if c + 1 < n_chip else None)
     back = by_chip(tail, lambda c: c + 2 if c + 2 < n_chip else None)
 

time: 89 us -> 88.1 us (0.990)
  other arithmetic: 4.66 us -> 1.99 us
  local copies, waits for them, and re-layouts: 4.62 us -> 5.98 us
  Pallas kernels: 39.3 us -> 40.3 us
    select_n x2 -> x0, other arithmetic: 2.66 us -> none  [the longest x1 1.65 us: paired(): tail = jnp.where(core == 0, theirs[-extra * BLK:], mine[-extra * BLK:])]
    unnamed x10, local copies, waits for them, and re-layouts: 1.76 us -> 3.5 us
    dynamic_slice x1 -> x0, local copies, waits for them, and re-layouts: 1.09 us -> none  [paired(): mine = lax.dynamic_slice_in_dim(kv_rows, core * kv_width, kv_width, 1)]
  transfers between devices with their start and end apart: 15 -> 15, of which waited for: 4 -> 4; matrix products, arithmetic and copies ran while one was open for 7% -> 5% of each run, Pallas kernels for 36% -> 35%
where the time goes in v4:
time: 88.1 us; the launch traced here: 87.5 us
  Pallas kernels  40.3 us (46%)
  starting transfers between devices  27.7 us (31%)
  waiting for transfers between devices  11.1 us (13%)
  local copies, waits for them, and re-layouts  5.98 us (7%)
  other arithmetic  1.99 us (2%)
    pallas_call x3, Pallas kernels, vertical_part(): pl.pallas_call(functools.partial(vertical_kernel, sources, kvs, n_kv, n_v...  18.6 us
    ppermute x6, starting transfers between devices, by_chip(): return lax.ppermute(array, 'seq', pairs)  15 us
    pallas_call x1, Pallas kernels, window_part(): pl.pallas_call(functools.partial(window_kernel, sizes, places, kvs, n_kv,...  12.8 us
    ppermute x6, waiting for transfers between devices, by_chip(): return lax.ppermute(array, 'seq', pairs)  8.05 us
    all_to_all x1, starting transfers between devices, paired(): held = lax.all_to_all(split, 'seq', split_axis=0, concat_axis=0, tiled=True)  7.35 us
    pallas_call x2, Pallas kernels, assemble(): pl.pallas_call(functools.partial(assemble_kernel, n), in_specs=[pl.BlockS...  4.94 us
    ppermute x6, starting transfers between devices, swap(): return lax.ppermute(array, ('seq', 'tp'), pairs)  4.86 us
    unnamed x10, local copies, waits for them, and re-layouts  3.5 us
  transfers between devices with their start and end apart: 15, of which 4 were waited for; matrix products, arithmetic and copies ran while one was open for 5% of the time, Pallas kernels for 35%

profile of v4, /device:TPU:1, one launch (start us, length us, event | category | flops | bytes accessed | tf_op | source)
XLA Modules:
  0.0 87.5 jit_solution(6361569935060973337)
XLA Ops:
  0.0 2.3 %shard_map.46 = (bf16[16,8,16,128]{3,2,1,0:T(8,128)(2,1)}, bf16[256,512]{1,0:T(8,128)(2,1)}, bf16[256,512]{1,0:T(8,128)(2,1)}) custom-call(s32[1]{0:T(128)} %bitcast.4.core_ref, bf16[256,1024]{1,0:T(8,128)(2,1)} %kv_ref.1), custom_call_target="tpu_custom_call" | custom-call | tf_op jit(solution)/shard_map/pallas_call | solution.py:397
  2.3 7.4 %all-to-all-start = ((bf16[16,8,16,128]{3,2,1,0:T(8,128)(2,1)}), bf16[16,8,16,128]{3,2,1,0:T(8,128)(2,1)}, u32[]{:S(2)}, u32[]{:S(2)}) async-start(bf16[16,8,16,128]{3,2,1,0:T(8,128)(2,1)} %get-tuple-element.34), calls=%async_computation | async-start | bytes 1048576 | tf_op jit(solution)/shard_map/all_to_all | solution.py:541
  9.6 0.2 collective-permute-start
  9.9 0.8 constant_dynamic-slice_fusion
  10.8 0.1 eq.81
  10.9 0.1 fusion
  11.0 0.1 convert_reduce_fusion
  11.2 0.3 fusion.2
  11.4 0.1 copy.17
  11.6 0.3 compare_reduce_fusion
  11.9 0.1 compare_reduce_fusion.2
  12.0 0.9 %copy-done.1 = bf16[256,512]{1,0:T(8,128)(2,1)S(1)} copy-done((bf16[256,512]{1,0:T(8,128)(2,1)S(1)}, bf16[256,512]{1,0:T(8,128)(2,1)}, u32[]{:S(2)}) %copy-start.1) | copy-done | bytes 262168
  13.0 0.7 shard_map.48
  13.7 0.8 copy-done.2
  14.5 1.1 %constant_dynamic-slice_fusion.1 = bf16[256,2048]{1,0:T(8,128)(2,1)} fusion(bf16[256,4096]{1,0:T(8,128)(2,1)S(1)} %copy-done, s32[]{:T(128)S(6)} %select_n.70), kind=kLoop, calls=%fused_computation.20 | loop fusion | bytes 2097156 | tf_op jit(solution)/shard_map/dynamic_slice | solution.py:550
  15.6 0.3 collective-permute-start.1
  15.9 0.1 compare_reduce_fusion.1
  16.0 0.1 copy.16
  16.0 0.1 add.131.index_ref
  16.1 0.1 and_and_fusion
  16.3 4.1 %collective-permute-start.7 = (bf16[512,512]{1,0:T(8,128)(2,1)}, bf16[512,512]{1,0:T(8,128)(2,1)}, u32[]{:S(2)}, u32[]{:S(2)}) collective-permute-start(bf16[512,512]{1,0:T(8,128)(2,1)} %copy-done.2), channel_id=1, source_target_pairs={{0,4},{2,6},{4,8},{6,10},{8,12},{10,14},{12,16},{14,18},{16,20},{1... | collective-permute-start | bytes 1572872 | tf_op jit(solution)/shard_map/ppermute | solution.py:535
  20.3 0.1 subtract_compare_fusion
  20.4 3.0 %collective-permute-start.6 = (bf16[192,512]{1,0:T(8,128)(2,1)}, bf16[192,512]{1,0:T(8,128)(2,1)}, u32[]{:S(2)}, u32[]{:S(2)}) collective-permute-start(bf16[192,512]{1,0:T(8,128)(2,1)} %get-tuple-element.38), channel_id=1, source_target_pairs={{0,8},{2,10},{4,12},{6,14},{8,16},{10,18},{12,20},{14,22},{16,24},... | collective-permute-start | bytes 589832 | tf_op jit(solution)/shard_map/ppermute | solution.py:535
  23.4 0.4 all-to-all-done
  23.8 1.1 %shard_map.47 = bf16[2,176,128]{2,1,0:T(8,128)(2,1)S(1)} custom-call(s32[22]{0:T(128)S(1)} %add.131.index_ref, bf16[128,16,128]{2,1,0:T(8,128)(2,1)} %bitcast.14.table), custom_call_target="tpu_custom_call" | custom-call | tf_op jit(solution)/shard_map/pallas_call | solution.py:436
  24.9 0.9 %collective-permute-start.2 = (bf16[2,176,128]{2,1,0:T(8,128)(2,1)S(1)}, bf16[2,176,128]{2,1,0:T(8,128)(2,1)S(1)}, u32[]{:S(2)}, u32[]{:S(2)}) collective-permute-start(bf16[2,176,128]{2,1,0:T(8,128)(2,1)S(1)} %shard_map.47), channel_id=1, source_target_pairs={{0,4},{2,6},{4,0},{6,2},{8,12},{10,14},{12,8},{14,10},{16,20},{18,... | collective-permute-start | bytes 270344 | tf_op jit(solution)/shard_map/ppermute | solution.py:535
  26.0 0.1 stack.86.pos_ref
  26.1 7.3 %collective-permute-done.2 = bf16[2,176,128]{2,1,0:T(8,128)(2,1)S(1)} collective-permute-done((bf16[2,176,128]{2,1,0:T(8,128)(2,1)S(1)}, bf16[2,176,128]{2,1,0:T(8,128)(2,1)S(1)}, u32[]{:S(2)}, u32[]{:S(2)}) %collective-permute-start.2) | collective-permute-done | bytes 90144 | tf_op jit(solution)/shard_map/ppermute | solution.py:535
  33.4 5.8 %collective-permute-start.5 = (bf16[2,2,176,128]{3,2,1,0:T(8,128)(2,1)S(1)}, bf16[2,2,176,128]{3,2,1,0:T(8,128)(2,1)S(1)}, u32[]{:S(2)}, u32[]{:S(2)}) collective-permute-start(bf16[2,2,176,128]{3,2,1,0:T(8,128)(2,1)S(1)} %maximum_select_fusion.refs_0_), channel_id=1, source_target_pairs={{0,24},{2,26},{4,28},{6,30},{8,0},{10,2},{12,4},{14,6},{16,8},{18,... | collective-permute-start | bytes 540680 | tf_op jit(solution)/shard_map/ppermute | solution.py:535
  39.2 1.2 %collective-permute-start.3 = (bf16[2,2,176,128]{3,2,1,0:T(8,128)(2,1)S(1)}, bf16[2,2,176,128]{3,2,1,0:T(8,128)(2,1)S(1)}, u32[]{:S(2)}, u32[]{:S(2)}) collective-permute-start(bf16[2,2,176,128]{3,2,1,0:T(8,128)(2,1)S(1)} %maximum_select_fusion.refs_0_), channel_id=1, source_target_pairs={{0,8},{2,10},{4,12},{6,14},{8,16},{10,18},{12,20},{14,22},{16,24},... | collective-permute-start | bytes 540680 | tf_op jit(solution)/shard_map/ppermute | solution.py:535
  40.4 1.0 %copy-done.3 = bf16[512,512]{1,0:T(8,128)(2,1)S(1)} copy-done((bf16[512,512]{1,0:T(8,128)(2,1)S(1)}, bf16[512,512]{1,0:T(8,128)(2,1)}, u32[]{:S(2)}) %copy-start.3) | copy-done | bytes 524312
  41.4 12.8 %shard_map.49 = (f32[16,512,128]{2,1,0:T(8,128)S(1)}, f32[16,512,128]{2,1,0:T(8,128)S(1)}) custom-call(s32[10]{0:T(128)S(1)} %stack.86.pos_ref, bf16[512,512]{1,0:T(8,128)(2,1)S(1)} %copy-done.3, bf16[192,512]{1,0:T(8,128)(2,1)} %collective-permute-done.6.refs_1_, bf16[512,512]{1,0:T(8,128)(2,1)} %collective-permute-done.7.refs_2_, ...), custom_call_target="tpu_custom_call" | custom-call | flops 6442450944 | bytes 16777216 | tf_op jit(solution)/shard_map/pallas_call | solution.py:191
  54.2 0.8 collective-permute-done.4.refs_2_
  55.0 4.9 %shard_map.50 = (bf16[128,1024]{1,0:T(8,128)(2,1)S(1)}, bf16[128,1024]{1,0:T(8,128)(2,1)}) custom-call(s32[10]{0:T(128)S(1)} %stack.86.pos_ref, bf16[2,2,176,128]{3,2,1,0:T(8,128)(2,1)S(1)} %maximum_select_fusion.refs_0_, bf16[2,2,176,128]{3,2,1,0:T(8,128)(2,1)S(1)} %collective-permute-done.3.refs_1_, ...), custom_call_target="tpu_custom_call" | custom-call | flops 1610612736 | bytes 8388608 | tf_op jit(solution)/shard_map/pallas_call | solution.py:351
  59.9 1.3 %collective-permute-start.12 = (bf16[128,1024]{1,0:T(8,128)(2,1)S(1)}, bf16[128,1024]{1,0:T(8,128)(2,1)S(1)}, u32[]{:S(2)}, u32[]{:S(2)}) collective-permute-start(bf16[128,1024]{1,0:T(8,128)(2,1)S(1)} %get-tuple-element.60), channel_id=1, source_target_pairs={{0,1},{1,0},{2,3},{3,2},{4,5},{5,4},{6,7},{7,6},{8,9},{9,8},{10,11... | collective-permute-start | bytes 786440 | tf_op jit(solution)/shard_map/ppermute | solution.py:583
  61.2 1.4 %collective-permute-start.13 = (bf16[128,1024]{1,0:T(8,128)(2,1)}, bf16[128,1024]{1,0:T(8,128)(2,1)}, u32[]{:S(2)}, u32[]{:S(2)}) collective-permute-start(bf16[128,1024]{1,0:T(8,128)(2,1)} %get-tuple-element.61), channel_id=1, source_target_pairs={{0,3},{1,2},{2,1},{3,0},{4,7},{5,6},{6,5},{7,4},{8,11},{9,10},{10,... | collective-permute-start | bytes 786440 | tf_op jit(solution)/shard_map/ppermute | solution.py:583
  62.7 5.0 %shard_map.51 = (bf16[128,1024]{1,0:T(8,128)(2,1)}, bf16[128,1024]{1,0:T(8,128)(2,1)}) custom-call(s32[10]{0:T(128)S(1)} %stack.86.pos_ref, bf16[2,2,176,128]{3,2,1,0:T(8,128)(2,1)S(1)} %maximum_select_fusion.refs_0_, bf16[2,2,176,128]{3,2,1,0:T(8,128)(2,1)S(1)} %collective-permute-done.3.refs_1_, ...), custom_call_target="tpu_custom_call" | custom-call | flops 1610612736 | bytes 8388608 | tf_op jit(solution)/shard_map/pallas_call | solution.py:351
  67.7 1.3 %collective-permute-start.8 = (bf16[128,1024]{1,0:T(8,128)(2,1)}, bf16[128,1024]{1,0:T(8,128)(2,1)S(1)}, u32[]{:S(2)}, u32[]{:S(2)}) collective-permute-start(bf16[128,1024]{1,0:T(8,128)(2,1)} %get-tuple-element.51), channel_id=1, source_target_pairs={{0,1},{1,0},{2,3},{3,2},{4,5},{5,4},{6,7},{7,6},{8,9},{9,8},{10,11... | collective-permute-start | bytes 786440 | tf_op jit(solution)/shard_map/ppermute | solution.py:583
  68.9 0.3 collective-permute-start.9
  69.2 8.6 %shard_map.52 = (bf16[128,8192]{1,0:T(8,128)(2,1)}, bf16[128,1024]{1,0:T(8,128)(2,1)}, bf16[128,1024]{1,0:T(8,128)(2,1)}) custom-call(s32[10]{0:T(128)S(1)} %stack.86.pos_ref, bf16[2,2,176,128]{3,2,1,0:T(8,128)(2,1)S(1)} %maximum_select_fusion.refs_0_, bf16[2,2,176,128]{3,2,1,0:T(8,128)(2,1)S(1)} %collective-permute-done.3.refs_1_, ...), custom_call_target="tpu_custom_call" | custom-call | flops 3221225472 | bytes 8388608 | tf_op jit(solution)/shard_map/pallas_call | solution.py:351
  77.9 0.4 collective-permute-start.10
  78.3 0.7 copy-done.4
  79.0 0.1 collective-permute-start.11
  79.2 0.7 pad_add_fusion.1.column_ref
  79.8 0.1 pad_add_fusion.column_ref
  79.9 2.4 %shard_map.53.refs_4_ = bf16[128,8192]{1,0:T(8,128)(2,1)} custom-call(s32[2]{0:T(128)} %pad_add_fusion.1.column_ref, bf16[128,1024]{1,0:T(8,128)(2,1)} %copy-done.4, bf16[128,1024]{1,0:T(8,128)(2,1)} %collective-permute-done.13.refs_1_, bf16[128,8192]{1,0:T(8,128)(2,1)} %get-tuple-element.62.refs_2_), custom_call_target="tpu_custom_call", output_to_operand_aliasing={{}: (3, {})} | custom-call | tf_op jit(solution)/shard_map/pallas_call | solution.py:468
  82.4 2.6 %collective-permute-done.9.refs_1_ = bf16[128,1024]{1,0:T(8,128)(2,1)} collective-permute-done((bf16[128,1024]{1,0:T(8,128)(2,1)}, bf16[128,1024]{1,0:T(8,128)(2,1)}, u32[]{:S(2)}, u32[]{:S(2)}) %collective-permute-start.9) | collective-permute-done | bytes 262176 | tf_op jit(solution)/shard_map/ppermute | solution.py:583
  85.0 2.5 %shard_map.54 = bf16[128,8192]{1,0:T(8,128)(2,1)} custom-call(s32[4]{0:T(128)S(1)} %pad_add_fusion.column_ref, bf16[128,1024]{1,0:T(8,128)(2,1)S(1)} %collective-permute-done.8.refs_0_, bf16[128,1024]{1,0:T(8,128)(2,1)} %collective-permute-done.9.refs_1_, bf16[128,1024]{1,0:T(8,128)(2,1)S(1)} %collective-permute-done.10.refs_2_, ...), custom_call_target="tpu_custom_call", output_to_operand_aliasing={{}: (5, {})} | custom-call | tf_op jit(solution)/shard_map/pallas_call | solution.py:468
  (32 shorter events, 0.4 us)
Async XLA Ops:
  0.0 14.5 %copy-start = (bf16[256,4096]{1,0:T(8,128)(2,1)S(1)}, bf16[256,4096]{1,0:T(8,128)(2,1)}, u32[]{:S(2)}) copy-start(bf16[256,4096]{1,0:T(8,128)(2,1)} %refs_5_.5) | copy-start | bytes 6291460
  2.3 21.5 %all-to-all-start = ((bf16[16,8,16,128]{3,2,1,0:T(8,128)(2,1)}), bf16[16,8,16,128]{3,2,1,0:T(8,128)(2,1)}, u32[]{:S(2)}, u32[]{:S(2)}) async-start(bf16[16,8,16,128]{3,2,1,0:T(8,128)(2,1)} %get-tuple-element.34), calls=%async_computation | async-start | bytes 1048576 | tf_op jit(solution)/shard_map/all_to_all | solution.py:541
  9.6 2.4 %collective-permute-start = (bf16[256,512]{1,0:T(8,128)(2,1)}, bf16[256,512]{1,0:T(8,128)(2,1)S(1)}, u32[]{:S(2)}, u32[]{:S(2)}) collective-permute-start(bf16[256,512]{1,0:T(8,128)(2,1)} %get-tuple-element.36), channel_id=1, source_target_pairs={{0,2},{2,0},{4,6},{6,4},{8,10},{10,8},{12,14},{14,12},{16,18},{18,... | collective-permute-start | bytes 786440 | tf_op jit(solution)/shard_map/ppermute | solution.py:539
  12.0 1.0 %copy-start.1 = (bf16[256,512]{1,0:T(8,128)(2,1)S(1)}, bf16[256,512]{1,0:T(8,128)(2,1)}, u32[]{:S(2)}) copy-start(bf16[256,512]{1,0:T(8,128)(2,1)} %get-tuple-element.35.mine_ref) | copy-start | bytes 786436
  13.7 0.8 copy-start.2
  15.6 9.3 %collective-permute-start.1 = (bf16[256,2048]{1,0:T(8,128)(2,1)}, bf16[256,2048]{1,0:T(8,128)(2,1)S(1)}, u32[]{:S(2)}, u32[]{:S(2)}) collective-permute-start(bf16[256,2048]{1,0:T(8,128)(2,1)} %constant_dynamic-slice_fusion.1), channel_id=1, source_target_pairs={{0,2},{2,0},{4,6},{6,4},{8,10},{10,8},{12,14},{14,12},{16,18},{18,... | collective-permute-start | bytes 3145736 | tf_op jit(solution)/shard_map/ppermute | solution.py:551
  16.3 24.1 %collective-permute-start.7 = (bf16[512,512]{1,0:T(8,128)(2,1)}, bf16[512,512]{1,0:T(8,128)(2,1)}, u32[]{:S(2)}, u32[]{:S(2)}) collective-permute-start(bf16[512,512]{1,0:T(8,128)(2,1)} %copy-done.2), channel_id=1, source_target_pairs={{0,4},{2,6},{4,8},{6,10},{8,12},{10,14},{12,16},{14,18},{16,20},{1... | collective-permute-start | bytes 1572872 | tf_op jit(solution)/shard_map/ppermute | solution.py:535
  20.4 20.0 %collective-permute-start.6 = (bf16[192,512]{1,0:T(8,128)(2,1)}, bf16[192,512]{1,0:T(8,128)(2,1)}, u32[]{:S(2)}, u32[]{:S(2)}) collective-permute-start(bf16[192,512]{1,0:T(8,128)(2,1)} %get-tuple-element.38), channel_id=1, source_target_pairs={{0,8},{2,10},{4,12},{6,14},{8,16},{10,18},{12,20},{14,22},{16,24},... | collective-permute-start | bytes 589832 | tf_op jit(solution)/shard_map/ppermute | solution.py:535
  24.9 8.4 %collective-permute-start.2 = (bf16[2,176,128]{2,1,0:T(8,128)(2,1)S(1)}, bf16[2,176,128]{2,1,0:T(8,128)(2,1)S(1)}, u32[]{:S(2)}, u32[]{:S(2)}) collective-permute-start(bf16[2,176,128]{2,1,0:T(8,128)(2,1)S(1)} %shard_map.47), channel_id=1, source_target_pairs={{0,4},{2,6},{4,0},{6,2},{8,12},{10,14},{12,8},{14,10},{16,20},{18,... | collective-permute-start | bytes 270344 | tf_op jit(solution)/shard_map/ppermute | solution.py:535
  33.4 20.9 %collective-permute-start.5 = (bf16[2,2,176,128]{3,2,1,0:T(8,128)(2,1)S(1)}, bf16[2,2,176,128]{3,2,1,0:T(8,128)(2,1)S(1)}, u32[]{:S(2)}, u32[]{:S(2)}) collective-permute-start(bf16[2,2,176,128]{3,2,1,0:T(8,128)(2,1)S(1)} %maximum_select_fusion.refs_0_), channel_id=1, source_target_pairs={{0,24},{2,26},{4,28},{6,30},{8,0},{10,2},{12,4},{14,6},{16,8},{18,... | collective-permute-start | bytes 540680 | tf_op jit(solution)/shard_map/ppermute | solution.py:535
  39.2 15.8 %collective-permute-start.4 = (bf16[2,2,176,128]{3,2,1,0:T(8,128)(2,1)S(1)}, bf16[2,2,176,128]{3,2,1,0:T(8,128)(2,1)S(1)}, u32[]{:S(2)}, u32[]{:S(2)}) collective-permute-start(bf16[2,2,176,128]{3,2,1,0:T(8,128)(2,1)S(1)} %maximum_select_fusion.refs_0_), channel_id=1, source_target_pairs={{0,16},{2,18},{4,20},{6,22},{8,24},{10,26},{12,28},{14,30},{16,0},... | collective-permute-start | bytes 540680 | tf_op jit(solution)/shard_map/ppermute | solution.py:535
  39.2 15.8 %collective-permute-start.3 = (bf16[2,2,176,128]{3,2,1,0:T(8,128)(2,1)S(1)}, bf16[2,2,176,128]{3,2,1,0:T(8,128)(2,1)S(1)}, u32[]{:S(2)}, u32[]{:S(2)}) collective-permute-start(bf16[2,2,176,128]{3,2,1,0:T(8,128)(2,1)S(1)} %maximum_select_fusion.refs_0_), channel_id=1, source_target_pairs={{0,8},{2,10},{4,12},{6,14},{8,16},{10,18},{12,20},{14,22},{16,24},... | collective-permute-start | bytes 540680 | tf_op jit(solution)/shard_map/ppermute | solution.py:535
  40.4 1.0 %copy-start.3 = (bf16[512,512]{1,0:T(8,128)(2,1)S(1)}, bf16[512,512]{1,0:T(8,128)(2,1)}, u32[]{:S(2)}) copy-start(bf16[512,512]{1,0:T(8,128)(2,1)} %copy-done.2) | copy-start | bytes 1572868
  59.9 18.4 %collective-permute-start.12 = (bf16[128,1024]{1,0:T(8,128)(2,1)S(1)}, bf16[128,1024]{1,0:T(8,128)(2,1)S(1)}, u32[]{:S(2)}, u32[]{:S(2)}) collective-permute-start(bf16[128,1024]{1,0:T(8,128)(2,1)S(1)} %get-tuple-element.60), channel_id=1, source_target_pairs={{0,1},{1,0},{2,3},{3,2},{4,5},{5,4},{6,7},{7,6},{8,9},{9,8},{10,11... | collective-permute-start | bytes 786440 | tf_op jit(solution)/shard_map/ppermute | solution.py:583
  61.2 18.7 %collective-permute-start.13 = (bf16[128,1024]{1,0:T(8,128)(2,1)}, bf16[128,1024]{1,0:T(8,128)(2,1)}, u32[]{:S(2)}, u32[]{:S(2)}) collective-permute-start(bf16[128,1024]{1,0:T(8,128)(2,1)} %get-tuple-element.61), channel_id=1, source_target_pairs={{0,3},{1,2},{2,1},{3,0},{4,7},{5,6},{6,5},{7,4},{8,11},{9,10},{10,... | collective-permute-start | bytes 786440 | tf_op jit(solution)/shard_map/ppermute | solution.py:583
  67.7 14.7 %collective-permute-start.8 = (bf16[128,1024]{1,0:T(8,128)(2,1)}, bf16[128,1024]{1,0:T(8,128)(2,1)S(1)}, u32[]{:S(2)}, u32[]{:S(2)}) collective-permute-start(bf16[128,1024]{1,0:T(8,128)(2,1)} %get-tuple-element.51), channel_id=1, source_target_pairs={{0,1},{1,0},{2,3},{3,2},{4,5},{5,4},{6,7},{7,6},{8,9},{9,8},{10,11... | collective-permute-start | bytes 786440 | tf_op jit(solution)/shard_map/ppermute | solution.py:583
  68.9 16.1 %collective-permute-start.9 = (bf16[128,1024]{1,0:T(8,128)(2,1)}, bf16[128,1024]{1,0:T(8,128)(2,1)}, u32[]{:S(2)}, u32[]{:S(2)}) collective-permute-start(bf16[128,1024]{1,0:T(8,128)(2,1)} %get-tuple-element.52), channel_id=1, source_target_pairs={{0,3},{1,2},{2,1},{3,0},{4,7},{5,6},{6,5},{7,4},{8,11},{9,10},{10,... | collective-permute-start | bytes 786440 | tf_op jit(solution)/shard_map/ppermute | solution.py:583
  77.9 7.1 %collective-permute-start.10 = (bf16[128,1024]{1,0:T(8,128)(2,1)}, bf16[128,1024]{1,0:T(8,128)(2,1)S(1)}, u32[]{:S(2)}, u32[]{:S(2)}) collective-permute-start(bf16[128,1024]{1,0:T(8,128)(2,1)} %get-tuple-element.58), channel_id=1, source_target_pairs={{0,2},{1,3},{2,0},{3,1},{4,6},{5,7},{6,4},{7,5},{8,10},{9,11},{10,... | collective-permute-start | bytes 786440 | tf_op jit(solution)/shard_map/ppermute | solution.py:583
  78.3 0.7 copy-start.4
  79.0 6.0 %collective-permute-start.11 = (bf16[128,1024]{1,0:T(8,128)(2,1)}, bf16[128,1024]{1,0:T(8,128)(2,1)S(1)}, u32[]{:S(2)}, u32[]{:S(2)}) collective-permute-start(bf16[128,1024]{1,0:T(8,128)(2,1)} %get-tuple-element.59), channel_id=1, source_target_pairs={{0,2},{1,3},{2,0},{3,1},{4,6},{5,7},{6,4},{7,5},{8,10},{9,11},{10,... | collective-permute-start | bytes 786440 | tf_op jit(solution)/shard_map/ppermute | solution.py:583

commit v5 on v4

--- a/solution.py
+++ b/solution.py
@@ -446,19 +446,14 @@
 
 
 def assemble_kernel(n, column_ref, *refs):
-    pieces, (_, out), buffers, sem = refs[:n], refs[n:n + 2], refs[n + 2:-1], refs[-1]
-    loads = [pltpu.make_async_copy(pieces[i], buffers[i], sem.at[0, i]) for i in range(n)]
-    start_all(loads)
-    stores = []
+    pieces, (_, out), sem = refs[:n], refs[n:n + 2], refs[-1]
+    copies = []
     for i in range(n):
-        loads[i].wait()
-        width = buffers[i].shape[1]
+        width = pieces[i].shape[1]
         start = pl.multiple_of(column_ref[i], width)
-        stores.append(
-            pltpu.make_async_copy(buffers[i], out.at[:, pl.ds(start, width)], sem.at[1, i])
-        )
-        stores[-1].start()
-    wait_all(stores)
+        copies.append(pltpu.make_async_copy(pieces[i], out.at[:, pl.ds(start, width)], sem.at[i]))
+    start_all(copies)
+    wait_all(copies)
 
 
 def assemble(out, results, vmem):
@@ -467,11 +462,12 @@
     n = len(pieces)
     return pl.pallas_call(
         functools.partial(assemble_kernel, n),
-        in_specs=[pl.BlockSpec(memory_space=pltpu.SMEM)] + [ANY] * (n + 1),
+        in_specs=[pl.BlockSpec(memory_space=pltpu.SMEM)]
+        + [pl.BlockSpec(memory_space=pltpu.VMEM)] * n
+        + [ANY],
         out_specs=ANY,
         out_shape=jax.ShapeDtypeStruct(out.shape, out.dtype),
-        scratch_shapes=[pltpu.VMEM(piece.shape, piece.dtype) for piece in pieces]
-        + [pltpu.SemaphoreType.DMA((2, n))],
+        scratch_shapes=[pltpu.SemaphoreType.DMA((n,))],
         input_output_aliases={n + 1: 0},
         compiler_params=pltpu.CompilerParams(vmem_limit_bytes=vmem),
     )(columns, *pieces, out)

time: 88.1 us -> 87.5 us (level)
  Pallas kernels: 40.3 us -> 39.2 us
    pallas_call x2, Pallas kernels: 4.94 us -> 3.81 us  [assemble(): pl.pallas_call(functools.partial(assemble_kernel, n), in_specs=[pl.BlockS...]
where the time goes in v5:
time: 87.5 us; the launch traced here: 87 us
  Pallas kernels  39.2 us (45%)
  starting transfers between devices  27.7 us (32%)
  waiting for transfers between devices  11.7 us (13%)
  local copies, waits for them, and re-layouts  5.98 us (7%)
  other arithmetic  1.99 us (2%)
    pallas_call x3, Pallas kernels, vertical_part(): pl.pallas_call(functools.partial(vertical_kernel, sources, kvs, n_kv, n_v...  18.6 us
    ppermute x6, starting transfers between devices, by_chip(): return lax.ppermute(array, 'seq', pairs)  15 us
    pallas_call x1, Pallas kernels, window_part(): pl.pallas_call(functools.partial(window_kernel, sizes, places, kvs, n_kv,...  12.8 us
    ppermute x6, waiting for transfers between devices, by_chip(): return lax.ppermute(array, 'seq', pairs)  8.05 us
    all_to_all x1, starting transfers between devices, paired(): held = lax.all_to_all(split, 'seq', split_axis=0, concat_axis=0, tiled=True)  7.35 us
    ppermute x6, starting transfers between devices, swap(): return lax.ppermute(array, ('seq', 'tp'), pairs)  4.86 us
    pallas_call x2, Pallas kernels, assemble(): pl.pallas_call(functools.partial(assemble_kernel, n), in_specs=[pl.BlockS...  3.81 us
    unnamed x10, local copies, waits for them, and re-layouts  3.5 us
  transfers between devices with their start and end apart: 15, of which 4 were waited for; matrix products, arithmetic and copies ran while one was open for 5% of the time, Pallas kernels for 35%

profile of v5, /device:TPU:1, one launch (start us, length us, event | category | flops | bytes accessed | tf_op | source)
XLA Modules:
  0.0 87.0 jit_solution(9888399296791343338)
XLA Ops:
  0.0 2.3 %shard_map.46 = (bf16[16,8,16,128]{3,2,1,0:T(8,128)(2,1)}, bf16[256,512]{1,0:T(8,128)(2,1)}, bf16[256,512]{1,0:T(8,128)(2,1)}) custom-call(s32[1]{0:T(128)} %bitcast.4.core_ref, bf16[256,1024]{1,0:T(8,128)(2,1)} %kv_ref.1), custom_call_target="tpu_custom_call" | custom-call | tf_op jit(solution)/shard_map/pallas_call | solution.py:397
  2.3 7.4 %all-to-all-start = ((bf16[16,8,16,128]{3,2,1,0:T(8,128)(2,1)}), bf16[16,8,16,128]{3,2,1,0:T(8,128)(2,1)}, u32[]{:S(2)}, u32[]{:S(2)}) async-start(bf16[16,8,16,128]{3,2,1,0:T(8,128)(2,1)} %get-tuple-element.34), calls=%async_computation | async-start | bytes 1048576 | tf_op jit(solution)/shard_map/all_to_all | solution.py:537
  9.6 0.2 collective-permute-start
  9.9 0.8 constant_dynamic-slice_fusion
  10.8 0.1 eq.81
  10.9 0.1 fusion
  11.0 0.1 convert_reduce_fusion
  11.2 0.3 fusion.2
  11.4 0.1 copy.17
  11.6 0.3 compare_reduce_fusion
  11.9 0.1 compare_reduce_fusion.2
  12.0 0.9 %copy-done.1 = bf16[256,512]{1,0:T(8,128)(2,1)S(1)} copy-done((bf16[256,512]{1,0:T(8,128)(2,1)S(1)}, bf16[256,512]{1,0:T(8,128)(2,1)}, u32[]{:S(2)}) %copy-start.1) | copy-done | bytes 262168
  13.0 0.7 shard_map.48
  13.7 0.8 copy-done.2
  14.5 1.1 %constant_dynamic-slice_fusion.1 = bf16[256,2048]{1,0:T(8,128)(2,1)} fusion(bf16[256,4096]{1,0:T(8,128)(2,1)S(1)} %copy-done, s32[]{:T(128)S(6)} %select_n.70), kind=kLoop, calls=%fused_computation.20 | loop fusion | bytes 2097156 | tf_op jit(solution)/shard_map/dynamic_slice | solution.py:546
  15.6 0.3 collective-permute-start.1
  15.9 0.1 compare_reduce_fusion.1
  16.0 0.1 copy.16
  16.0 0.1 add.131.index_ref
  16.1 0.1 and_and_fusion
  16.3 4.1 %collective-permute-start.7 = (bf16[512,512]{1,0:T(8,128)(2,1)}, bf16[512,512]{1,0:T(8,128)(2,1)}, u32[]{:S(2)}, u32[]{:S(2)}) collective-permute-start(bf16[512,512]{1,0:T(8,128)(2,1)} %copy-done.2), channel_id=1, source_target_pairs={{0,4},{2,6},{4,8},{6,10},{8,12},{10,14},{12,16},{14,18},{16,20},{1... | collective-permute-start | bytes 1572872 | tf_op jit(solution)/shard_map/ppermute | solution.py:531
  20.3 0.1 subtract_compare_fusion
  20.4 3.0 %collective-permute-start.6 = (bf16[192,512]{1,0:T(8,128)(2,1)}, bf16[192,512]{1,0:T(8,128)(2,1)}, u32[]{:S(2)}, u32[]{:S(2)}) collective-permute-start(bf16[192,512]{1,0:T(8,128)(2,1)} %get-tuple-element.38), channel_id=1, source_target_pairs={{0,8},{2,10},{4,12},{6,14},{8,16},{10,18},{12,20},{14,22},{16,24},... | collective-permute-start | bytes 589832 | tf_op jit(solution)/shard_map/ppermute | solution.py:531
  23.4 0.4 all-to-all-done
  23.8 1.1 %shard_map.47 = bf16[2,176,128]{2,1,0:T(8,128)(2,1)S(1)} custom-call(s32[22]{0:T(128)S(1)} %add.131.index_ref, bf16[128,16,128]{2,1,0:T(8,128)(2,1)} %bitcast.14.table), custom_call_target="tpu_custom_call" | custom-call | tf_op jit(solution)/shard_map/pallas_call | solution.py:436
  24.9 0.9 %collective-permute-start.2 = (bf16[2,176,128]{2,1,0:T(8,128)(2,1)S(1)}, bf16[2,176,128]{2,1,0:T(8,128)(2,1)S(1)}, u32[]{:S(2)}, u32[]{:S(2)}) collective-permute-start(bf16[2,176,128]{2,1,0:T(8,128)(2,1)S(1)} %shard_map.47), channel_id=1, source_target_pairs={{0,4},{2,6},{4,0},{6,2},{8,12},{10,14},{12,8},{14,10},{16,20},{18,... | collective-permute-start | bytes 270344 | tf_op jit(solution)/shard_map/ppermute | solution.py:531
  26.0 0.1 stack.86.pos_ref
  26.1 7.3 %collective-permute-done.2 = bf16[2,176,128]{2,1,0:T(8,128)(2,1)S(1)} collective-permute-done((bf16[2,176,128]{2,1,0:T(8,128)(2,1)S(1)}, bf16[2,176,128]{2,1,0:T(8,128)(2,1)S(1)}, u32[]{:S(2)}, u32[]{:S(2)}) %collective-permute-start.2) | collective-permute-done | bytes 90144 | tf_op jit(solution)/shard_map/ppermute | solution.py:531
  33.4 5.8 %collective-permute-start.5 = (bf16[2,2,176,128]{3,2,1,0:T(8,128)(2,1)S(1)}, bf16[2,2,176,128]{3,2,1,0:T(8,128)(2,1)S(1)}, u32[]{:S(2)}, u32[]{:S(2)}) collective-permute-start(bf16[2,2,176,128]{3,2,1,0:T(8,128)(2,1)S(1)} %maximum_select_fusion.refs_0_), channel_id=1, source_target_pairs={{0,24},{2,26},{4,28},{6,30},{8,0},{10,2},{12,4},{14,6},{16,8},{18,... | collective-permute-start | bytes 540680 | tf_op jit(solution)/shard_map/ppermute | solution.py:531
  39.2 1.2 %collective-permute-start.3 = (bf16[2,2,176,128]{3,2,1,0:T(8,128)(2,1)S(1)}, bf16[2,2,176,128]{3,2,1,0:T(8,128)(2,1)S(1)}, u32[]{:S(2)}, u32[]{:S(2)}) collective-permute-start(bf16[2,2,176,128]{3,2,1,0:T(8,128)(2,1)S(1)} %maximum_select_fusion.refs_0_), channel_id=1, source_target_pairs={{0,8},{2,10},{4,12},{6,14},{8,16},{10,18},{12,20},{14,22},{16,24},... | collective-permute-start | bytes 540680 | tf_op jit(solution)/shard_map/ppermute | solution.py:531
  40.4 1.0 %copy-done.3 = bf16[512,512]{1,0:T(8,128)(2,1)S(1)} copy-done((bf16[512,512]{1,0:T(8,128)(2,1)S(1)}, bf16[512,512]{1,0:T(8,128)(2,1)}, u32[]{:S(2)}) %copy-start.3) | copy-done | bytes 524312
  41.4 12.8 %shard_map.49 = (f32[16,512,128]{2,1,0:T(8,128)S(1)}, f32[16,512,128]{2,1,0:T(8,128)S(1)}) custom-call(s32[10]{0:T(128)S(1)} %stack.86.pos_ref, bf16[512,512]{1,0:T(8,128)(2,1)S(1)} %copy-done.3, bf16[192,512]{1,0:T(8,128)(2,1)} %collective-permute-done.6.refs_1_, bf16[512,512]{1,0:T(8,128)(2,1)} %collective-permute-done.7.refs_2_, ...), custom_call_target="tpu_custom_call" | custom-call | flops 6442450944 | bytes 16777216 | tf_op jit(solution)/shard_map/pallas_call | solution.py:191
  54.2 0.8 collective-permute-done.4.refs_2_
  55.0 4.9 %shard_map.50 = (bf16[128,1024]{1,0:T(8,128)(2,1)S(1)}, bf16[128,1024]{1,0:T(8,128)(2,1)}) custom-call(s32[10]{0:T(128)S(1)} %stack.86.pos_ref, bf16[2,2,176,128]{3,2,1,0:T(8,128)(2,1)S(1)} %maximum_select_fusion.refs_0_, bf16[2,2,176,128]{3,2,1,0:T(8,128)(2,1)S(1)} %collective-permute-done.3.refs_1_, ...), custom_call_target="tpu_custom_call" | custom-call | flops 1610612736 | bytes 8388608 | tf_op jit(solution)/shard_map/pallas_call | solution.py:351
  59.9 1.3 %collective-permute-start.12 = (bf16[128,1024]{1,0:T(8,128)(2,1)S(1)}, bf16[128,1024]{1,0:T(8,128)(2,1)S(1)}, u32[]{:S(2)}, u32[]{:S(2)}) collective-permute-start(bf16[128,1024]{1,0:T(8,128)(2,1)S(1)} %get-tuple-element.60), channel_id=1, source_target_pairs={{0,1},{1,0},{2,3},{3,2},{4,5},{5,4},{6,7},{7,6},{8,9},{9,8},{10,11... | collective-permute-start | bytes 786440 | tf_op jit(solution)/shard_map/ppermute | solution.py:579
  61.2 1.4 %collective-permute-start.13 = (bf16[128,1024]{1,0:T(8,128)(2,1)}, bf16[128,1024]{1,0:T(8,128)(2,1)}, u32[]{:S(2)}, u32[]{:S(2)}) collective-permute-start(bf16[128,1024]{1,0:T(8,128)(2,1)} %get-tuple-element.61), channel_id=1, source_target_pairs={{0,3},{1,2},{2,1},{3,0},{4,7},{5,6},{6,5},{7,4},{8,11},{9,10},{10,... | collective-permute-start | bytes 786440 | tf_op jit(solution)/shard_map/ppermute | solution.py:579
  62.7 5.0 %shard_map.51 = (bf16[128,1024]{1,0:T(8,128)(2,1)}, bf16[128,1024]{1,0:T(8,128)(2,1)}) custom-call(s32[10]{0:T(128)S(1)} %stack.86.pos_ref, bf16[2,2,176,128]{3,2,1,0:T(8,128)(2,1)S(1)} %maximum_select_fusion.refs_0_, bf16[2,2,176,128]{3,2,1,0:T(8,128)(2,1)S(1)} %collective-permute-done.3.refs_1_, ...), custom_call_target="tpu_custom_call" | custom-call | flops 1610612736 | bytes 8388608 | tf_op jit(solution)/shard_map/pallas_call | solution.py:351
  67.7 1.3 %collective-permute-start.8 = (bf16[128,1024]{1,0:T(8,128)(2,1)}, bf16[128,1024]{1,0:T(8,128)(2,1)S(1)}, u32[]{:S(2)}, u32[]{:S(2)}) collective-permute-start(bf16[128,1024]{1,0:T(8,128)(2,1)} %get-tuple-element.51), channel_id=1, source_target_pairs={{0,1},{1,0},{2,3},{3,2},{4,5},{5,4},{6,7},{7,6},{8,9},{9,8},{10,11... | collective-permute-start | bytes 786440 | tf_op jit(solution)/shard_map/ppermute | solution.py:579
  68.9 0.3 collective-permute-start.9
  69.2 8.6 %shard_map.52 = (bf16[128,8192]{1,0:T(8,128)(2,1)}, bf16[128,1024]{1,0:T(8,128)(2,1)}, bf16[128,1024]{1,0:T(8,128)(2,1)}) custom-call(s32[10]{0:T(128)S(1)} %stack.86.pos_ref, bf16[2,2,176,128]{3,2,1,0:T(8,128)(2,1)S(1)} %maximum_select_fusion.refs_0_, bf16[2,2,176,128]{3,2,1,0:T(8,128)(2,1)S(1)} %collective-permute-done.3.refs_1_, ...), custom_call_target="tpu_custom_call" | custom-call | flops 3221225472 | bytes 8388608 | tf_op jit(solution)/shard_map/pallas_call | solution.py:351
  77.9 0.4 collective-permute-start.10
  78.3 0.7 copy-done.4
  79.0 0.1 collective-permute-start.11
  79.2 0.7 pad_add_fusion.1.column_ref
  79.8 0.1 pad_add_fusion.column_ref
  79.9 1.8 %shard_map.53.refs_4_ = bf16[128,8192]{1,0:T(8,128)(2,1)} custom-call(s32[2]{0:T(128)} %pad_add_fusion.1.column_ref, bf16[128,1024]{1,0:T(8,128)(2,1)} %copy-done.4, bf16[128,1024]{1,0:T(8,128)(2,1)} %collective-permute-done.13.refs_1_, bf16[128,8192]{1,0:T(8,128)(2,1)} %get-tuple-element.62.refs_2_), custom_call_target="tpu_custom_call", output_to_operand_aliasing={{}: (3, {})} | custom-call | tf_op jit(solution)/shard_map/pallas_call | solution.py:463
  81.8 3.2 %collective-permute-done.9.refs_1_ = bf16[128,1024]{1,0:T(8,128)(2,1)} collective-permute-done((bf16[128,1024]{1,0:T(8,128)(2,1)}, bf16[128,1024]{1,0:T(8,128)(2,1)}, u32[]{:S(2)}, u32[]{:S(2)}) %collective-permute-start.9) | collective-permute-done | bytes 262176 | tf_op jit(solution)/shard_map/ppermute | solution.py:579
  85.0 2.0 %shard_map.54 = bf16[128,8192]{1,0:T(8,128)(2,1)} custom-call(s32[4]{0:T(128)S(1)} %pad_add_fusion.column_ref, bf16[128,1024]{1,0:T(8,128)(2,1)S(1)} %collective-permute-done.8.refs_0_, bf16[128,1024]{1,0:T(8,128)(2,1)} %collective-permute-done.9.refs_1_, bf16[128,1024]{1,0:T(8,128)(2,1)S(1)} %collective-permute-done.10.refs_2_, ...), custom_call_target="tpu_custom_call", output_to_operand_aliasing={{}: (5, {})} | custom-call | tf_op jit(solution)/shard_map/pallas_call | solution.py:463
  (32 shorter events, 0.4 us)
Async XLA Ops:
  0.0 14.5 %copy-start = (bf16[256,4096]{1,0:T(8,128)(2,1)S(1)}, bf16[256,4096]{1,0:T(8,128)(2,1)}, u32[]{:S(2)}) copy-start(bf16[256,4096]{1,0:T(8,128)(2,1)} %refs_5_.5) | copy-start | bytes 6291460
  2.3 21.5 %all-to-all-start = ((bf16[16,8,16,128]{3,2,1,0:T(8,128)(2,1)}), bf16[16,8,16,128]{3,2,1,0:T(8,128)(2,1)}, u32[]{:S(2)}, u32[]{:S(2)}) async-start(bf16[16,8,16,128]{3,2,1,0:T(8,128)(2,1)} %get-tuple-element.34), calls=%async_computation | async-start | bytes 1048576 | tf_op jit(solution)/shard_map/all_to_all | solution.py:537
  9.6 2.4 %collective-permute-start = (bf16[256,512]{1,0:T(8,128)(2,1)}, bf16[256,512]{1,0:T(8,128)(2,1)S(1)}, u32[]{:S(2)}, u32[]{:S(2)}) collective-permute-start(bf16[256,512]{1,0:T(8,128)(2,1)} %get-tuple-element.36), channel_id=1, source_target_pairs={{0,2},{2,0},{4,6},{6,4},{8,10},{10,8},{12,14},{14,12},{16,18},{18,... | collective-permute-start | bytes 786440 | tf_op jit(solution)/shard_map/ppermute | solution.py:535
  12.0 1.0 %copy-start.1 = (bf16[256,512]{1,0:T(8,128)(2,1)S(1)}, bf16[256,512]{1,0:T(8,128)(2,1)}, u32[]{:S(2)}) copy-start(bf16[256,512]{1,0:T(8,128)(2,1)} %get-tuple-element.35.mine_ref) | copy-start | bytes 786436
  13.7 0.8 copy-start.2
  15.6 9.3 %collective-permute-start.1 = (bf16[256,2048]{1,0:T(8,128)(2,1)}, bf16[256,2048]{1,0:T(8,128)(2,1)S(1)}, u32[]{:S(2)}, u32[]{:S(2)}) collective-permute-start(bf16[256,2048]{1,0:T(8,128)(2,1)} %constant_dynamic-slice_fusion.1), channel_id=1, source_target_pairs={{0,2},{2,0},{4,6},{6,4},{8,10},{10,8},{12,14},{14,12},{16,18},{18,... | collective-permute-start | bytes 3145736 | tf_op jit(solution)/shard_map/ppermute | solution.py:547
  16.3 24.1 %collective-permute-start.7 = (bf16[512,512]{1,0:T(8,128)(2,1)}, bf16[512,512]{1,0:T(8,128)(2,1)}, u32[]{:S(2)}, u32[]{:S(2)}) collective-permute-start(bf16[512,512]{1,0:T(8,128)(2,1)} %copy-done.2), channel_id=1, source_target_pairs={{0,4},{2,6},{4,8},{6,10},{8,12},{10,14},{12,16},{14,18},{16,20},{1... | collective-permute-start | bytes 1572872 | tf_op jit(solution)/shard_map/ppermute | solution.py:531
  20.4 20.0 %collective-permute-start.6 = (bf16[192,512]{1,0:T(8,128)(2,1)}, bf16[192,512]{1,0:T(8,128)(2,1)}, u32[]{:S(2)}, u32[]{:S(2)}) collective-permute-start(bf16[192,512]{1,0:T(8,128)(2,1)} %get-tuple-element.38), channel_id=1, source_target_pairs={{0,8},{2,10},{4,12},{6,14},{8,16},{10,18},{12,20},{14,22},{16,24},... | collective-permute-start | bytes 589832 | tf_op jit(solution)/shard_map/ppermute | solution.py:531
  24.9 8.4 %collective-permute-start.2 = (bf16[2,176,128]{2,1,0:T(8,128)(2,1)S(1)}, bf16[2,176,128]{2,1,0:T(8,128)(2,1)S(1)}, u32[]{:S(2)}, u32[]{:S(2)}) collective-permute-start(bf16[2,176,128]{2,1,0:T(8,128)(2,1)S(1)} %shard_map.47), channel_id=1, source_target_pairs={{0,4},{2,6},{4,0},{6,2},{8,12},{10,14},{12,8},{14,10},{16,20},{18,... | collective-permute-start | bytes 270344 | tf_op jit(solution)/shard_map/ppermute | solution.py:531
  33.4 20.9 %collective-permute-start.5 = (bf16[2,2,176,128]{3,2,1,0:T(8,128)(2,1)S(1)}, bf16[2,2,176,128]{3,2,1,0:T(8,128)(2,1)S(1)}, u32[]{:S(2)}, u32[]{:S(2)}) collective-permute-start(bf16[2,2,176,128]{3,2,1,0:T(8,128)(2,1)S(1)} %maximum_select_fusion.refs_0_), channel_id=1, source_target_pairs={{0,24},{2,26},{4,28},{6,30},{8,0},{10,2},{12,4},{14,6},{16,8},{18,... | collective-permute-start | bytes 540680 | tf_op jit(solution)/shard_map/ppermute | solution.py:531
  39.2 15.8 %collective-permute-start.4 = (bf16[2,2,176,128]{3,2,1,0:T(8,128)(2,1)S(1)}, bf16[2,2,176,128]{3,2,1,0:T(8,128)(2,1)S(1)}, u32[]{:S(2)}, u32[]{:S(2)}) collective-permute-start(bf16[2,2,176,128]{3,2,1,0:T(8,128)(2,1)S(1)} %maximum_select_fusion.refs_0_), channel_id=1, source_target_pairs={{0,16},{2,18},{4,20},{6,22},{8,24},{10,26},{12,28},{14,30},{16,0},... | collective-permute-start | bytes 540680 | tf_op jit(solution)/shard_map/ppermute | solution.py:531
  39.2 15.8 %collective-permute-start.3 = (bf16[2,2,176,128]{3,2,1,0:T(8,128)(2,1)S(1)}, bf16[2,2,176,128]{3,2,1,0:T(8,128)(2,1)S(1)}, u32[]{:S(2)}, u32[]{:S(2)}) collective-permute-start(bf16[2,2,176,128]{3,2,1,0:T(8,128)(2,1)S(1)} %maximum_select_fusion.refs_0_), channel_id=1, source_target_pairs={{0,8},{2,10},{4,12},{6,14},{8,16},{10,18},{12,20},{14,22},{16,24},... | collective-permute-start | bytes 540680 | tf_op jit(solution)/shard_map/ppermute | solution.py:531
  40.4 1.0 %copy-start.3 = (bf16[512,512]{1,0:T(8,128)(2,1)S(1)}, bf16[512,512]{1,0:T(8,128)(2,1)}, u32[]{:S(2)}) copy-start(bf16[512,512]{1,0:T(8,128)(2,1)} %copy-done.2) | copy-start | bytes 1572868
  59.9 18.4 %collective-permute-start.12 = (bf16[128,1024]{1,0:T(8,128)(2,1)S(1)}, bf16[128,1024]{1,0:T(8,128)(2,1)S(1)}, u32[]{:S(2)}, u32[]{:S(2)}) collective-permute-start(bf16[128,1024]{1,0:T(8,128)(2,1)S(1)} %get-tuple-element.60), channel_id=1, source_target_pairs={{0,1},{1,0},{2,3},{3,2},{4,5},{5,4},{6,7},{7,6},{8,9},{9,8},{10,11... | collective-permute-start | bytes 786440 | tf_op jit(solution)/shard_map/ppermute | solution.py:579
  61.2 18.7 %collective-permute-start.13 = (bf16[128,1024]{1,0:T(8,128)(2,1)}, bf16[128,1024]{1,0:T(8,128)(2,1)}, u32[]{:S(2)}, u32[]{:S(2)}) collective-permute-start(bf16[128,1024]{1,0:T(8,128)(2,1)} %get-tuple-element.61), channel_id=1, source_target_pairs={{0,3},{1,2},{2,1},{3,0},{4,7},{5,6},{6,5},{7,4},{8,11},{9,10},{10,... | collective-permute-start | bytes 786440 | tf_op jit(solution)/shard_map/ppermute | solution.py:579
  67.7 14.1 %collective-permute-start.8 = (bf16[128,1024]{1,0:T(8,128)(2,1)}, bf16[128,1024]{1,0:T(8,128)(2,1)S(1)}, u32[]{:S(2)}, u32[]{:S(2)}) collective-permute-start(bf16[128,1024]{1,0:T(8,128)(2,1)} %get-tuple-element.51), channel_id=1, source_target_pairs={{0,1},{1,0},{2,3},{3,2},{4,5},{5,4},{6,7},{7,6},{8,9},{9,8},{10,11... | collective-permute-start | bytes 786440 | tf_op jit(solution)/shard_map/ppermute | solution.py:579
  68.9 16.1 %collective-permute-start.9 = (bf16[128,1024]{1,0:T(8,128)(2,1)}, bf16[128,1024]{1,0:T(8,128)(2,1)}, u32[]{:S(2)}, u32[]{:S(2)}) collective-permute-start(bf16[128,1024]{1,0:T(8,128)(2,1)} %get-tuple-element.52), channel_id=1, source_target_pairs={{0,3},{1,2},{2,1},{3,0},{4,7},{5,6},{6,5},{7,4},{8,11},{9,10},{10,... | collective-permute-start | bytes 786440 | tf_op jit(solution)/shard_map/ppermute | solution.py:579
  77.9 7.1 %collective-permute-start.10 = (bf16[128,1024]{1,0:T(8,128)(2,1)}, bf16[128,1024]{1,0:T(8,128)(2,1)S(1)}, u32[]{:S(2)}, u32[]{:S(2)}) collective-permute-start(bf16[128,1024]{1,0:T(8,128)(2,1)} %get-tuple-element.58), channel_id=1, source_target_pairs={{0,2},{1,3},{2,0},{3,1},{4,6},{5,7},{6,4},{7,5},{8,10},{9,11},{10,... | collective-permute-start | bytes 786440 | tf_op jit(solution)/shard_map/ppermute | solution.py:579
  78.3 0.7 copy-start.4
  79.0 6.0 %collective-permute-start.11 = (bf16[128,1024]{1,0:T(8,128)(2,1)}, bf16[128,1024]{1,0:T(8,128)(2,1)S(1)}, u32[]{:S(2)}, u32[]{:S(2)}) collective-permute-start(bf16[128,1024]{1,0:T(8,128)(2,1)} %get-tuple-element.59), channel_id=1, source_target_pairs={{0,2},{1,3},{2,0},{3,1},{4,6},{5,7},{6,4},{7,5},{8,10},{9,11},{10,... | collective-permute-start | bytes 786440 | tf_op jit(solution)/shard_map/ppermute | solution.py:579

commit v6 on v5

--- a/solution.py
+++ b/solution.py
@@ -319,7 +319,8 @@
         for source in range(n_src):
             turn = m * n_src + source
             if direct and source == 0:
-                column = pl.multiple_of(((tp_pos * n_src + core) * n_kv + kvs[m]) * width, width)
+                side = tp_pos * n_src + core if n_dst > 1 else 0
+                column = pl.multiple_of((side * n_kv + kvs[m]) * width, width)
                 target = outs_ref[0].at[:, pl.ds(column, width)]
             elif direct:
                 target = outs_ref[1 + m]

time: 87.5 us -> 87.5 us (level)
  no operation moved by 1% of the time
where the time goes in v6:
time: 87.5 us; the launch traced here: 87 us
  Pallas kernels  39.2 us (45%)
  starting transfers between devices  27.7 us (32%)
  waiting for transfers between devices  11.7 us (13%)
  local copies, waits for them, and re-layouts  5.98 us (7%)
  other arithmetic  1.99 us (2%)
    pallas_call x3, Pallas kernels, vertical_part(): pl.pallas_call(functools.partial(vertical_kernel, sources, kvs, n_kv, n_v...  18.6 us
    ppermute x6, starting transfers between devices, by_chip(): return lax.ppermute(array, 'seq', pairs)  15 us
    pallas_call x1, Pallas kernels, window_part(): pl.pallas_call(functools.partial(window_kernel, sizes, places, kvs, n_kv,...  12.8 us
    ppermute x6, waiting for transfers between devices, by_chip(): return lax.ppermute(array, 'seq', pairs)  8.05 us
    all_to_all x1, starting transfers between devices, paired(): held = lax.all_to_all(split, 'seq', split_axis=0, concat_axis=0, tiled=True)  7.35 us
    ppermute x6, starting transfers between devices, swap(): return lax.ppermute(array, ('seq', 'tp'), pairs)  4.86 us
    pallas_call x2, Pallas kernels, assemble(): pl.pallas_call(functools.partial(assemble_kernel, n), in_specs=[pl.BlockS...  3.81 us
    unnamed x10, local copies, waits for them, and re-layouts  3.5 us
  transfers between devices with their start and end apart: 15, of which 4 were waited for; matrix products, arithmetic and copies ran while one was open for 5% of the time, Pallas kernels for 35%

profile of v6, /device:TPU:1, one launch (start us, length us, event | category | flops | bytes accessed | tf_op | source)
XLA Modules:
  0.0 87.0 jit_solution(9888399296791343338)
XLA Ops:
  0.0 2.3 %shard_map.46 = (bf16[16,8,16,128]{3,2,1,0:T(8,128)(2,1)}, bf16[256,512]{1,0:T(8,128)(2,1)}, bf16[256,512]{1,0:T(8,128)(2,1)}) custom-call(s32[1]{0:T(128)} %bitcast.4.core_ref, bf16[256,1024]{1,0:T(8,128)(2,1)} %kv_ref.1), custom_call_target="tpu_custom_call" | custom-call | tf_op jit(solution)/shard_map/pallas_call | solution.py:398
  2.3 7.4 %all-to-all-start = ((bf16[16,8,16,128]{3,2,1,0:T(8,128)(2,1)}), bf16[16,8,16,128]{3,2,1,0:T(8,128)(2,1)}, u32[]{:S(2)}, u32[]{:S(2)}) async-start(bf16[16,8,16,128]{3,2,1,0:T(8,128)(2,1)} %get-tuple-element.34), calls=%async_computation | async-start | bytes 1048576 | tf_op jit(solution)/shard_map/all_to_all | solution.py:538
  9.6 0.2 collective-permute-start
  9.9 0.8 constant_dynamic-slice_fusion
  10.8 0.1 eq.81
  10.9 0.1 fusion
  11.0 0.1 convert_reduce_fusion
  11.2 0.3 fusion.2
  11.4 0.1 copy.17
  11.6 0.3 compare_reduce_fusion
  11.9 0.1 compare_reduce_fusion.2
  12.0 0.9 %copy-done.1 = bf16[256,512]{1,0:T(8,128)(2,1)S(1)} copy-done((bf16[256,512]{1,0:T(8,128)(2,1)S(1)}, bf16[256,512]{1,0:T(8,128)(2,1)}, u32[]{:S(2)}) %copy-start.1) | copy-done | bytes 262168
  13.0 0.7 shard_map.48
  13.7 0.8 copy-done.2
  14.5 1.1 %constant_dynamic-slice_fusion.1 = bf16[256,2048]{1,0:T(8,128)(2,1)} fusion(bf16[256,4096]{1,0:T(8,128)(2,1)S(1)} %copy-done, s32[]{:T(128)S(6)} %select_n.70), kind=kLoop, calls=%fused_computation.20 | loop fusion | bytes 2097156 | tf_op jit(solution)/shard_map/dynamic_slice | solution.py:547
  15.6 0.3 collective-permute-start.1
  15.9 0.1 compare_reduce_fusion.1
  16.0 0.1 copy.16
  16.0 0.1 add.131.index_ref
  16.1 0.1 and_and_fusion
  16.3 4.1 %collective-permute-start.7 = (bf16[512,512]{1,0:T(8,128)(2,1)}, bf16[512,512]{1,0:T(8,128)(2,1)}, u32[]{:S(2)}, u32[]{:S(2)}) collective-permute-start(bf16[512,512]{1,0:T(8,128)(2,1)} %copy-done.2), channel_id=1, source_target_pairs={{0,4},{2,6},{4,8},{6,10},{8,12},{10,14},{12,16},{14,18},{16,20},{1... | collective-permute-start | bytes 1572872 | tf_op jit(solution)/shard_map/ppermute | solution.py:532
  20.3 0.1 subtract_compare_fusion
  20.4 3.0 %collective-permute-start.6 = (bf16[192,512]{1,0:T(8,128)(2,1)}, bf16[192,512]{1,0:T(8,128)(2,1)}, u32[]{:S(2)}, u32[]{:S(2)}) collective-permute-start(bf16[192,512]{1,0:T(8,128)(2,1)} %get-tuple-element.38), channel_id=1, source_target_pairs={{0,8},{2,10},{4,12},{6,14},{8,16},{10,18},{12,20},{14,22},{16,24},... | collective-permute-start | bytes 589832 | tf_op jit(solution)/shard_map/ppermute | solution.py:532
  23.4 0.4 all-to-all-done
  23.8 1.1 %shard_map.47 = bf16[2,176,128]{2,1,0:T(8,128)(2,1)S(1)} custom-call(s32[22]{0:T(128)S(1)} %add.131.index_ref, bf16[128,16,128]{2,1,0:T(8,128)(2,1)} %bitcast.14.table), custom_call_target="tpu_custom_call" | custom-call | tf_op jit(solution)/shard_map/pallas_call | solution.py:437
  24.9 0.9 %collective-permute-start.2 = (bf16[2,176,128]{2,1,0:T(8,128)(2,1)S(1)}, bf16[2,176,128]{2,1,0:T(8,128)(2,1)S(1)}, u32[]{:S(2)}, u32[]{:S(2)}) collective-permute-start(bf16[2,176,128]{2,1,0:T(8,128)(2,1)S(1)} %shard_map.47), channel_id=1, source_target_pairs={{0,4},{2,6},{4,0},{6,2},{8,12},{10,14},{12,8},{14,10},{16,20},{18,... | collective-permute-start | bytes 270344 | tf_op jit(solution)/shard_map/ppermute | solution.py:532
  26.0 0.1 stack.86.pos_ref
  26.1 7.3 %collective-permute-done.2 = bf16[2,176,128]{2,1,0:T(8,128)(2,1)S(1)} collective-permute-done((bf16[2,176,128]{2,1,0:T(8,128)(2,1)S(1)}, bf16[2,176,128]{2,1,0:T(8,128)(2,1)S(1)}, u32[]{:S(2)}, u32[]{:S(2)}) %collective-permute-start.2) | collective-permute-done | bytes 90144 | tf_op jit(solution)/shard_map/ppermute | solution.py:532
  33.4 5.8 %collective-permute-start.5 = (bf16[2,2,176,128]{3,2,1,0:T(8,128)(2,1)S(1)}, bf16[2,2,176,128]{3,2,1,0:T(8,128)(2,1)S(1)}, u32[]{:S(2)}, u32[]{:S(2)}) collective-permute-start(bf16[2,2,176,128]{3,2,1,0:T(8,128)(2,1)S(1)} %maximum_select_fusion.refs_0_), channel_id=1, source_target_pairs={{0,24},{2,26},{4,28},{6,30},{8,0},{10,2},{12,4},{14,6},{16,8},{18,... | collective-permute-start | bytes 540680 | tf_op jit(solution)/shard_map/ppermute | solution.py:532
  39.2 1.2 %collective-permute-start.3 = (bf16[2,2,176,128]{3,2,1,0:T(8,128)(2,1)S(1)}, bf16[2,2,176,128]{3,2,1,0:T(8,128)(2,1)S(1)}, u32[]{:S(2)}, u32[]{:S(2)}) collective-permute-start(bf16[2,2,176,128]{3,2,1,0:T(8,128)(2,1)S(1)} %maximum_select_fusion.refs_0_), channel_id=1, source_target_pairs={{0,8},{2,10},{4,12},{6,14},{8,16},{10,18},{12,20},{14,22},{16,24},... | collective-permute-start | bytes 540680 | tf_op jit(solution)/shard_map/ppermute | solution.py:532
  40.4 1.0 %copy-done.3 = bf16[512,512]{1,0:T(8,128)(2,1)S(1)} copy-done((bf16[512,512]{1,0:T(8,128)(2,1)S(1)}, bf16[512,512]{1,0:T(8,128)(2,1)}, u32[]{:S(2)}) %copy-start.3) | copy-done | bytes 524312
  41.4 12.8 %shard_map.49 = (f32[16,512,128]{2,1,0:T(8,128)S(1)}, f32[16,512,128]{2,1,0:T(8,128)S(1)}) custom-call(s32[10]{0:T(128)S(1)} %stack.86.pos_ref, bf16[512,512]{1,0:T(8,128)(2,1)S(1)} %copy-done.3, bf16[192,512]{1,0:T(8,128)(2,1)} %collective-permute-done.6.refs_1_, bf16[512,512]{1,0:T(8,128)(2,1)} %collective-permute-done.7.refs_2_, ...), custom_call_target="tpu_custom_call" | custom-call | flops 6442450944 | bytes 16777216 | tf_op jit(solution)/shard_map/pallas_call | solution.py:191
  54.2 0.8 collective-permute-done.4.refs_2_
  55.0 4.9 %shard_map.50 = (bf16[128,1024]{1,0:T(8,128)(2,1)S(1)}, bf16[128,1024]{1,0:T(8,128)(2,1)}) custom-call(s32[10]{0:T(128)S(1)} %stack.86.pos_ref, bf16[2,2,176,128]{3,2,1,0:T(8,128)(2,1)S(1)} %maximum_select_fusion.refs_0_, bf16[2,2,176,128]{3,2,1,0:T(8,128)(2,1)S(1)} %collective-permute-done.3.refs_1_, ...), custom_call_target="tpu_custom_call" | custom-call | flops 1610612736 | bytes 8388608 | tf_op jit(solution)/shard_map/pallas_call | solution.py:352
  59.9 1.3 %collective-permute-start.12 = (bf16[128,1024]{1,0:T(8,128)(2,1)S(1)}, bf16[128,1024]{1,0:T(8,128)(2,1)S(1)}, u32[]{:S(2)}, u32[]{:S(2)}) collective-permute-start(bf16[128,1024]{1,0:T(8,128)(2,1)S(1)} %get-tuple-element.60), channel_id=1, source_target_pairs={{0,1},{1,0},{2,3},{3,2},{4,5},{5,4},{6,7},{7,6},{8,9},{9,8},{10,11... | collective-permute-start | bytes 786440 | tf_op jit(solution)/shard_map/ppermute | solution.py:580
  61.2 1.4 %collective-permute-start.13 = (bf16[128,1024]{1,0:T(8,128)(2,1)}, bf16[128,1024]{1,0:T(8,128)(2,1)}, u32[]{:S(2)}, u32[]{:S(2)}) collective-permute-start(bf16[128,1024]{1,0:T(8,128)(2,1)} %get-tuple-element.61), channel_id=1, source_target_pairs={{0,3},{1,2},{2,1},{3,0},{4,7},{5,6},{6,5},{7,4},{8,11},{9,10},{10,... | collective-permute-start | bytes 786440 | tf_op jit(solution)/shard_map/ppermute | solution.py:580
  62.7 5.0 %shard_map.51 = (bf16[128,1024]{1,0:T(8,128)(2,1)}, bf16[128,1024]{1,0:T(8,128)(2,1)}) custom-call(s32[10]{0:T(128)S(1)} %stack.86.pos_ref, bf16[2,2,176,128]{3,2,1,0:T(8,128)(2,1)S(1)} %maximum_select_fusion.refs_0_, bf16[2,2,176,128]{3,2,1,0:T(8,128)(2,1)S(1)} %collective-permute-done.3.refs_1_, ...), custom_call_target="tpu_custom_call" | custom-call | flops 1610612736 | bytes 8388608 | tf_op jit(solution)/shard_map/pallas_call | solution.py:352
  67.7 1.3 %collective-permute-start.8 = (bf16[128,1024]{1,0:T(8,128)(2,1)}, bf16[128,1024]{1,0:T(8,128)(2,1)S(1)}, u32[]{:S(2)}, u32[]{:S(2)}) collective-permute-start(bf16[128,1024]{1,0:T(8,128)(2,1)} %get-tuple-element.51), channel_id=1, source_target_pairs={{0,1},{1,0},{2,3},{3,2},{4,5},{5,4},{6,7},{7,6},{8,9},{9,8},{10,11... | collective-permute-start | bytes 786440 | tf_op jit(solution)/shard_map/ppermute | solution.py:580
  68.9 0.3 collective-permute-start.9
  69.2 8.6 %shard_map.52 = (bf16[128,8192]{1,0:T(8,128)(2,1)}, bf16[128,1024]{1,0:T(8,128)(2,1)}, bf16[128,1024]{1,0:T(8,128)(2,1)}) custom-call(s32[10]{0:T(128)S(1)} %stack.86.pos_ref, bf16[2,2,176,128]{3,2,1,0:T(8,128)(2,1)S(1)} %maximum_select_fusion.refs_0_, bf16[2,2,176,128]{3,2,1,0:T(8,128)(2,1)S(1)} %collective-permute-done.3.refs_1_, ...), custom_call_target="tpu_custom_call" | custom-call | flops 3221225472 | bytes 8388608 | tf_op jit(solution)/shard_map/pallas_call | solution.py:352
  77.9 0.4 collective-permute-start.10
  78.3 0.7 copy-done.4
  79.0 0.1 collective-permute-start.11
  79.2 0.7 pad_add_fusion.1.column_ref
  79.8 0.1 pad_add_fusion.column_ref
  79.9 1.8 %shard_map.53.refs_4_ = bf16[128,8192]{1,0:T(8,128)(2,1)} custom-call(s32[2]{0:T(128)} %pad_add_fusion.1.column_ref, bf16[128,1024]{1,0:T(8,128)(2,1)} %copy-done.4, bf16[128,1024]{1,0:T(8,128)(2,1)} %collective-permute-done.13.refs_1_, bf16[128,8192]{1,0:T(8,128)(2,1)} %get-tuple-element.62.refs_2_), custom_call_target="tpu_custom_call", output_to_operand_aliasing={{}: (3, {})} | custom-call | tf_op jit(solution)/shard_map/pallas_call | solution.py:464
  81.8 3.2 %collective-permute-done.9.refs_1_ = bf16[128,1024]{1,0:T(8,128)(2,1)} collective-permute-done((bf16[128,1024]{1,0:T(8,128)(2,1)}, bf16[128,1024]{1,0:T(8,128)(2,1)}, u32[]{:S(2)}, u32[]{:S(2)}) %collective-permute-start.9) | collective-permute-done | bytes 262176 | tf_op jit(solution)/shard_map/ppermute | solution.py:580
  85.0 2.0 %shard_map.54 = bf16[128,8192]{1,0:T(8,128)(2,1)} custom-call(s32[4]{0:T(128)S(1)} %pad_add_fusion.column_ref, bf16[128,1024]{1,0:T(8,128)(2,1)S(1)} %collective-permute-done.8.refs_0_, bf16[128,1024]{1,0:T(8,128)(2,1)} %collective-permute-done.9.refs_1_, bf16[128,1024]{1,0:T(8,128)(2,1)S(1)} %collective-permute-done.10.refs_2_, ...), custom_call_target="tpu_custom_call", output_to_operand_aliasing={{}: (5, {})} | custom-call | tf_op jit(solution)/shard_map/pallas_call | solution.py:464
  (32 shorter events, 0.4 us)
Async XLA Ops:
  0.0 14.5 %copy-start = (bf16[256,4096]{1,0:T(8,128)(2,1)S(1)}, bf16[256,4096]{1,0:T(8,128)(2,1)}, u32[]{:S(2)}) copy-start(bf16[256,4096]{1,0:T(8,128)(2,1)} %refs_5_.5) | copy-start | bytes 6291460
  2.3 21.5 %all-to-all-start = ((bf16[16,8,16,128]{3,2,1,0:T(8,128)(2,1)}), bf16[16,8,16,128]{3,2,1,0:T(8,128)(2,1)}, u32[]{:S(2)}, u32[]{:S(2)}) async-start(bf16[16,8,16,128]{3,2,1,0:T(8,128)(2,1)} %get-tuple-element.34), calls=%async_computation | async-start | bytes 1048576 | tf_op jit(solution)/shard_map/all_to_all | solution.py:538
  9.6 2.4 %collective-permute-start = (bf16[256,512]{1,0:T(8,128)(2,1)}, bf16[256,512]{1,0:T(8,128)(2,1)S(1)}, u32[]{:S(2)}, u32[]{:S(2)}) collective-permute-start(bf16[256,512]{1,0:T(8,128)(2,1)} %get-tuple-element.36), channel_id=1, source_target_pairs={{0,2},{2,0},{4,6},{6,4},{8,10},{10,8},{12,14},{14,12},{16,18},{18,... | collective-permute-start | bytes 786440 | tf_op jit(solution)/shard_map/ppermute | solution.py:536
  12.0 1.0 %copy-start.1 = (bf16[256,512]{1,0:T(8,128)(2,1)S(1)}, bf16[256,512]{1,0:T(8,128)(2,1)}, u32[]{:S(2)}) copy-start(bf16[256,512]{1,0:T(8,128)(2,1)} %get-tuple-element.35.mine_ref) | copy-start | bytes 786436
  13.7 0.8 copy-start.2
  15.6 9.3 %collective-permute-start.1 = (bf16[256,2048]{1,0:T(8,128)(2,1)}, bf16[256,2048]{1,0:T(8,128)(2,1)S(1)}, u32[]{:S(2)}, u32[]{:S(2)}) collective-permute-start(bf16[256,2048]{1,0:T(8,128)(2,1)} %constant_dynamic-slice_fusion.1), channel_id=1, source_target_pairs={{0,2},{2,0},{4,6},{6,4},{8,10},{10,8},{12,14},{14,12},{16,18},{18,... | collective-permute-start | bytes 3145736 | tf_op jit(solution)/shard_map/ppermute | solution.py:548
  16.3 24.1 %collective-permute-start.7 = (bf16[512,512]{1,0:T(8,128)(2,1)}, bf16[512,512]{1,0:T(8,128)(2,1)}, u32[]{:S(2)}, u32[]{:S(2)}) collective-permute-start(bf16[512,512]{1,0:T(8,128)(2,1)} %copy-done.2), channel_id=1, source_target_pairs={{0,4},{2,6},{4,8},{6,10},{8,12},{10,14},{12,16},{14,18},{16,20},{1... | collective-permute-start | bytes 1572872 | tf_op jit(solution)/shard_map/ppermute | solution.py:532
  20.4 20.0 %collective-permute-start.6 = (bf16[192,512]{1,0:T(8,128)(2,1)}, bf16[192,512]{1,0:T(8,128)(2,1)}, u32[]{:S(2)}, u32[]{:S(2)}) collective-permute-start(bf16[192,512]{1,0:T(8,128)(2,1)} %get-tuple-element.38), channel_id=1, source_target_pairs={{0,8},{2,10},{4,12},{6,14},{8,16},{10,18},{12,20},{14,22},{16,24},... | collective-permute-start | bytes 589832 | tf_op jit(solution)/shard_map/ppermute | solution.py:532
  24.9 8.4 %collective-permute-start.2 = (bf16[2,176,128]{2,1,0:T(8,128)(2,1)S(1)}, bf16[2,176,128]{2,1,0:T(8,128)(2,1)S(1)}, u32[]{:S(2)}, u32[]{:S(2)}) collective-permute-start(bf16[2,176,128]{2,1,0:T(8,128)(2,1)S(1)} %shard_map.47), channel_id=1, source_target_pairs={{0,4},{2,6},{4,0},{6,2},{8,12},{10,14},{12,8},{14,10},{16,20},{18,... | collective-permute-start | bytes 270344 | tf_op jit(solution)/shard_map/ppermute | solution.py:532
  33.4 20.9 %collective-permute-start.5 = (bf16[2,2,176,128]{3,2,1,0:T(8,128)(2,1)S(1)}, bf16[2,2,176,128]{3,2,1,0:T(8,128)(2,1)S(1)}, u32[]{:S(2)}, u32[]{:S(2)}) collective-permute-start(bf16[2,2,176,128]{3,2,1,0:T(8,128)(2,1)S(1)} %maximum_select_fusion.refs_0_), channel_id=1, source_target_pairs={{0,24},{2,26},{4,28},{6,30},{8,0},{10,2},{12,4},{14,6},{16,8},{18,... | collective-permute-start | bytes 540680 | tf_op jit(solution)/shard_map/ppermute | solution.py:532
  39.2 15.8 %collective-permute-start.4 = (bf16[2,2,176,128]{3,2,1,0:T(8,128)(2,1)S(1)}, bf16[2,2,176,128]{3,2,1,0:T(8,128)(2,1)S(1)}, u32[]{:S(2)}, u32[]{:S(2)}) collective-permute-start(bf16[2,2,176,128]{3,2,1,0:T(8,128)(2,1)S(1)} %maximum_select_fusion.refs_0_), channel_id=1, source_target_pairs={{0,16},{2,18},{4,20},{6,22},{8,24},{10,26},{12,28},{14,30},{16,0},... | collective-permute-start | bytes 540680 | tf_op jit(solution)/shard_map/ppermute | solution.py:532
  39.2 15.8 %collective-permute-start.3 = (bf16[2,2,176,128]{3,2,1,0:T(8,128)(2,1)S(1)}, bf16[2,2,176,128]{3,2,1,0:T(8,128)(2,1)S(1)}, u32[]{:S(2)}, u32[]{:S(2)}) collective-permute-start(bf16[2,2,176,128]{3,2,1,0:T(8,128)(2,1)S(1)} %maximum_select_fusion.refs_0_), channel_id=1, source_target_pairs={{0,8},{2,10},{4,12},{6,14},{8,16},{10,18},{12,20},{14,22},{16,24},... | collective-permute-start | bytes 540680 | tf_op jit(solution)/shard_map/ppermute | solution.py:532
  40.4 1.0 %copy-start.3 = (bf16[512,512]{1,0:T(8,128)(2,1)S(1)}, bf16[512,512]{1,0:T(8,128)(2,1)}, u32[]{:S(2)}) copy-start(bf16[512,512]{1,0:T(8,128)(2,1)} %copy-done.2) | copy-start | bytes 1572868
  59.9 18.4 %collective-permute-start.12 = (bf16[128,1024]{1,0:T(8,128)(2,1)S(1)}, bf16[128,1024]{1,0:T(8,128)(2,1)S(1)}, u32[]{:S(2)}, u32[]{:S(2)}) collective-permute-start(bf16[128,1024]{1,0:T(8,128)(2,1)S(1)} %get-tuple-element.60), channel_id=1, source_target_pairs={{0,1},{1,0},{2,3},{3,2},{4,5},{5,4},{6,7},{7,6},{8,9},{9,8},{10,11... | collective-permute-start | bytes 786440 | tf_op jit(solution)/shard_map/ppermute | solution.py:580
  61.2 18.7 %collective-permute-start.13 = (bf16[128,1024]{1,0:T(8,128)(2,1)}, bf16[128,1024]{1,0:T(8,128)(2,1)}, u32[]{:S(2)}, u32[]{:S(2)}) collective-permute-start(bf16[128,1024]{1,0:T(8,128)(2,1)} %get-tuple-element.61), channel_id=1, source_target_pairs={{0,3},{1,2},{2,1},{3,0},{4,7},{5,6},{6,5},{7,4},{8,11},{9,10},{10,... | collective-permute-start | bytes 786440 | tf_op jit(solution)/shard_map/ppermute | solution.py:580
  67.7 14.1 %collective-permute-start.8 = (bf16[128,1024]{1,0:T(8,128)(2,1)}, bf16[128,1024]{1,0:T(8,128)(2,1)S(1)}, u32[]{:S(2)}, u32[]{:S(2)}) collective-permute-start(bf16[128,1024]{1,0:T(8,128)(2,1)} %get-tuple-element.51), channel_id=1, source_target_pairs={{0,1},{1,0},{2,3},{3,2},{4,5},{5,4},{6,7},{7,6},{8,9},{9,8},{10,11... | collective-permute-start | bytes 786440 | tf_op jit(solution)/shard_map/ppermute | solution.py:580
  68.9 16.1 %collective-permute-start.9 = (bf16[128,1024]{1,0:T(8,128)(2,1)}, bf16[128,1024]{1,0:T(8,128)(2,1)}, u32[]{:S(2)}, u32[]{:S(2)}) collective-permute-start(bf16[128,1024]{1,0:T(8,128)(2,1)} %get-tuple-element.52), channel_id=1, source_target_pairs={{0,3},{1,2},{2,1},{3,0},{4,7},{5,6},{6,5},{7,4},{8,11},{9,10},{10,... | collective-permute-start | bytes 786440 | tf_op jit(solution)/shard_map/ppermute | solution.py:580
  77.9 7.1 %collective-permute-start.10 = (bf16[128,1024]{1,0:T(8,128)(2,1)}, bf16[128,1024]{1,0:T(8,128)(2,1)S(1)}, u32[]{:S(2)}, u32[]{:S(2)}) collective-permute-start(bf16[128,1024]{1,0:T(8,128)(2,1)} %get-tuple-element.58), channel_id=1, source_target_pairs={{0,2},{1,3},{2,0},{3,1},{4,6},{5,7},{6,4},{7,5},{8,10},{9,11},{10,... | collective-permute-start | bytes 786440 | tf_op jit(solution)/shard_map/ppermute | solution.py:580
  78.3 0.7 copy-start.4
  79.0 6.0 %collective-permute-start.11 = (bf16[128,1024]{1,0:T(8,128)(2,1)}, bf16[128,1024]{1,0:T(8,128)(2,1)S(1)}, u32[]{:S(2)}, u32[]{:S(2)}) collective-permute-start(bf16[128,1024]{1,0:T(8,128)(2,1)} %get-tuple-element.59), channel_id=1, source_target_pairs={{0,2},{1,3},{2,0},{3,1},{4,6},{5,7},{6,4},{7,5},{8,10},{9,11},{10,... | collective-permute-start | bytes 786440 | tf_op jit(solution)/shard_map/ppermute | solution.py:580
